TPU v7x, 128 devices: a whole 4x4x4 slice. The times are simulated.
128 devices in a mesh: fsdp: 16 (over x_hi, z, core), tensor: 8 (over y, x_lo).
Axes of the slice: x: 4 (x_hi: 2, x_lo: 2; x = x_hi * 2 + x_lo), y: 4, z: 4, core: 2. Of those that a mesh axis runs over, the one named last changes fastest.
Arguments:
- grad: bfloat16 [12288, 53248], P('fsdp', 'tensor'), may hold values from -2 to 2
- old_stats: float32 [12288, 3, 768], P(('fsdp', 'tensor')), may hold values from -6 to 6
Outputs:
- new_stats: float32 [12288, 3, 768], P(('fsdp', 'tensor'))
All inputs are finite; a program needn't handle non-finite values.
Results may differ from a plain program's by a relative error of at most 0.0003.
Values may be sent and summed in bfloat16 or wider, within the bound.
No kernel may reach another device: no remote copies, remote signals or barrier semaphores. Data moves between devices by JAX's collectives and lax.ppermute only.
A program may use at most 128 MiB of HBM per device.

v0:
```python
import jax
import jax.numpy as jnp
from jax import lax
from jax.sharding import PartitionSpec as P

COLS = 53248


decay_rate = 0.95


def passed_along(value, axis, steps):
    count = lax.axis_size(axis)
    pairs = [(source, (source + steps) % count) for source in range(count)]
    return lax.ppermute(value, axis, pairs)


def shards(grad, old_stats):
    following = passed_along(grad, "fsdp", -1)
    far_right = passed_along(grad, "fsdp", -2)
    contract = (((1,), (1,)), ((), ()))
    diagonal_part = lax.dot_general(grad, grad, contract, preferred_element_type=jnp.float32)
    near_part = lax.dot_general(grad, following, contract, preferred_element_type=jnp.float32)
    far_part = lax.dot_general(grad, far_right, contract, preferred_element_type=jnp.float32)
    summed = lax.psum_scatter(
        jnp.stack([diagonal_part, near_part, far_part], axis=1),
        "tensor",
        scatter_dimension=0,
        tiled=True,
    )
    return decay_rate * old_stats + (1.0 - decay_rate) * COLS ** (-0.5) * summed


def solution(mesh):
    return jax.shard_map(
        shards,
        mesh=mesh,
        in_specs=(P("fsdp", "tensor"), P(("fsdp", "tensor"), None, None)),
        out_specs=P(("fsdp", "tensor"), None, None),
        check_vma=False,
    )
```

profile of v0, /device:TPU:97, one launch (start us, length us, event | category | flops | bytes accessed | tf_op | source)
XLA Modules:
  0.0 511.8 jit_solution(1103821752184181953)
XLA Ops:
  6.5 0.0 reduce-scatter.2.cloned.1.call-start
  6.5 0.1 collective-permute-start.1
  6.7 1.0 collective-permute-start
  7.6 12.5 %convolution_bitcast_fusion.2 = f32[768,1,768]{2,0,1:T(8,128)S(1)} fusion(bf16[768,6656]{1,0:T(8,128)(2,1)} %param.2), kind=kOutput, calls=%fused_computation.3 | convolution fusion | flops 7851737088 | bytes 12582912 | tf_op jit(solution)/shard_map/dot_general | solution.py:22
  20.1 211.0 %collective-permute-done.1 = bf16[768,6656]{1,0:T(8,128)(2,1)} collective-permute-done((bf16[768,6656]{1,0:T(8,128)(2,1)}, bf16[768,6656]{1,0:T(8,128)(2,1)}, u32[]{:S(2)}, u32[]{:S(2)}) %collective-permute-start.1) | collective-permute-done | bytes 10223648 | tf_op jit(solution)/shard_map/ppermute | solution.py:15
  231.1 12.3 %convolution_bitcast_fusion = f32[768,1,768]{2,0,1:T(8,128)S(1)} fusion(bf16[768,6656]{1,0:T(8,128)(2,1)} %param.2, bf16[768,6656]{1,0:T(8,128)(2,1)} %collective-permute-done.1), kind=kOutput, calls=%fused_computation.1 | convolution fusion | flops 7851737088 | bytes 22806528 | tf_op jit(solution)/shard_map/dot_general | solution.py:24
  243.5 98.1 %collective-permute-done = bf16[768,6656]{1,0:T(8,128)(2,1)} collective-permute-done((bf16[768,6656]{1,0:T(8,128)(2,1)}, bf16[768,6656]{1,0:T(8,128)(2,1)}, u32[]{:S(2)}, u32[]{:S(2)}) %collective-permute-start) | collective-permute-done | bytes 10223648 | tf_op jit(solution)/shard_map/ppermute | solution.py:15
  341.5 12.4 %convolution_bitcast_fusion.1 = f32[768,1,768]{2,0,1:T(8,128)S(1)} fusion(bf16[768,6656]{1,0:T(8,128)(2,1)} %param.2, bf16[768,6656]{1,0:T(8,128)(2,1)} %collective-permute-done), kind=kOutput, calls=%fused_computation.2 | convolution fusion | flops 7851737088 | bytes 22806528 | tf_op jit(solution)/shard_map/dot_general | solution.py:23
  353.9 0.0 copy-start
  353.9 3.4 pad_maximum_fusion
  357.3 0.0 reduce-scatter.2.cloned.1.call-update
  357.3 145.5 %reduce-scatter.2.cloned.1.call-done = f32[96,3,768]{2,0,1:T(8,128)} async-done(((f32[768,3,768]{2,0,1:T(8,128)}), f32[96,3,768]{2,0,1:T(8,128)}) %reduce-scatter.2.cloned.1.call-update) | async-done | bytes 884752 | tf_op jit(solution)/shard_map/reduce_scatter | solution.py:25
  502.7 0.0 copy-done
  502.8 2.2 multiply_add_fusion
Async XLA Ops:
  6.5 496.2 %reduce-scatter.2.cloned.1.call-start = ((), (), s32[]{:S(2)}) async-start(), calls=%async_computation.1 | async-start | bytes 7962624 | tf_op jit(solution)/shard_map/reduce_scatter | solution.py:25
  6.5 224.6 %collective-permute-start.1 = (bf16[768,6656]{1,0:T(8,128)(2,1)}, bf16[768,6656]{1,0:T(8,128)(2,1)}, u32[]{:S(2)}, u32[]{:S(2)}) collective-permute-start(bf16[768,6656]{1,0:T(8,128)(2,1)} %param.2), channel_id=1, source_target_pairs={{0,112},{8,120},{16,0},{24,8},{32,16},{40,24},{48,32},{56,40},{64,... | collective-permute-start | bytes 30670856 | tf_op jit(solution)/shard_map/ppermute | solution.py:15
  6.7 334.9 %collective-permute-start = (bf16[768,6656]{1,0:T(8,128)(2,1)}, bf16[768,6656]{1,0:T(8,128)(2,1)}, u32[]{:S(2)}, u32[]{:S(2)}) collective-permute-start(bf16[768,6656]{1,0:T(8,128)(2,1)} %param.2), channel_id=1, source_target_pairs={{0,120},{8,0},{16,8},{24,16},{32,24},{40,32},{48,40},{56,48},{64,5... | collective-permute-start | bytes 30670856 | tf_op jit(solution)/shard_map/ppermute | solution.py:15
  353.9 148.9 %copy-start = (f32[96,3,768]{2,0,1:T(8,128)S(1)}, f32[96,3,768]{2,0,1:T(8,128)}, u32[]{:S(2)}) copy-start(f32[96,3,768]{2,0,1:T(8,128)} %param.3) | copy-start | bytes 2654212
Sparse Core Ops, SparseCore 0:
  357.4 145.2 reduce-scatter.1
where the time goes:
time: 514 us; the launch traced here: 512 us
  waiting for transfers between devices  455 us (89%)
  matrix products  37.2 us (7%)
  between operations  13.4 us (3%)
  other arithmetic  5.59 us (1%)
    ppermute x2, waiting for transfers between devices, passed_along(): return lax.ppermute(value, axis, pairs)  309 us
    reduce_scatter x1, waiting for transfers between devices, shards(): lax.psum_scatter(jnp.stack([diagonal_part, near_part, far_part], axis=1),...  145 us
    dot_general x1, matrix products, shards(): lax.dot_general(grad, grad, contract, preferred_element_type=jnp.float32)  12.5 us
    dot_general x1, matrix products, shards(): lax.dot_general(grad, following, contract, preferred_element_type=jnp.flo...  12.4 us
    dot_general x1, matrix products, shards(): lax.dot_general(grad, far_right, contract, preferred_element_type=jnp.flo...  12.3 us
  transfers between devices with their start and end apart: 3, of which 3 were waited for; matrix products, arithmetic and copies ran while one was open for 5% of the time, Pallas kernels for 0%

commit v1 on v0

v1 whole, which is shorter than its diff:
```python
import functools

import jax
import jax.numpy as jnp
from jax import lax
from jax.experimental import pallas as pl
from jax.experimental.pallas import tpu as pltpu
from jax.sharding import PartitionSpec as P

COLS = 53248
decay_rate = 0.95
CHUNKS = (256, 256, 128, 128)
BEGINS = (0, 256, 512, 640)
VMEM_LIMIT = 5 << 20
AXES = ("fsdp", "tensor")


def place(x_hi, z, core, y, x_lo):
    return ((x_hi % 2) * 8 + (z % 4) * 2 + core) * 8 + (y % 4) * 2 + x_lo


def moved(value, target):
    pairs = []
    for source in range(128):
        block, shard = divmod(source, 8)
        pairs.append((source, target(block // 8, (block // 2) % 4, block % 2, shard // 2, shard % 2)))
    return lax.ppermute(value, AXES, pairs)


def next_chip(x_hi, z, core, y, x_lo, steps):
    chip = (x_hi * 4 + z + steps) % 8
    return place(chip // 4, chip % 4, core, y, x_lo)


def block_flow(x_hi, z, core, y, x_lo):
    return next_chip(x_hi, z, core, y, x_lo, 1 if core else -1)


def swap_cores(x_hi, z, core, y, x_lo):
    return place(x_hi, z, 1 - core, y, x_lo)


def swap_both(x_hi, z, core, y, x_lo):
    return place(x_hi, z, 1 - core, y, 1 - x_lo)


def to_owner(x_hi, z, core, y, x_lo):
    return next_chip(x_hi, z, core, y, x_lo, -1 if core else 0)


def to_owner_x(x_hi, z, core, y, x_lo):
    return next_chip(x_hi, z, core, y, 1 - x_lo, -1 if core else 0)


def swap_x(x_hi, z, core, y, x_lo):
    return place(x_hi, z, core, y, 1 - x_lo)


def along_y(steps):
    return lambda x_hi, z, core, y, x_lo: place(x_hi, z, core, y + steps, x_lo)


def contract(left, right):
    return lax.dot_general(left, right, (((1,), (1,)), ((), ())), preferred_element_type=jnp.float32)


def pick_kernel(begin, thin, where_ref, grad_ref, out_ref, sems):
    core = where_ref[0]
    copies = []
    for i in range(8):
        offset = pl.multiple_of(jnp.where(core == 0, begin + thin * i, 96 * i + begin // 8), 16)
        copies.append(pltpu.make_async_copy(grad_ref.at[pl.ds(offset, thin)], out_ref.at[pl.ds(thin * i, thin)], sems.at[i]))
    for copy in copies:
        copy.start()
    for copy in copies:
        copy.wait()


def picked(where, grad, begin, wide):
    depth = grad.shape[1]
    return pl.pallas_call(
        functools.partial(pick_kernel, begin, wide // 8),
        out_shape=jax.ShapeDtypeStruct((wide, depth), grad.dtype),
        in_specs=[pl.BlockSpec(memory_space=pltpu.SMEM), pl.BlockSpec(memory_space=pl.ANY)],
        out_specs=pl.BlockSpec(memory_space=pltpu.VMEM),
        scratch_shapes=[pltpu.SemaphoreType.DMA((8,))],
        cost_estimate=pl.CostEstimate(flops=0, bytes_accessed=4 * wide * depth, transcendentals=0),
        compiler_params=pltpu.CompilerParams(vmem_limit_bytes=VMEM_LIMIT),
    )(where, pltpu.with_memory_space_constraint(grad, pltpu.HBM))


def hold_kernel(source_ref, out_ref, sem):
    copy = pltpu.make_async_copy(source_ref, out_ref, sem)
    copy.start()
    copy.wait()


def held(value):
    return pl.pallas_call(
        hold_kernel,
        out_shape=pltpu.VMEM(value.shape, value.dtype),
        in_specs=[pl.BlockSpec(memory_space=pl.ANY)],
        out_specs=pl.BlockSpec(memory_space=pltpu.VMEM),
        scratch_shapes=[pltpu.SemaphoreType.DMA],
        cost_estimate=pl.CostEstimate(flops=0, bytes_accessed=4 * value.size, transcendentals=0),
        compiler_params=pltpu.CompilerParams(vmem_limit_bytes=VMEM_LIMIT),
    )(pltpu.with_memory_space_constraint(value, pltpu.HBM))


def resident(value):
    return pltpu.with_memory_space_constraint(value, pltpu.VMEM)


def vmem_specs(count):
    return [pl.BlockSpec(memory_space=pltpu.SMEM)] + [pl.BlockSpec(memory_space=pltpu.VMEM)] * count


def owner_rows(y, hop, side, count):
    shard = 2 * ((y + hop) & 3) + side
    return pl.ds(pl.multiple_of(count * shard, count), count)


def square_kernel(where_ref, own_ref, *refs):
    outs, total = refs[:4], refs[4]
    y = where_ref[1]
    total[...] = contract(own_ref[...], own_ref[...])
    for hop in range(4):
        for side in range(2):
            outs[hop][side] = total[owner_rows(y, hop, side, 96), :]


def squared(where, grad):
    rows, depth = grad.shape
    piece = (2, rows // 8, rows)
    return pl.pallas_call(
        square_kernel,
        out_shape=[jax.ShapeDtypeStruct(piece, jnp.float32)] * 4,
        in_specs=vmem_specs(1),
        out_specs=[pl.BlockSpec(memory_space=pltpu.VMEM)] * 4,
        scratch_shapes=[pltpu.VMEM((rows, rows), jnp.float32)],
        cost_estimate=pl.CostEstimate(
            flops=2 * rows * rows * depth, bytes_accessed=2 * depth * rows + 4 * rows * rows, transcendentals=0
        ),
        compiler_params=pltpu.CompilerParams(vmem_limit_bytes=VMEM_LIMIT),
    )(where, resident(grad))


def cross_kernel(begin, wide, where_ref, own_ref, pair_ref, got_ref, *refs):
    outs, (tall, flat, mixed) = refs[:4], refs[4:]
    core, y = where_ref[0], where_ref[1]
    thin = wide // 8
    blocks = 768 // wide

    @pl.when(core == 0)
    def _():
        tall[...] = contract(own_ref[...], got_ref[...])
        mixed[...] = contract(pair_ref[...], got_ref[...])
        for hop in range(4):
            for side in range(2):
                outs[hop][side, 0] = tall[owner_rows(y, hop, side, 96), :]

    @pl.when(core != 0)
    def _():
        flat[...] = contract(got_ref[...], own_ref[...])
        mixed[...] = contract(pair_ref[...], own_ref[begin : begin + wide, :])
        for hop in range(4):
            for side in range(2):
                rows = owner_rows(y, hop, side, thin)
                for i in range(blocks):
                    outs[hop][side, 0, i * thin : (i + 1) * thin, :] = flat[rows, i * wide : (i + 1) * wide]

    for hop in range(4):
        for side in range(2):
            outs[hop][side, 1] = mixed[owner_rows(y, hop, side, 96), :]


def crossed(where, grad, partner, arrived, begin):
    wide, depth = arrived.shape
    rows = grad.shape[0]
    piece = (2, 2, rows // 8, wide)
    return pl.pallas_call(
        functools.partial(cross_kernel, begin, wide),
        out_shape=[jax.ShapeDtypeStruct(piece, jnp.float32)] * 4,
        in_specs=vmem_specs(3),
        out_specs=[pl.BlockSpec(memory_space=pltpu.VMEM)] * 4,
        scratch_shapes=[
            pltpu.VMEM((rows, wide), jnp.float32),
            pltpu.VMEM((wide, rows), jnp.float32),
            pltpu.VMEM((rows, wide), jnp.float32),
        ],
        cost_estimate=pl.CostEstimate(
            flops=4 * rows * wide * depth, bytes_accessed=2 * depth * (2 * rows + wide) + 16 * rows * wide, transcendentals=0
        ),
        compiler_params=pltpu.CompilerParams(vmem_limit_bytes=VMEM_LIMIT),
    )(where, resident(grad), resident(partner), resident(arrived))


def total_of(refs, *at):
    return (refs[0][at] + refs[1][at]) + (refs[2][at] + refs[3][at])


def first_sums_kernel(where_ref, *refs):
    x_lo = where_ref[2]
    keep_ref, give_ref = refs[-2:]
    for side, out_ref in ((x_lo, keep_ref), (1 - x_lo, give_ref)):
        out_ref[0] = total_of(refs[:4], side)
        for j in range(len(CHUNKS) - 1):
            span = slice(BEGINS[j], BEGINS[j] + CHUNKS[j])
            for product in range(2):
                out_ref[1 + product, :, span] = total_of(refs[4 + 4 * j : 8 + 4 * j], side, product)
        for product in range(2):
            out_ref[1 + product, :, BEGINS[-1] :] = jnp.zeros((96, CHUNKS[-1]), jnp.float32)


def first_sums(where, pieces):
    shape = jax.ShapeDtypeStruct((3, 96, 768), jnp.float32)
    return pl.pallas_call(
        first_sums_kernel,
        out_shape=[shape, shape],
        in_specs=vmem_specs(len(pieces)),
        out_specs=[pl.BlockSpec(memory_space=pltpu.VMEM)] * 2,
        cost_estimate=pl.CostEstimate(flops=4 * 3 * 96 * 768 * 2, bytes_accessed=10 * 3 * 96 * 768 * 4, transcendentals=0),
        compiler_params=pltpu.CompilerParams(vmem_limit_bytes=2 * VMEM_LIMIT),
    )(where, *pieces)


def last_sums_kernel(where_ref, keep_ref, got_ref, piece_0, piece_1, piece_2, piece_3, diagonal_ref, far_ref, near_ref, give_ref):
    core, x_lo = where_ref[0], where_ref[2]
    pieces = (piece_0, piece_1, piece_2, piece_3)
    start = BEGINS[-1]
    diagonal_ref[...] = keep_ref[0] + got_ref[0]
    near_ref[:, :start] = keep_ref[2, :, :start] + got_ref[2, :, :start]
    near_ref[:, start:] = total_of(pieces, x_lo, 1)
    for product in range(2):
        give_ref[product] = total_of(pieces, 1 - x_lo, product)

    @pl.when(core == 0)
    def _():
        far_ref[:, :start] = keep_ref[1, :, :start] + got_ref[1, :, :start]
        far_ref[:, start:] = total_of(pieces, x_lo, 0)

    @pl.when(core != 0)
    def _():
        for begin, wide in zip(BEGINS, CHUNKS):
            thin = wide // 8
            for i in range(768 // wide):
                rows = slice(i * thin, (i + 1) * thin)
                if begin == start:
                    value = total_of(pieces, x_lo, 0, rows)
                else:
                    value = keep_ref[1, rows, begin : begin + wide] + got_ref[1, rows, begin : begin + wide]
                far_ref[begin // 8 : begin // 8 + thin, i * wide : (i + 1) * wide] = value


def last_sums(where, keep, got, pieces):
    shape = jax.ShapeDtypeStruct((96, 768), jnp.float32)
    return pl.pallas_call(
        last_sums_kernel,
        out_shape=[shape, shape, shape, jax.ShapeDtypeStruct((2, 96, CHUNKS[-1]), jnp.float32)],
        in_specs=vmem_specs(6),
        out_specs=[pl.BlockSpec(memory_space=pltpu.VMEM)] * 4,
        cost_estimate=pl.CostEstimate(flops=2 * 3 * 96 * 768, bytes_accessed=4 * 3 * 96 * 768 * 4, transcendentals=0),
        compiler_params=pltpu.CompilerParams(vmem_limit_bytes=VMEM_LIMIT),
    )(where, keep, got, *pieces)


def tied(*values):
    return lax.optimization_barrier(values)


def shards(grad, old_stats):
    rows = grad.shape[0]
    core = lax.axis_index("fsdp") & 1
    y, x_lo = lax.axis_index("tensor") >> 1, lax.axis_index("tensor") & 1
    where = jnp.stack([core, y, x_lo]).astype(jnp.int32)

    def spread(pieces):
        return [moved(pieces[hop], along_y(hop)) for hop in (1, 3, 2)]

    def pick(j):
        return picked(where, grad, BEGINS[j], CHUNKS[j])

    def cross(j):
        return crossed(where, here, partner, flight[j], BEGINS[j])

    partner = moved(grad, swap_cores)
    flight = [moved(pick(0), block_flow)]
    here = held(grad)
    square = squared(where, here)
    *square, partner, out1 = tied(*square, partner, pick(1))
    flight.append(moved(out1, block_flow))
    square_got = spread(square)
    partner = held(partner)
    out2, out3 = pick(2), pick(3)
    flight[0], partner, out2, out3 = tied(flight[0], partner, out2, out3)

    part0 = cross(0)
    *part0, out2, square_got[0], square_got[1], square_got[2] = tied(*part0, out2, *square_got)
    got0 = spread(part0)
    flight.append(moved(out2, block_flow))

    out3, got0[0], got0[1], got0[2] = tied(out3, *got0)
    flight.append(moved(out3, block_flow))
    flight[1], part0[0] = tied(flight[1], part0[0])
    part1 = list(cross(1))
    got1 = spread(part1)

    flight[2], part1[0] = tied(flight[2], part1[0])
    part2 = cross(2)
    *part2, got1[0], got1[1], got1[2] = tied(*part2, *got1)
    got2 = spread(part2)

    flight[3], got2[0], got2[1], got2[2] = tied(flight[3], *got2)
    firsts = [square[0], *square_got, part0[0], *got0, part1[0], *got1, part2[0], *got2]
    keep, give = first_sums(where, firsts)
    got = moved(give, swap_x)
    flight[3], keep = tied(flight[3], keep)
    part3 = cross(3)
    got3 = spread(part3)
    diagonal, far, near, give = last_sums(where, keep, got, [part3[0], *got3])

    far_more, near_more = moved(give[0], to_owner_x), moved(give[1], swap_both)
    far, near = moved(far, to_owner), moved(near, swap_cores)
    near = jnp.concatenate([near[:, :-128], near[:, -128:] + near_more], axis=1)
    far_low = jnp.pad(far_more, ((0, 0), (rows - 128, 0)))
    far_high = jnp.pad(far_more.reshape(6, 16, 128).transpose(1, 0, 2).reshape(16, rows), ((80, 0), (0, 0)))
    far = far + jnp.where(core == 0, far_low, far_high)
    summed = jnp.stack([diagonal, near, far], axis=1)
    return decay_rate * old_stats + (1.0 - decay_rate) * COLS ** (-0.5) * summed


def solution(mesh):
    return jax.shard_map(
        shards,
        mesh=mesh,
        in_specs=(P("fsdp", "tensor"), P(("fsdp", "tensor"), None, None)),
        out_specs=P(("fsdp", "tensor"), None, None),
        check_vma=False,
    )
```

time: 514 us -> 157 us (0.31)
  waiting for transfers between devices: 455 us -> 60 us
  Pallas kernels: 0 us -> 52.9 us
  starting transfers between devices: 1.08 us -> 41.2 us
  matrix products: 37.2 us -> 0 us
  between operations: 13.4 us -> 0.25 us
    ppermute x2 -> x25, waiting for transfers between devices: 309 us -> 60 us  [moved(): return lax.ppermute(value, AXES, pairs)]
    reduce_scatter x1 -> x0, waiting for transfers between devices: 145 us -> none  [shards(): lax.psum_scatter(jnp.stack([diagonal_part, near_part, far_part], axis=1),...]
    pallas_call x0 -> x13, Pallas kernels: none -> 52.9 us  [the longest x4 25.4 us: crossed(): pl.pallas_call(functools.partial(cross_kernel, begin, wide), out_shape=[j...]
    ppermute x2 -> x25, starting transfers between devices: 1.08 us -> 41.2 us  [moved(): return lax.ppermute(value, AXES, pairs)]
    dot_general x3 -> x0, matrix products: 37.2 us -> none  [the longest x1 12.5 us: shards(): lax.dot_general(grad, grad, contract, preferred_element_type=jnp.float32)]
  transfers between devices with their start and end apart: 3 -> 25, of which waited for: 3 -> 12; matrix products, arithmetic and copies ran while one was open for 5% -> 0% of each run, Pallas kernels for 0% -> 33%
where the time goes in v1:
time: 157 us; the launch traced here: 156 us
  waiting for transfers between devices  60 us (38%)
  Pallas kernels  52.9 us (34%)
  starting transfers between devices  41.2 us (26%)
    ppermute x25, waiting for transfers between devices, moved(): return lax.ppermute(value, AXES, pairs)  60 us
    ppermute x25, starting transfers between devices, moved(): return lax.ppermute(value, AXES, pairs)  41.2 us
    pallas_call x4, Pallas kernels, crossed(): pl.pallas_call(functools.partial(cross_kernel, begin, wide), out_shape=[j...  25.4 us
    pallas_call x4, Pallas kernels, picked(): pl.pallas_call(functools.partial(pick_kernel, begin, wide // 8), out_shap...  9.29 us
    pallas_call x1, Pallas kernels, squared(): pl.pallas_call(square_kernel, out_shape=[jax.ShapeDtypeStruct(piece, jnp....  8.83 us
    pallas_call x2, Pallas kernels, held(): pl.pallas_call(hold_kernel, out_shape=pltpu.VMEM(value.shape, value.dtype...  7.85 us
  transfers between devices with their start and end apart: 25, of which 12 were waited for; matrix products, arithmetic and copies ran while one was open for 0% of the time, Pallas kernels for 33%

profile of v1, /device:TPU:97, one launch (start us, length us, event | category | flops | bytes accessed | tf_op | source)
XLA Modules:
  0.0 155.5 jit_solution(8084356244966199374)
XLA Ops:
  0.0 0.7 collective-permute-start.1
  0.7 0.1 pad_add_fusion.where_ref
  0.8 2.5 %shard_map.28 = bf16[256,6656]{1,0:T(8,128)(2,1)S(1)} custom-call(s32[3]{0:T(128)S(1)} %pad_add_fusion.where_ref, bf16[768,6656]{1,0:T(8,128)(2,1)} %grad_ref.7), custom_call_target="tpu_custom_call" | custom-call | bytes 6815744 | tf_op jit(solution)/shard_map/pallas_call | solution.py:81
  3.3 1.4 collective-permute-start
  4.7 3.9 %shard_map.29.own_ref = bf16[768,6656]{1,0:T(8,128)(2,1)S(1)} custom-call(bf16[768,6656]{1,0:T(8,128)(2,1)} %grad_ref.7), custom_call_target="tpu_custom_call" | custom-call | bytes 20447232 | tf_op jit(solution)/shard_map/pallas_call | solution.py:99
  8.7 2.5 %shard_map.31 = bf16[256,6656]{1,0:T(8,128)(2,1)S(1)} custom-call(s32[3]{0:T(128)S(1)} %pad_add_fusion.where_ref, bf16[768,6656]{1,0:T(8,128)(2,1)} %grad_ref.7), custom_call_target="tpu_custom_call" | custom-call | bytes 6815744 | tf_op jit(solution)/shard_map/pallas_call | solution.py:81
  11.2 8.8 %shard_map.30 = (f32[2,96,768]{2,1,0:T(8,128)S(1)}, f32[2,96,768]{2,1,0:T(8,128)S(1)}, f32[2,96,768]{2,1,0:T(8,128)S(1)}, f32[2,96,768]{2,1,0:T(8,128)S(1)}) custom-call(s32[3]{0:T(128)S(1)} %pad_add_fusion.where_ref, bf16[768,6656]{1,0:T(8,128)(2,1)S(1)} %shard_map.29.own_ref), custom_call_target="tpu_custom_call" | custom-call | flops 7851737088 | bytes 12582912 | tf_op jit(solution)/shard_map/pallas_call | solution.py:135
  20.0 0.0 collective-permute-done.1.source_ref
  20.0 1.7 %collective-permute-start.10 = (bf16[256,6656]{1,0:T(8,128)(2,1)S(1)}, bf16[256,6656]{1,0:T(8,128)(2,1)S(1)}, u32[]{:S(2)}, u32[]{:S(2)}) collective-permute-start(bf16[256,6656]{1,0:T(8,128)(2,1)S(1)} %shard_map.31), channel_id=1, source_target_pairs={{0,112},{1,113},{2,114},{3,115},{4,116},{5,117},{6,118},{7,119},{8... | collective-permute-start | bytes 10223624 | tf_op jit(solution)/shard_map/ppermute | solution.py:27
  21.8 1.3 collective-permute-start.2
  23.1 1.4 collective-permute-start.3
  24.5 1.6 %collective-permute-start.4 = (f32[2,96,768]{2,1,0:T(8,128)S(1)}, f32[2,96,768]{2,1,0:T(8,128)S(1)}, u32[]{:S(2)}, u32[]{:S(2)}) collective-permute-start(f32[2,96,768]{2,1,0:T(8,128)S(1)} %get-tuple-element.85), channel_id=1, source_target_pairs={{0,4},{1,5},{2,6},{3,7},{4,0},{5,1},{6,2},{7,3},{8,12},{9,13},{10,... | collective-permute-start | bytes 1769480 | tf_op jit(solution)/shard_map/ppermute | solution.py:27
  26.1 2.1 %shard_map.33 = bf16[128,6656]{1,0:T(8,128)(2,1)S(1)} custom-call(s32[3]{0:T(128)S(1)} %pad_add_fusion.where_ref, bf16[768,6656]{1,0:T(8,128)(2,1)} %grad_ref.7), custom_call_target="tpu_custom_call" | custom-call | bytes 3407872 | tf_op jit(solution)/shard_map/pallas_call | solution.py:81
  28.3 2.1 %shard_map.34 = bf16[128,6656]{1,0:T(8,128)(2,1)S(1)} custom-call(s32[3]{0:T(128)S(1)} %pad_add_fusion.where_ref, bf16[768,6656]{1,0:T(8,128)(2,1)} %grad_ref.7), custom_call_target="tpu_custom_call" | custom-call | bytes 3407872 | tf_op jit(solution)/shard_map/pallas_call | solution.py:81
  30.4 3.9 %shard_map.32.pair_ref = bf16[768,6656]{1,0:T(8,128)(2,1)S(1)} custom-call(bf16[768,6656]{1,0:T(8,128)(2,1)} %collective-permute-done.1.source_ref), custom_call_target="tpu_custom_call" | custom-call | bytes 20447232 | tf_op jit(solution)/shard_map/pallas_call | solution.py:99
  34.3 8.3 %collective-permute-done.got_ref = bf16[256,6656]{1,0:T(8,128)(2,1)S(1)} collective-permute-done((bf16[256,6656]{1,0:T(8,128)(2,1)S(1)}, bf16[256,6656]{1,0:T(8,128)(2,1)S(1)}, u32[]{:S(2)}, u32[]{:S(2)}) %collective-permute-start) | collective-permute-done | bytes 3407904 | tf_op jit(solution)/shard_map/ppermute | solution.py:27
  42.6 6.1 %shard_map.35 = (f32[2,2,96,256]{3,2,1,0:T(8,128)S(1)}, f32[2,2,96,256]{3,2,1,0:T(8,128)S(1)}, f32[2,2,96,256]{3,2,1,0:T(8,128)S(1)}, f32[2,2,96,256]{3,2,1,0:T(8,128)S(1)}) custom-call(s32[3]{0:T(128)S(1)} %pad_add_fusion.where_ref, bf16[768,6656]{1,0:T(8,128)(2,1)S(1)} %shard_map.29.own_ref, bf16[768,6656]{1,0:T(8,128)(2,1)S(1)} %shard_map.32.pair_ref, ...), custom_call_target="tpu_custom_call" | custom-call | flops 5234491392 | bytes 27000832 | tf_op jit(solution)/shard_map/pallas_call | solution.py:181
  48.7 0.0 collective-permute-done.2.refs_1_
  48.7 0.0 collective-permute-done.3.refs_2_
  48.7 1.4 collective-permute-done.4.refs_3_
  50.1 3.5 %collective-permute-start.9 = (bf16[128,6656]{1,0:T(8,128)(2,1)S(1)}, bf16[128,6656]{1,0:T(8,128)(2,1)S(1)}, u32[]{:S(2)}, u32[]{:S(2)}) collective-permute-start(bf16[128,6656]{1,0:T(8,128)(2,1)S(1)} %shard_map.33), channel_id=1, source_target_pairs={{0,112},{1,113},{2,114},{3,115},{4,116},{5,117},{6,118},{7,119},{8... | collective-permute-start | bytes 5111816 | tf_op jit(solution)/shard_map/ppermute | solution.py:27
  53.7 1.3 collective-permute-start.5
  55.0 1.4 collective-permute-start.6
  56.4 1.6 %collective-permute-start.7 = (f32[2,2,96,256]{3,2,1,0:T(8,128)S(1)}, f32[2,2,96,256]{3,2,1,0:T(8,128)S(1)}, u32[]{:S(2)}, u32[]{:S(2)}) collective-permute-start(f32[2,2,96,256]{3,2,1,0:T(8,128)S(1)} %get-tuple-element.88), channel_id=1, source_target_pairs={{0,4},{1,5},{2,6},{3,7},{4,0},{5,1},{6,2},{7,3},{8,12},{9,13},{10,... | collective-permute-start | bytes 1179656 | tf_op jit(solution)/shard_map/ppermute | solution.py:27
  58.1 7.8 %collective-permute-done.5.refs_5_ = f32[2,2,96,256]{3,2,1,0:T(8,128)S(1)} collective-permute-done((f32[2,2,96,256]{3,2,1,0:T(8,128)S(1)}, f32[2,2,96,256]{3,2,1,0:T(8,128)S(1)}, u32[]{:S(2)}, u32[]{:S(2)}) %collective-permute-start.5) | collective-permute-done | bytes 393248 | tf_op jit(solution)/shard_map/ppermute | solution.py:27
  65.9 0.0 collective-permute-done.6.refs_6_
  65.9 9.5 %collective-permute-done.7.refs_7_ = f32[2,2,96,256]{3,2,1,0:T(8,128)S(1)} collective-permute-done((f32[2,2,96,256]{3,2,1,0:T(8,128)S(1)}, f32[2,2,96,256]{3,2,1,0:T(8,128)S(1)}, u32[]{:S(2)}, u32[]{:S(2)}) %collective-permute-start.7) | collective-permute-done | bytes 393248 | tf_op jit(solution)/shard_map/ppermute | solution.py:27
  75.4 0.0 collective-permute-start.8
  75.4 3.7 %collective-permute-done.10.got_ref = bf16[256,6656]{1,0:T(8,128)(2,1)S(1)} collective-permute-done((bf16[256,6656]{1,0:T(8,128)(2,1)S(1)}, bf16[256,6656]{1,0:T(8,128)(2,1)S(1)}, u32[]{:S(2)}, u32[]{:S(2)}) %collective-permute-start.10) | collective-permute-done | bytes 3407904 | tf_op jit(solution)/shard_map/ppermute | solution.py:27
  79.1 6.1 %shard_map.36 = (f32[2,2,96,256]{3,2,1,0:T(8,128)S(1)}, f32[2,2,96,256]{3,2,1,0:T(8,128)S(1)}, f32[2,2,96,256]{3,2,1,0:T(8,128)S(1)}, f32[2,2,96,256]{3,2,1,0:T(8,128)S(1)}) custom-call(s32[3]{0:T(128)S(1)} %pad_add_fusion.where_ref, bf16[768,6656]{1,0:T(8,128)(2,1)S(1)} %shard_map.29.own_ref, bf16[768,6656]{1,0:T(8,128)(2,1)S(1)} %shard_map.32.pair_ref, ...), custom_call_target="tpu_custom_call" | custom-call | flops 5234491392 | bytes 27000832 | tf_op jit(solution)/shard_map/pallas_call | solution.py:181
  85.2 1.4 collective-permute-start.11
  86.6 1.5 collective-permute-start.12
  88.1 1.6 %collective-permute-start.13 = (f32[2,2,96,256]{3,2,1,0:T(8,128)S(1)}, f32[2,2,96,256]{3,2,1,0:T(8,128)S(1)}, u32[]{:S(2)}, u32[]{:S(2)}) collective-permute-start(f32[2,2,96,256]{3,2,1,0:T(8,128)S(1)} %get-tuple-element.102), channel_id=1, source_target_pairs={{0,4},{1,5},{2,6},{3,7},{4,0},{5,1},{6,2},{7,3},{8,12},{9,13},{10,... | collective-permute-start | bytes 1179656 | tf_op jit(solution)/shard_map/ppermute | solution.py:27
  89.7 7.7 %collective-permute-done.9.got_ref = bf16[128,6656]{1,0:T(8,128)(2,1)S(1)} collective-permute-done((bf16[128,6656]{1,0:T(8,128)(2,1)S(1)}, bf16[128,6656]{1,0:T(8,128)(2,1)S(1)}, u32[]{:S(2)}, u32[]{:S(2)}) %collective-permute-start.9) | collective-permute-done | bytes 1703968 | tf_op jit(solution)/shard_map/ppermute | solution.py:27
  97.3 6.7 %shard_map.37 = (f32[2,2,96,128]{3,2,1,0:T(8,128)S(1)}, f32[2,2,96,128]{3,2,1,0:T(8,128)S(1)}, f32[2,2,96,128]{3,2,1,0:T(8,128)S(1)}, f32[2,2,96,128]{3,2,1,0:T(8,128)S(1)}) custom-call(s32[3]{0:T(128)S(1)} %pad_add_fusion.where_ref, bf16[768,6656]{1,0:T(8,128)(2,1)S(1)} %shard_map.29.own_ref, bf16[768,6656]{1,0:T(8,128)(2,1)S(1)} %shard_map.32.pair_ref, ...), custom_call_target="tpu_custom_call" | custom-call | flops 2617245696 | bytes 23724032 | tf_op jit(solution)/shard_map/pallas_call | solution.py:181
  104.0 0.0 collective-permute-done.11.refs_9_
  104.0 0.0 collective-permute-done.12.refs_10_
  104.0 0.0 collective-permute-done.13.refs_11_
  104.1 1.4 collective-permute-start.14
  105.4 1.5 collective-permute-start.15
  106.9 1.6 %collective-permute-start.16 = (f32[2,2,96,128]{3,2,1,0:T(8,128)S(1)}, f32[2,2,96,128]{3,2,1,0:T(8,128)S(1)}, u32[]{:S(2)}, u32[]{:S(2)}) collective-permute-start(f32[2,2,96,128]{3,2,1,0:T(8,128)S(1)} %get-tuple-element.105), channel_id=1, source_target_pairs={{0,4},{1,5},{2,6},{3,7},{4,0},{5,1},{6,2},{7,3},{8,12},{9,13},{10,... | collective-permute-start | bytes 589832 | tf_op jit(solution)/shard_map/ppermute | solution.py:27
  108.5 7.1 %collective-permute-done.8.got_ref = bf16[128,6656]{1,0:T(8,128)(2,1)S(1)} collective-permute-done((bf16[128,6656]{1,0:T(8,128)(2,1)S(1)}, bf16[128,6656]{1,0:T(8,128)(2,1)S(1)}, u32[]{:S(2)}, u32[]{:S(2)}) %collective-permute-start.8) | collective-permute-done | bytes 1703968 | tf_op jit(solution)/shard_map/ppermute | solution.py:27
  115.6 0.0 collective-permute-done.14.refs_13_
  115.6 0.0 collective-permute-done.15.refs_14_
  115.6 0.0 collective-permute-done.16.refs_15_
  115.6 0.8 shard_map.38
  116.5 1.3 collective-permute-start.17
  117.8 6.4 %shard_map.39 = (f32[2,2,96,128]{3,2,1,0:T(8,128)S(1)}, f32[2,2,96,128]{3,2,1,0:T(8,128)S(1)}, f32[2,2,96,128]{3,2,1,0:T(8,128)S(1)}, f32[2,2,96,128]{3,2,1,0:T(8,128)S(1)}) custom-call(s32[3]{0:T(128)S(1)} %pad_add_fusion.where_ref, bf16[768,6656]{1,0:T(8,128)(2,1)S(1)} %shard_map.29.own_ref, bf16[768,6656]{1,0:T(8,128)(2,1)S(1)} %shard_map.32.pair_ref, ...), custom_call_target="tpu_custom_call" | custom-call | flops 2617245696 | bytes 23724032 | tf_op jit(solution)/shard_map/pallas_call | solution.py:181
  124.2 0.0 copy-start
  124.2 1.4 collective-permute-start.18
  125.6 1.5 collective-permute-start.19
  127.1 1.6 %collective-permute-start.20 = (f32[2,2,96,128]{3,2,1,0:T(8,128)S(1)}, f32[2,2,96,128]{3,2,1,0:T(8,128)S(1)}, u32[]{:S(2)}, u32[]{:S(2)}) collective-permute-start(f32[2,2,96,128]{3,2,1,0:T(8,128)S(1)} %get-tuple-element.130), channel_id=1, source_target_pairs={{0,4},{1,5},{2,6},{3,7},{4,0},{5,1},{6,2},{7,3},{8,12},{9,13},{10,... | collective-permute-start | bytes 589832 | tf_op jit(solution)/shard_map/ppermute | solution.py:27
  128.7 1.4 collective-permute-done.18.piece_1
  130.1 1.7 %collective-permute-done.19.piece_2 = f32[2,2,96,128]{3,2,1,0:T(8,128)S(1)} collective-permute-done((f32[2,2,96,128]{3,2,1,0:T(8,128)S(1)}, f32[2,2,96,128]{3,2,1,0:T(8,128)S(1)}, u32[]{:S(2)}, u32[]{:S(2)}) %collective-permute-start.19) | collective-permute-done | bytes 196640 | tf_op jit(solution)/shard_map/ppermute | solution.py:27
  131.8 1.6 %collective-permute-done.20.piece_3 = f32[2,2,96,128]{3,2,1,0:T(8,128)S(1)} collective-permute-done((f32[2,2,96,128]{3,2,1,0:T(8,128)S(1)}, f32[2,2,96,128]{3,2,1,0:T(8,128)S(1)}, u32[]{:S(2)}, u32[]{:S(2)}) %collective-permute-start.20) | collective-permute-done | bytes 196640 | tf_op jit(solution)/shard_map/ppermute | solution.py:27
  133.4 0.0 collective-permute-done.17.got_ref
  133.4 0.7 shard_map.40
  134.1 5.7 %collective-permute-start.21 = (f32[96,768]{1,0:T(8,128)S(1)}, f32[96,768]{1,0:T(8,128)S(1)}, u32[]{:S(2)}, u32[]{:S(2)}) collective-permute-start(f32[96,768]{1,0:T(8,128)S(1)} %get-tuple-element.132), channel_id=1, source_target_pairs={{0,8},{1,9},{2,10},{3,11},{4,12},{5,13},{6,14},{7,15},{8,0},{9,1},... | collective-permute-start | bytes 884744 | tf_op jit(solution)/shard_map/ppermute | solution.py:27
  139.8 2.1 %collective-permute-start.24 = (f32[96,128]{1,0:T(8,128)S(1)}, f32[96,128]{1,0:T(8,128)S(1)}, u32[]{:S(2)}, u32[]{:S(2)}) collective-permute-start(f32[96,128]{1,0:T(8,128)S(1)} %get-tuple-element.136), channel_id=1, source_target_pairs={{0,1},{1,0},{2,3},{3,2},{4,5},{5,4},{6,7},{7,6},{8,121},{9,120},{1... | collective-permute-start | bytes 147464 | tf_op jit(solution)/shard_map/ppermute | solution.py:27
  141.9 2.6 %collective-permute-start.23 = (f32[96,768]{1,0:T(8,128)S(1)}, f32[96,768]{1,0:T(8,128)S(1)}, u32[]{:S(2)}, u32[]{:S(2)}) collective-permute-start(f32[96,768]{1,0:T(8,128)S(1)} %get-tuple-element.134), channel_id=1, source_target_pairs={{0,0},{1,1},{2,2},{3,3},{4,4},{5,5},{6,6},{7,7},{8,120},{9,121},{1... | collective-permute-start | bytes 884744 | tf_op jit(solution)/shard_map/ppermute | solution.py:27
  144.5 3.0 %collective-permute-done.24 = f32[96,128]{1,0:T(8,128)S(1)} collective-permute-done((f32[96,128]{1,0:T(8,128)S(1)}, f32[96,128]{1,0:T(8,128)S(1)}, u32[]{:S(2)}, u32[]{:S(2)}) %collective-permute-start.24) | collective-permute-done | bytes 49184 | tf_op jit(solution)/shard_map/ppermute | solution.py:27
  147.6 0.0 collective-permute-done.22
  147.7 6.8 %collective-permute-done.23 = f32[96,768]{1,0:T(8,128)S(1)} collective-permute-done((f32[96,768]{1,0:T(8,128)S(1)}, f32[96,768]{1,0:T(8,128)S(1)}, u32[]{:S(2)}, u32[]{:S(2)}) %collective-permute-start.23) | collective-permute-done | bytes 294944 | tf_op jit(solution)/shard_map/ppermute | solution.py:27
  154.5 1.0 fusion
  (10 shorter events, 0.1 us)
Async XLA Ops:
  0.0 20.0 %collective-permute-start.1 = (bf16[768,6656]{1,0:T(8,128)(2,1)}, bf16[768,6656]{1,0:T(8,128)(2,1)}, u32[]{:S(2)}, u32[]{:S(2)}) collective-permute-start(bf16[768,6656]{1,0:T(8,128)(2,1)} %grad_ref.7), channel_id=1, source_target_pairs={{0,8},{1,9},{2,10},{3,11},{4,12},{5,13},{6,14},{7,15},{8,0},{9,1},... | collective-permute-start | bytes 30670856 | tf_op jit(solution)/shard_map/ppermute | solution.py:27
  3.3 39.3 %collective-permute-start = (bf16[256,6656]{1,0:T(8,128)(2,1)S(1)}, bf16[256,6656]{1,0:T(8,128)(2,1)S(1)}, u32[]{:S(2)}, u32[]{:S(2)}) collective-permute-start(bf16[256,6656]{1,0:T(8,128)(2,1)S(1)} %shard_map.28), channel_id=1, source_target_pairs={{0,112},{1,113},{2,114},{3,115},{4,116},{5,117},{6,118},{7,119},{8... | collective-permute-start | bytes 10223624 | tf_op jit(solution)/shard_map/ppermute | solution.py:27
  20.0 59.0 %collective-permute-start.10 = (bf16[256,6656]{1,0:T(8,128)(2,1)S(1)}, bf16[256,6656]{1,0:T(8,128)(2,1)S(1)}, u32[]{:S(2)}, u32[]{:S(2)}) collective-permute-start(bf16[256,6656]{1,0:T(8,128)(2,1)S(1)} %shard_map.31), channel_id=1, source_target_pairs={{0,112},{1,113},{2,114},{3,115},{4,116},{5,117},{6,118},{7,119},{8... | collective-permute-start | bytes 10223624 | tf_op jit(solution)/shard_map/ppermute | solution.py:27
  21.8 27.0 %collective-permute-start.2 = (f32[2,96,768]{2,1,0:T(8,128)S(1)}, f32[2,96,768]{2,1,0:T(8,128)S(1)}, u32[]{:S(2)}, u32[]{:S(2)}) collective-permute-start(f32[2,96,768]{2,1,0:T(8,128)S(1)} %get-tuple-element.83), channel_id=1, source_target_pairs={{0,2},{1,3},{2,4},{3,5},{4,6},{5,7},{6,0},{7,1},{8,10},{9,11},{10,... | collective-permute-start | bytes 1769480 | tf_op jit(solution)/shard_map/ppermute | solution.py:27
  23.1 25.7 %collective-permute-start.3 = (f32[2,96,768]{2,1,0:T(8,128)S(1)}, f32[2,96,768]{2,1,0:T(8,128)S(1)}, u32[]{:S(2)}, u32[]{:S(2)}) collective-permute-start(f32[2,96,768]{2,1,0:T(8,128)S(1)} %get-tuple-element.84), channel_id=1, source_target_pairs={{0,6},{1,7},{2,0},{3,1},{4,2},{5,3},{6,4},{7,5},{8,14},{9,15},{10,... | collective-permute-start | bytes 1769480 | tf_op jit(solution)/shard_map/ppermute | solution.py:27
  24.5 25.7 %collective-permute-start.4 = (f32[2,96,768]{2,1,0:T(8,128)S(1)}, f32[2,96,768]{2,1,0:T(8,128)S(1)}, u32[]{:S(2)}, u32[]{:S(2)}) collective-permute-start(f32[2,96,768]{2,1,0:T(8,128)S(1)} %get-tuple-element.85), channel_id=1, source_target_pairs={{0,4},{1,5},{2,6},{3,7},{4,0},{5,1},{6,2},{7,3},{8,12},{9,13},{10,... | collective-permute-start | bytes 1769480 | tf_op jit(solution)/shard_map/ppermute | solution.py:27
  50.1 47.2 %collective-permute-start.9 = (bf16[128,6656]{1,0:T(8,128)(2,1)S(1)}, bf16[128,6656]{1,0:T(8,128)(2,1)S(1)}, u32[]{:S(2)}, u32[]{:S(2)}) collective-permute-start(bf16[128,6656]{1,0:T(8,128)(2,1)S(1)} %shard_map.33), channel_id=1, source_target_pairs={{0,112},{1,113},{2,114},{3,115},{4,116},{5,117},{6,118},{7,119},{8... | collective-permute-start | bytes 5111816 | tf_op jit(solution)/shard_map/ppermute | solution.py:27
  53.7 12.2 %collective-permute-start.5 = (f32[2,2,96,256]{3,2,1,0:T(8,128)S(1)}, f32[2,2,96,256]{3,2,1,0:T(8,128)S(1)}, u32[]{:S(2)}, u32[]{:S(2)}) collective-permute-start(f32[2,2,96,256]{3,2,1,0:T(8,128)S(1)} %get-tuple-element.86), channel_id=1, source_target_pairs={{0,2},{1,3},{2,4},{3,5},{4,6},{5,7},{6,0},{7,1},{8,10},{9,11},{10,... | collective-permute-start | bytes 1179656 | tf_op jit(solution)/shard_map/ppermute | solution.py:27
  55.0 10.9 %collective-permute-start.6 = (f32[2,2,96,256]{3,2,1,0:T(8,128)S(1)}, f32[2,2,96,256]{3,2,1,0:T(8,128)S(1)}, u32[]{:S(2)}, u32[]{:S(2)}) collective-permute-start(f32[2,2,96,256]{3,2,1,0:T(8,128)S(1)} %get-tuple-element.87), channel_id=1, source_target_pairs={{0,6},{1,7},{2,0},{3,1},{4,2},{5,3},{6,4},{7,5},{8,14},{9,15},{10,... | collective-permute-start | bytes 1179656 | tf_op jit(solution)/shard_map/ppermute | solution.py:27
  56.4 19.0 %collective-permute-start.7 = (f32[2,2,96,256]{3,2,1,0:T(8,128)S(1)}, f32[2,2,96,256]{3,2,1,0:T(8,128)S(1)}, u32[]{:S(2)}, u32[]{:S(2)}) collective-permute-start(f32[2,2,96,256]{3,2,1,0:T(8,128)S(1)} %get-tuple-element.88), channel_id=1, source_target_pairs={{0,4},{1,5},{2,6},{3,7},{4,0},{5,1},{6,2},{7,3},{8,12},{9,13},{10,... | collective-permute-start | bytes 1179656 | tf_op jit(solution)/shard_map/ppermute | solution.py:27
  75.4 40.2 %collective-permute-start.8 = (bf16[128,6656]{1,0:T(8,128)(2,1)S(1)}, bf16[128,6656]{1,0:T(8,128)(2,1)S(1)}, u32[]{:S(2)}, u32[]{:S(2)}) collective-permute-start(bf16[128,6656]{1,0:T(8,128)(2,1)S(1)} %shard_map.34), channel_id=1, source_target_pairs={{0,112},{1,113},{2,114},{3,115},{4,116},{5,117},{6,118},{7,119},{8... | collective-permute-start | bytes 5111816 | tf_op jit(solution)/shard_map/ppermute | solution.py:27
  85.2 18.8 %collective-permute-start.11 = (f32[2,2,96,256]{3,2,1,0:T(8,128)S(1)}, f32[2,2,96,256]{3,2,1,0:T(8,128)S(1)}, u32[]{:S(2)}, u32[]{:S(2)}) collective-permute-start(f32[2,2,96,256]{3,2,1,0:T(8,128)S(1)} %get-tuple-element.100), channel_id=1, source_target_pairs={{0,2},{1,3},{2,4},{3,5},{4,6},{5,7},{6,0},{7,1},{8,10},{9,11},{10,... | collective-permute-start | bytes 1179656 | tf_op jit(solution)/shard_map/ppermute | solution.py:27
  86.6 17.4 %collective-permute-start.12 = (f32[2,2,96,256]{3,2,1,0:T(8,128)S(1)}, f32[2,2,96,256]{3,2,1,0:T(8,128)S(1)}, u32[]{:S(2)}, u32[]{:S(2)}) collective-permute-start(f32[2,2,96,256]{3,2,1,0:T(8,128)S(1)} %get-tuple-element.101), channel_id=1, source_target_pairs={{0,6},{1,7},{2,0},{3,1},{4,2},{5,3},{6,4},{7,5},{8,14},{9,15},{10,... | collective-permute-start | bytes 1179656 | tf_op jit(solution)/shard_map/ppermute | solution.py:27
  88.1 15.9 %collective-permute-start.13 = (f32[2,2,96,256]{3,2,1,0:T(8,128)S(1)}, f32[2,2,96,256]{3,2,1,0:T(8,128)S(1)}, u32[]{:S(2)}, u32[]{:S(2)}) collective-permute-start(f32[2,2,96,256]{3,2,1,0:T(8,128)S(1)} %get-tuple-element.102), channel_id=1, source_target_pairs={{0,4},{1,5},{2,6},{3,7},{4,0},{5,1},{6,2},{7,3},{8,12},{9,13},{10,... | collective-permute-start | bytes 1179656 | tf_op jit(solution)/shard_map/ppermute | solution.py:27
  104.1 11.5 %collective-permute-start.14 = (f32[2,2,96,128]{3,2,1,0:T(8,128)S(1)}, f32[2,2,96,128]{3,2,1,0:T(8,128)S(1)}, u32[]{:S(2)}, u32[]{:S(2)}) collective-permute-start(f32[2,2,96,128]{3,2,1,0:T(8,128)S(1)} %get-tuple-element.103), channel_id=1, source_target_pairs={{0,2},{1,3},{2,4},{3,5},{4,6},{5,7},{6,0},{7,1},{8,10},{9,11},{10,... | collective-permute-start | bytes 589832 | tf_op jit(solution)/shard_map/ppermute | solution.py:27
  105.4 10.2 %collective-permute-start.15 = (f32[2,2,96,128]{3,2,1,0:T(8,128)S(1)}, f32[2,2,96,128]{3,2,1,0:T(8,128)S(1)}, u32[]{:S(2)}, u32[]{:S(2)}) collective-permute-start(f32[2,2,96,128]{3,2,1,0:T(8,128)S(1)} %get-tuple-element.104), channel_id=1, source_target_pairs={{0,6},{1,7},{2,0},{3,1},{4,2},{5,3},{6,4},{7,5},{8,14},{9,15},{10,... | collective-permute-start | bytes 589832 | tf_op jit(solution)/shard_map/ppermute | solution.py:27
  106.9 8.7 %collective-permute-start.16 = (f32[2,2,96,128]{3,2,1,0:T(8,128)S(1)}, f32[2,2,96,128]{3,2,1,0:T(8,128)S(1)}, u32[]{:S(2)}, u32[]{:S(2)}) collective-permute-start(f32[2,2,96,128]{3,2,1,0:T(8,128)S(1)} %get-tuple-element.105), channel_id=1, source_target_pairs={{0,4},{1,5},{2,6},{3,7},{4,0},{5,1},{6,2},{7,3},{8,12},{9,13},{10,... | collective-permute-start | bytes 589832 | tf_op jit(solution)/shard_map/ppermute | solution.py:27
  116.5 17.0 %collective-permute-start.17 = (f32[3,96,768]{2,1,0:T(8,128)S(1)}, f32[3,96,768]{2,1,0:T(8,128)S(1)}, u32[]{:S(2)}, u32[]{:S(2)}) collective-permute-start(f32[3,96,768]{2,1,0:T(8,128)S(1)} %get-tuple-element.125), channel_id=1, source_target_pairs={{0,1},{1,0},{2,3},{3,2},{4,5},{5,4},{6,7},{7,6},{8,9},{9,8},{10,11... | collective-permute-start | bytes 2654216 | tf_op jit(solution)/shard_map/ppermute | solution.py:27
  124.2 30.3 %copy-start = (f32[96,3,768]{2,0,1:T(8,128)S(1)}, f32[96,3,768]{2,0,1:T(8,128)}, u32[]{:S(2)}) copy-start(f32[96,3,768]{2,0,1:T(8,128)} %param.3) | copy-start | bytes 2654212
  124.2 5.9 %collective-permute-start.18 = (f32[2,2,96,128]{3,2,1,0:T(8,128)S(1)}, f32[2,2,96,128]{3,2,1,0:T(8,128)S(1)}, u32[]{:S(2)}, u32[]{:S(2)}) collective-permute-start(f32[2,2,96,128]{3,2,1,0:T(8,128)S(1)} %get-tuple-element.128), channel_id=1, source_target_pairs={{0,2},{1,3},{2,4},{3,5},{4,6},{5,7},{6,0},{7,1},{8,10},{9,11},{10,... | collective-permute-start | bytes 589832 | tf_op jit(solution)/shard_map/ppermute | solution.py:27
  125.6 6.2 %collective-permute-start.19 = (f32[2,2,96,128]{3,2,1,0:T(8,128)S(1)}, f32[2,2,96,128]{3,2,1,0:T(8,128)S(1)}, u32[]{:S(2)}, u32[]{:S(2)}) collective-permute-start(f32[2,2,96,128]{3,2,1,0:T(8,128)S(1)} %get-tuple-element.129), channel_id=1, source_target_pairs={{0,6},{1,7},{2,0},{3,1},{4,2},{5,3},{6,4},{7,5},{8,14},{9,15},{10,... | collective-permute-start | bytes 589832 | tf_op jit(solution)/shard_map/ppermute | solution.py:27
  127.1 6.3 %collective-permute-start.20 = (f32[2,2,96,128]{3,2,1,0:T(8,128)S(1)}, f32[2,2,96,128]{3,2,1,0:T(8,128)S(1)}, u32[]{:S(2)}, u32[]{:S(2)}) collective-permute-start(f32[2,2,96,128]{3,2,1,0:T(8,128)S(1)} %get-tuple-element.130), channel_id=1, source_target_pairs={{0,4},{1,5},{2,6},{3,7},{4,0},{5,1},{6,2},{7,3},{8,12},{9,13},{10,... | collective-permute-start | bytes 589832 | tf_op jit(solution)/shard_map/ppermute | solution.py:27
  134.1 13.5 %collective-permute-start.21 = (f32[96,768]{1,0:T(8,128)S(1)}, f32[96,768]{1,0:T(8,128)S(1)}, u32[]{:S(2)}, u32[]{:S(2)}) collective-permute-start(f32[96,768]{1,0:T(8,128)S(1)} %get-tuple-element.132), channel_id=1, source_target_pairs={{0,8},{1,9},{2,10},{3,11},{4,12},{5,13},{6,14},{7,15},{8,0},{9,1},... | collective-permute-start | bytes 884744 | tf_op jit(solution)/shard_map/ppermute | solution.py:27
  139.8 7.7 %collective-permute-start.24 = (f32[96,128]{1,0:T(8,128)S(1)}, f32[96,128]{1,0:T(8,128)S(1)}, u32[]{:S(2)}, u32[]{:S(2)}) collective-permute-start(f32[96,128]{1,0:T(8,128)S(1)} %get-tuple-element.136), channel_id=1, source_target_pairs={{0,1},{1,0},{2,3},{3,2},{4,5},{5,4},{6,7},{7,6},{8,121},{9,120},{1... | collective-permute-start | bytes 147464 | tf_op jit(solution)/shard_map/ppermute | solution.py:27
  141.9 5.7 %collective-permute-start.22 = (f32[96,128]{1,0:T(8,128)S(1)}, f32[96,128]{1,0:T(8,128)S(1)}, u32[]{:S(2)}, u32[]{:S(2)}) collective-permute-start(f32[96,128]{1,0:T(8,128)S(1)} %get-tuple-element.135), channel_id=1, source_target_pairs={{0,9},{1,8},{2,11},{3,10},{4,13},{5,12},{6,15},{7,14},{8,1},{9,0},... | collective-permute-start | bytes 147464 | tf_op jit(solution)/shard_map/ppermute | solution.py:27
  141.9 12.6 %collective-permute-start.23 = (f32[96,768]{1,0:T(8,128)S(1)}, f32[96,768]{1,0:T(8,128)S(1)}, u32[]{:S(2)}, u32[]{:S(2)}) collective-permute-start(f32[96,768]{1,0:T(8,128)S(1)} %get-tuple-element.134), channel_id=1, source_target_pairs={{0,0},{1,1},{2,2},{3,3},{4,4},{5,5},{6,6},{7,7},{8,120},{9,121},{1... | collective-permute-start | bytes 884744 | tf_op jit(solution)/shard_map/ppermute | solution.py:27

commit v2 on v1

v2 whole, which is shorter than its diff:
```python
import functools

import jax
import jax.numpy as jnp
from jax import lax
from jax.experimental import pallas as pl
from jax.experimental.pallas import tpu as pltpu
from jax.sharding import PartitionSpec as P

COLS = 53248
decay_rate = 0.95
CHUNKS = (256, 256, 128, 128)
BEGINS = (0, 256, 512, 640)
VMEM_LIMIT = 5 << 20
SPLIT = 4608
FIRST = 2
AXES = ("fsdp", "tensor")


def place(x_hi, z, core, y, x_lo):
    return ((x_hi % 2) * 8 + (z % 4) * 2 + core) * 8 + (y % 4) * 2 + x_lo


def moved(value, target):
    pairs = []
    for source in range(128):
        block, shard = divmod(source, 8)
        pairs.append((source, target(block // 8, (block // 2) % 4, block % 2, shard // 2, shard % 2)))
    return lax.ppermute(value, AXES, pairs)


def next_chip(x_hi, z, core, y, x_lo, steps):
    chip = (x_hi * 4 + z + steps) % 8
    return place(chip // 4, chip % 4, core, y, x_lo)


def block_flow(x_hi, z, core, y, x_lo):
    return next_chip(x_hi, z, 1 - core, y, x_lo, 1 if core else -1)


def swap_cores(x_hi, z, core, y, x_lo):
    return place(x_hi, z, 1 - core, y, x_lo)


def swap_x(x_hi, z, core, y, x_lo):
    return place(x_hi, z, core, y, 1 - x_lo)


def to_owner(x_hi, z, core, y, x_lo):
    return next_chip(x_hi, z, 1 - core, y, x_lo, 0 if core else -1)


def to_owner_x(x_hi, z, core, y, x_lo):
    return to_owner(x_hi, z, core, y, 1 - x_lo)


def along_y(steps):
    return lambda x_hi, z, core, y, x_lo: place(x_hi, z, core, y + steps, x_lo)


def contract(left, right):
    return lax.dot_general(left, right, (((1,), (1,)), ((), ())), preferred_element_type=jnp.float32)


def pick_kernel(begin, thin, span, where_ref, grad_ref, out_ref, sems):
    core = where_ref[0]
    copies = []
    for i in range(8):
        offset = pl.multiple_of(jnp.where(core == 0, begin + thin * i, 96 * i + begin // 8), 16)
        source = grad_ref.at[pl.ds(offset, thin), pl.ds(span[0], span[1] - span[0])]
        copies.append(pltpu.make_async_copy(source, out_ref.at[pl.ds(thin * i, thin)], sems.at[i]))
    for copy in copies:
        copy.start()
    for copy in copies:
        copy.wait()


def picked(where, grad, begin, wide, span):
    depth = span[1] - span[0]
    return pl.pallas_call(
        functools.partial(pick_kernel, begin, wide // 8, span),
        out_shape=jax.ShapeDtypeStruct((wide, depth), grad.dtype),
        in_specs=[pl.BlockSpec(memory_space=pltpu.SMEM), pl.BlockSpec(memory_space=pl.ANY)],
        out_specs=pl.BlockSpec(memory_space=pltpu.VMEM),
        scratch_shapes=[pltpu.SemaphoreType.DMA((8,))],
        cost_estimate=pl.CostEstimate(flops=0, bytes_accessed=4 * wide * depth, transcendentals=0),
        compiler_params=pltpu.CompilerParams(vmem_limit_bytes=VMEM_LIMIT),
    )(where, pltpu.with_memory_space_constraint(grad, pltpu.HBM))


def hold_kernel(source_ref, out_ref, sem):
    copy = pltpu.make_async_copy(source_ref, out_ref, sem)
    copy.start()
    copy.wait()


def held(value):
    return pl.pallas_call(
        hold_kernel,
        out_shape=pltpu.VMEM(value.shape, value.dtype),
        in_specs=[pl.BlockSpec(memory_space=pl.ANY)],
        out_specs=pl.BlockSpec(memory_space=pltpu.VMEM),
        scratch_shapes=[pltpu.SemaphoreType.DMA],
        cost_estimate=pl.CostEstimate(flops=0, bytes_accessed=4 * value.size, transcendentals=0),
        compiler_params=pltpu.CompilerParams(vmem_limit_bytes=VMEM_LIMIT),
    )(pltpu.with_memory_space_constraint(value, pltpu.HBM))


def resident(value):
    return pltpu.with_memory_space_constraint(value, pltpu.VMEM)


def vmem_specs(count):
    return [pl.BlockSpec(memory_space=pltpu.SMEM)] + [pl.BlockSpec(memory_space=pltpu.VMEM)] * count


def owner_rows(y, hop, side, count):
    shard = 2 * ((y + hop) & 3) + side
    return pl.ds(pl.multiple_of(count * shard, count), count)


def square_kernel(where_ref, own_ref, *refs):
    outs, total = refs[:4], refs[4]
    y = where_ref[1]
    total[...] = contract(own_ref[...], own_ref[...])
    for hop in range(4):
        for side in range(2):
            outs[hop][side] = total[owner_rows(y, hop, side, 96), :]


def squared(where, grad):
    rows, depth = grad.shape
    piece = (2, rows // 8, rows)
    return pl.pallas_call(
        square_kernel,
        out_shape=[jax.ShapeDtypeStruct(piece, jnp.float32)] * 4,
        in_specs=vmem_specs(1),
        out_specs=[pl.BlockSpec(memory_space=pltpu.VMEM)] * 4,
        scratch_shapes=[pltpu.VMEM((rows, rows), jnp.float32)],
        cost_estimate=pl.CostEstimate(
            flops=2 * rows * rows * depth, bytes_accessed=2 * depth * rows + 4 * rows * rows, transcendentals=0
        ),
        compiler_params=pltpu.CompilerParams(vmem_limit_bytes=VMEM_LIMIT),
    )(where, resident(grad))


def cut_up(core, y, tall, flat, mixed, outs):
    wide = mixed.shape[1]
    thin = wide // 8

    @pl.when(core != 0)
    def _():
        for hop in range(4):
            for side in range(2):
                outs[hop][side, 0] = tall[owner_rows(y, hop, side, 96), :]

    @pl.when(core == 0)
    def _():
        for hop in range(4):
            for side in range(2):
                rows = owner_rows(y, hop, side, thin)
                for i in range(768 // wide):
                    outs[hop][side, 0, i * thin : (i + 1) * thin, :] = flat[rows, i * wide : (i + 1) * wide]

    for hop in range(4):
        for side in range(2):
            outs[hop][side, 1] = mixed[owner_rows(y, hop, side, 96), :]


def cross_kernel(begin, where_ref, own_ref, pair_ref, got_ref, *refs):
    outs, (tall, flat, mixed) = refs[:4], refs[4:]
    core = where_ref[0]
    wide = got_ref.shape[0]

    @pl.when(core == 0)
    def _():
        flat[...] = contract(got_ref[...], pair_ref[...])
        mixed[...] = contract(own_ref[...], pair_ref[begin : begin + wide, :])

    @pl.when(core != 0)
    def _():
        tall[...] = contract(pair_ref[...], got_ref[...])
        mixed[...] = contract(own_ref[...], got_ref[...])

    cut_up(core, where_ref[1], tall, flat, mixed, outs)


def early_kernel(begin, wide, where_ref, own_ref, pair_ref, mixed_ref):
    @pl.when(where_ref[0] == 0)
    def _():
        mixed_ref[...] = contract(own_ref[...], pair_ref[begin : begin + wide, :])


def middle_kernel(where_ref, own_ref, pair_ref, got_ref, tall_ref, mixed_ref):
    @pl.when(where_ref[3] != 0)
    def _():
        tall_ref[...] = contract(pair_ref[...], got_ref[...])
        mixed_ref[...] = contract(own_ref[...], got_ref[...])


def late_kernel(where_ref, own_ref, pair_ref, got_ref, early_ref, tall_ref, middle_ref, *refs):
    outs, (tall, flat, mixed) = refs[:4], refs[4:]
    core, ahead = where_ref[0], where_ref[3]

    @pl.when(core == 0)
    def _():
        flat[...] = contract(got_ref[...], pair_ref[...])
        mixed[...] = early_ref[...]

    @pl.when((core != 0) & (ahead == 0))
    def _():
        tall[...] = contract(pair_ref[...], got_ref[...])
        mixed[...] = contract(own_ref[...], got_ref[...])

    @pl.when(ahead != 0)
    def _():
        tall[...] = tall_ref[...]
        mixed[...] = middle_ref[...]

    cut_up(core, where_ref[1], tall, flat, mixed, outs)


def product_call(kernel, shapes, scratch, flops, where, *arrays):
    return pl.pallas_call(
        kernel,
        out_shape=[jax.ShapeDtypeStruct(shape, jnp.float32) for shape in shapes],
        in_specs=vmem_specs(len(arrays)),
        out_specs=[pl.BlockSpec(memory_space=pltpu.VMEM)] * len(shapes),
        scratch_shapes=[pltpu.VMEM(shape, jnp.float32) for shape in scratch],
        cost_estimate=pl.CostEstimate(flops=flops, bytes_accessed=4 * flops // 768, transcendentals=0),
        compiler_params=pltpu.CompilerParams(vmem_limit_bytes=VMEM_LIMIT),
    )(where, *[resident(array) for array in arrays])


def crossed(where, grad, partner, arrived, begin):
    wide, depth = arrived.shape
    rows = grad.shape[0]
    pieces = [(2, 2, rows // 8, wide)] * 4
    sums = [(rows, wide), (wide, rows), (rows, wide)]
    kernel = functools.partial(cross_kernel, begin)
    return product_call(kernel, pieces, sums, 4 * rows * wide * depth, where, grad, partner, arrived)


def total_of(refs, *at):
    return (refs[0][at] + refs[1][at]) + (refs[2][at] + refs[3][at])


def columns_of(product, part):
    start = 768 + product * BEGINS[FIRST] + BEGINS[part]
    return slice(start, start + CHUNKS[part])


def first_sums_kernel(where_ref, *refs):
    x_lo = where_ref[2]
    for side, out_ref in ((x_lo, refs[-2]), (1 - x_lo, refs[-1])):
        out_ref[:, :768] = total_of(refs[:4], side)
        for j in range(FIRST):
            for product in range(2):
                out_ref[:, columns_of(product, j)] = total_of(refs[4 + 4 * j : 8 + 4 * j], side, product)


def first_sums(where, pieces):
    shape = jax.ShapeDtypeStruct((96, 768 + 2 * BEGINS[FIRST]), jnp.float32)
    return pl.pallas_call(
        first_sums_kernel,
        out_shape=[shape, shape],
        in_specs=vmem_specs(len(pieces)),
        out_specs=[pl.BlockSpec(memory_space=pltpu.VMEM)] * 2,
        cost_estimate=pl.CostEstimate(flops=4 * 3 * 96 * 768 * 2, bytes_accessed=10 * 3 * 96 * 768 * 4, transcendentals=0),
        compiler_params=pltpu.CompilerParams(vmem_limit_bytes=2 * VMEM_LIMIT),
    )(where, *pieces)


def far_sums_kernel(where_ref, keep_ref, got_ref, *refs):
    pieces, (far_ref, give_ref) = refs[:-2], refs[-2:]
    core, x_lo = where_ref[0], where_ref[2]
    start = BEGINS[FIRST]
    for j in range(FIRST, len(CHUNKS)):
        columns = slice(BEGINS[j] - start, BEGINS[j] - start + CHUNKS[j])
        give_ref[:, columns] = total_of(pieces[4 * (j - FIRST) : 4 * (j - FIRST) + 4], 1 - x_lo, 0)

    @pl.when(core != 0)
    def _():
        far_ref[:, :start] = keep_ref[:, 768 : 768 + start] + got_ref[:, 768 : 768 + start]
        for j in range(FIRST, len(CHUNKS)):
            columns = slice(BEGINS[j], BEGINS[j] + CHUNKS[j])
            far_ref[:, columns] = total_of(pieces[4 * (j - FIRST) : 4 * (j - FIRST) + 4], x_lo, 0)

    @pl.when(core == 0)
    def _():
        for j, (begin, wide) in enumerate(zip(BEGINS, CHUNKS)):
            thin = wide // 8
            for i in range(768 // wide):
                rows = slice(i * thin, (i + 1) * thin)
                if j < FIRST:
                    value = keep_ref[rows, columns_of(0, j)] + got_ref[rows, columns_of(0, j)]
                else:
                    value = total_of(pieces[4 * (j - FIRST) : 4 * (j - FIRST) + 4], x_lo, 0, rows)
                far_ref[begin // 8 : begin // 8 + thin, i * wide : (i + 1) * wide] = value


def near_sums_kernel(where_ref, keep_ref, got_ref, *refs):
    pieces, (diagonal_ref, near_ref, give_ref) = refs[:-3], refs[-3:]
    x_lo = where_ref[2]
    start = BEGINS[FIRST]
    diagonal_ref[...] = keep_ref[:, :768] + got_ref[:, :768]
    near_ref[:, :start] = keep_ref[:, 768 + start :] + got_ref[:, 768 + start :]
    for j in range(FIRST, len(CHUNKS)):
        part = pieces[4 * (j - FIRST) : 4 * (j - FIRST) + 4]
        near_ref[:, BEGINS[j] : BEGINS[j] + CHUNKS[j]] = total_of(part, x_lo, 1)
        give_ref[:, BEGINS[j] - start : BEGINS[j] - start + CHUNKS[j]] = total_of(part, 1 - x_lo, 1)


def last_sums(kernel, widths, where, keep, got, pieces):
    return pl.pallas_call(
        kernel,
        out_shape=[jax.ShapeDtypeStruct((96, wide), jnp.float32) for wide in widths],
        in_specs=vmem_specs(2 + len(pieces)),
        out_specs=[pl.BlockSpec(memory_space=pltpu.VMEM)] * len(widths),
        cost_estimate=pl.CostEstimate(flops=2 * 3 * 96 * 768, bytes_accessed=4 * 3 * 96 * 768 * 4, transcendentals=0),
        compiler_params=pltpu.CompilerParams(vmem_limit_bytes=VMEM_LIMIT),
    )(where, keep, got, *pieces)


def tied(*values):
    return lax.optimization_barrier(values)


def shards(grad, old_stats):
    rows = grad.shape[0]
    core = lax.axis_index("fsdp") & 1
    y, x_lo = lax.axis_index("tensor") >> 1, lax.axis_index("tensor") & 1
    ahead = core * ((lax.axis_index("fsdp") & 6) == 0)
    where = jnp.stack([core, y, x_lo, ahead]).astype(jnp.int32)

    def spread(pieces):
        return [moved(pieces[hop], along_y(hop)) for hop in (1, 3, 2)]

    def pick(j, span=(0, grad.shape[1])):
        return picked(where, grad, BEGINS[j], CHUNKS[j], span)

    def cross(j):
        return list(crossed(where, here, partner, flight[j], BEGINS[j]))

    partner = moved(grad, swap_cores)
    flight = [moved(pick(0), block_flow)]
    here = held(grad)
    square = squared(where, here)
    *square, partner, out1 = tied(*square, partner, pick(1))
    flight.append(moved(out1, block_flow))
    square_got = spread(square)
    partner = held(partner)
    out2, out3 = pick(2), pick(3)
    flight[0], partner, out2, out3 = tied(flight[0], partner, out2, out3)

    part0 = cross(0)
    *part0, out2, square_got[0], square_got[1], square_got[2] = tied(*part0, out2, *square_got)
    got0 = spread(part0)
    flight.append(moved(out2, block_flow))

    out3, got0[0], got0[1], got0[2] = tied(out3, *got0)
    flight.append(moved(out3, block_flow))
    flight[1], part0[0] = tied(flight[1], part0[0])
    part1 = cross(1)
    got1 = spread(part1)

    flight[2], part1[0] = tied(flight[2], part1[0])
    part2 = cross(2)
    *part2, got1[0], got1[1], got1[2] = tied(*part2, *got1)
    got2 = spread(part2)

    firsts = [square[0], *square_got, part0[0], *got0, part1[0], *got1]
    keep, give = first_sums(where, firsts)
    wide, start = CHUNKS[3], BEGINS[3]
    flops = 2 * rows * wide * grad.shape[1]
    tall = (rows, wide)
    (early,) = product_call(functools.partial(early_kernel, start, wide), [tall], [], flops, where, here, partner)
    flight[3], early, keep = tied(flight[3], early, keep)
    far3, near3 = product_call(middle_kernel, [tall, tall], [], flops, where, here, partner, flight[3])
    give, far3, got2[0], got2[1], got2[2] = tied(give, far3, *got2)
    got = moved(give, swap_x)
    scratch = [tall, (wide, rows), tall]
    part3 = product_call(
        late_kernel, [(2, 2, rows // 8, wide)] * 4, scratch, flops, where, here, partner, flight[3], early, far3, near3
    )
    pieces = [part2[0], *got2, part3[0], *spread(part3)]
    more = rows - BEGINS[FIRST]
    diagonal, near, near_give = last_sums(near_sums_kernel, (rows, rows, more), where, keep, got, pieces)
    far, far_give = last_sums(far_sums_kernel, (rows, more), where, keep, got, pieces)

    near_more = moved(near_give, swap_x)
    far_more = moved(far_give, to_owner_x)
    far = moved(far, to_owner)
    near = near + jnp.pad(near_more, ((0, 0), (rows - more, 0)))
    far_low = jnp.pad(far_more, ((0, 0), (rows - more, 0)))
    turned = [
        far_more[:, BEGINS[j] - BEGINS[FIRST] :][:, :wide].reshape(rows // wide, wide // 8, wide).transpose(1, 0, 2).reshape(wide // 8, rows)
        for j, wide in enumerate(CHUNKS)
        if j >= FIRST
    ]
    far_high = jnp.pad(jnp.concatenate(turned, axis=0), ((96 - more // 8, 0), (0, 0)))
    far = far + jnp.where(core == 0, far_low, far_high)
    summed = jnp.stack([diagonal, near, far], axis=1)
    return decay_rate * old_stats + (1.0 - decay_rate) * COLS ** (-0.5) * summed


def solution(mesh):
    return jax.shard_map(
        shards,
        mesh=mesh,
        in_specs=(P("fsdp", "tensor"), P(("fsdp", "tensor"), None, None)),
        out_specs=P(("fsdp", "tensor"), None, None),
        check_vma=False,
    )
```

time: 157 us -> 152 us (0.968)
  starting transfers between devices: 41.2 us -> 35.7 us
    ppermute x25 -> x24, starting transfers between devices: 41.2 us -> 35.7 us  [moved(): return lax.ppermute(value, AXES, pairs)]
    pallas_call x9 -> x12, Pallas kernels: 35.3 us -> 36.1 us  [the longest x6 25.6 us: product_call(): pl.pallas_call(kernel, out_shape=[jax.ShapeDtypeStruct(shape, jnp.float32...]
    ppermute x25 -> x24, waiting for transfers between devices: 60 us -> 60.6 us  [moved(): return lax.ppermute(value, AXES, pairs)]
  transfers between devices with their start and end apart: 25 -> 24, of which waited for: 12 -> 13; matrix products, arithmetic and copies ran while one was open for 0% -> 0% of each run, Pallas kernels for 33% -> 35%
where the time goes in v2:
time: 152 us
  waiting for transfers between devices  60.6 us (40%)
  Pallas kernels  53.6 us (35%)
  starting transfers between devices  35.7 us (23%)
    ppermute x24, waiting for transfers between devices, moved(): return lax.ppermute(value, AXES, pairs)  60.6 us
    ppermute x24, starting transfers between devices, moved(): return lax.ppermute(value, AXES, pairs)  35.7 us
    pallas_call x6, Pallas kernels, product_call(): pl.pallas_call(kernel, out_shape=[jax.ShapeDtypeStruct(shape, jnp.float32...  25.6 us
    pallas_call x4, Pallas kernels, picked(): pl.pallas_call(functools.partial(pick_kernel, begin, wide // 8, span), ou...  9.29 us
    pallas_call x1, Pallas kernels, squared(): pl.pallas_call(square_kernel, out_shape=[jax.ShapeDtypeStruct(piece, jnp....  8.82 us
    pallas_call x2, Pallas kernels, held(): pl.pallas_call(hold_kernel, out_shape=pltpu.VMEM(value.shape, value.dtype...  7.85 us
  transfers between devices with their start and end apart: 24, of which 13 were waited for; matrix products, arithmetic and copies ran while one was open for 0% of the time, Pallas kernels for 35%

profile of v2, /device:TPU:97, one launch (start us, length us, event | category | flops | bytes accessed | tf_op | source)
XLA Modules:
  0.0 151.5 jit_solution(6352004097154991460)
XLA Ops:
  0.0 0.7 collective-permute-start.1
  0.7 0.1 pad_add_fusion.where_ref
  0.8 2.5 %shard_map.28 = bf16[256,6656]{1,0:T(8,128)(2,1)S(1)} custom-call(s32[4]{0:T(128)S(1)} %pad_add_fusion.where_ref, bf16[768,6656]{1,0:T(8,128)(2,1)} %grad_ref.7), custom_call_target="tpu_custom_call" | custom-call | bytes 6815744 | tf_op jit(solution)/shard_map/pallas_call | solution.py:80
  3.3 1.3 collective-permute-start
  4.6 3.9 %shard_map.29.own_ref = bf16[768,6656]{1,0:T(8,128)(2,1)S(1)} custom-call(bf16[768,6656]{1,0:T(8,128)(2,1)} %grad_ref.7), custom_call_target="tpu_custom_call" | custom-call | bytes 20447232 | tf_op jit(solution)/shard_map/pallas_call | solution.py:98
  8.6 2.5 %shard_map.31 = bf16[256,6656]{1,0:T(8,128)(2,1)S(1)} custom-call(s32[4]{0:T(128)S(1)} %pad_add_fusion.where_ref, bf16[768,6656]{1,0:T(8,128)(2,1)} %grad_ref.7), custom_call_target="tpu_custom_call" | custom-call | bytes 6815744 | tf_op jit(solution)/shard_map/pallas_call | solution.py:80
  11.1 8.8 %shard_map.30 = (f32[2,96,768]{2,1,0:T(8,128)S(1)}, f32[2,96,768]{2,1,0:T(8,128)S(1)}, f32[2,96,768]{2,1,0:T(8,128)S(1)}, f32[2,96,768]{2,1,0:T(8,128)S(1)}) custom-call(s32[4]{0:T(128)S(1)} %pad_add_fusion.where_ref, bf16[768,6656]{1,0:T(8,128)(2,1)S(1)} %shard_map.29.own_ref), custom_call_target="tpu_custom_call" | custom-call | flops 7851737088 | bytes 12582912 | tf_op jit(solution)/shard_map/pallas_call | solution.py:134
  19.9 0.0 collective-permute-done.1.source_ref
  19.9 4.2 %collective-permute-start.9 = (bf16[256,6656]{1,0:T(8,128)(2,1)S(1)}, bf16[256,6656]{1,0:T(8,128)(2,1)S(1)}, u32[]{:S(2)}, u32[]{:S(2)}) collective-permute-start(bf16[256,6656]{1,0:T(8,128)(2,1)S(1)} %shard_map.31), channel_id=1, source_target_pairs={{0,120},{1,121},{2,122},{3,123},{4,124},{5,125},{6,126},{7,127},{8... | collective-permute-start | bytes 10223624 | tf_op jit(solution)/shard_map/ppermute | solution.py:29
  24.1 1.3 collective-permute-start.2
  25.4 1.4 collective-permute-start.3
  26.9 1.6 %collective-permute-start.4 = (f32[2,96,768]{2,1,0:T(8,128)S(1)}, f32[2,96,768]{2,1,0:T(8,128)S(1)}, u32[]{:S(2)}, u32[]{:S(2)}) collective-permute-start(f32[2,96,768]{2,1,0:T(8,128)S(1)} %get-tuple-element.90), channel_id=1, source_target_pairs={{0,4},{1,5},{2,6},{3,7},{4,0},{5,1},{6,2},{7,3},{8,12},{9,13},{10,... | collective-permute-start | bytes 1769480 | tf_op jit(solution)/shard_map/ppermute | solution.py:29
  28.5 2.1 %shard_map.33 = bf16[128,6656]{1,0:T(8,128)(2,1)S(1)} custom-call(s32[4]{0:T(128)S(1)} %pad_add_fusion.where_ref, bf16[768,6656]{1,0:T(8,128)(2,1)} %grad_ref.7), custom_call_target="tpu_custom_call" | custom-call | bytes 3407872 | tf_op jit(solution)/shard_map/pallas_call | solution.py:80
  30.6 2.1 %shard_map.34 = bf16[128,6656]{1,0:T(8,128)(2,1)S(1)} custom-call(s32[4]{0:T(128)S(1)} %pad_add_fusion.where_ref, bf16[768,6656]{1,0:T(8,128)(2,1)} %grad_ref.7), custom_call_target="tpu_custom_call" | custom-call | bytes 3407872 | tf_op jit(solution)/shard_map/pallas_call | solution.py:80
  32.8 3.9 %shard_map.32.pair_ref = bf16[768,6656]{1,0:T(8,128)(2,1)S(1)} custom-call(bf16[768,6656]{1,0:T(8,128)(2,1)} %collective-permute-done.1.source_ref), custom_call_target="tpu_custom_call" | custom-call | bytes 20447232 | tf_op jit(solution)/shard_map/pallas_call | solution.py:98
  36.7 9.8 %collective-permute-done.got_ref = bf16[256,6656]{1,0:T(8,128)(2,1)S(1)} collective-permute-done((bf16[256,6656]{1,0:T(8,128)(2,1)S(1)}, bf16[256,6656]{1,0:T(8,128)(2,1)S(1)}, u32[]{:S(2)}, u32[]{:S(2)}) %collective-permute-start) | collective-permute-done | bytes 3407904 | tf_op jit(solution)/shard_map/ppermute | solution.py:29
  46.5 6.1 %shard_map.35 = (f32[2,2,96,256]{3,2,1,0:T(8,128)S(1)}, f32[2,2,96,256]{3,2,1,0:T(8,128)S(1)}, f32[2,2,96,256]{3,2,1,0:T(8,128)S(1)}, f32[2,2,96,256]{3,2,1,0:T(8,128)S(1)}) custom-call(s32[4]{0:T(128)S(1)} %pad_add_fusion.where_ref, bf16[768,6656]{1,0:T(8,128)(2,1)S(1)} %shard_map.29.own_ref, bf16[768,6656]{1,0:T(8,128)(2,1)S(1)} %shard_map.32.pair_ref, ...), custom_call_target="tpu_custom_call" | custom-call | flops 5234491392 | bytes 27262976 | tf_op jit(solution)/shard_map/pallas_call | solution.py:224
  52.6 0.0 collective-permute-done.2.refs_1_
  52.6 0.0 collective-permute-done.3.refs_2_
  52.6 1.4 collective-permute-start.5
  54.0 1.7 %collective-permute-start.6 = (f32[2,2,96,256]{3,2,1,0:T(8,128)S(1)}, f32[2,2,96,256]{3,2,1,0:T(8,128)S(1)}, u32[]{:S(2)}, u32[]{:S(2)}) collective-permute-start(f32[2,2,96,256]{3,2,1,0:T(8,128)S(1)} %get-tuple-element.92), channel_id=1, source_target_pairs={{0,6},{1,7},{2,0},{3,1},{4,2},{5,3},{6,4},{7,5},{8,14},{9,15},{10,... | collective-permute-start | bytes 1179656 | tf_op jit(solution)/shard_map/ppermute | solution.py:29
  55.7 1.4 collective-permute-start.7
  57.1 2.1 %collective-permute-start.10 = (bf16[128,6656]{1,0:T(8,128)(2,1)S(1)}, bf16[128,6656]{1,0:T(8,128)(2,1)S(1)}, u32[]{:S(2)}, u32[]{:S(2)}) collective-permute-start(bf16[128,6656]{1,0:T(8,128)(2,1)S(1)} %shard_map.33), channel_id=1, source_target_pairs={{0,120},{1,121},{2,122},{3,123},{4,124},{5,125},{6,126},{7,127},{8... | collective-permute-start | bytes 5111816 | tf_op jit(solution)/shard_map/ppermute | solution.py:29
  59.2 4.7 %collective-permute-done.5.refs_5_ = f32[2,2,96,256]{3,2,1,0:T(8,128)S(1)} collective-permute-done((f32[2,2,96,256]{3,2,1,0:T(8,128)S(1)}, f32[2,2,96,256]{3,2,1,0:T(8,128)S(1)}, u32[]{:S(2)}, u32[]{:S(2)}) %collective-permute-start.5) | collective-permute-done | bytes 393248 | tf_op jit(solution)/shard_map/ppermute | solution.py:29
  63.9 1.3 collective-permute-done.6.refs_6_
  65.2 6.1 %collective-permute-done.7.refs_7_ = f32[2,2,96,256]{3,2,1,0:T(8,128)S(1)} collective-permute-done((f32[2,2,96,256]{3,2,1,0:T(8,128)S(1)}, f32[2,2,96,256]{3,2,1,0:T(8,128)S(1)}, u32[]{:S(2)}, u32[]{:S(2)}) %collective-permute-start.7) | collective-permute-done | bytes 393248 | tf_op jit(solution)/shard_map/ppermute | solution.py:29
  71.3 1.8 %collective-permute-start.8 = (bf16[128,6656]{1,0:T(8,128)(2,1)S(1)}, bf16[128,6656]{1,0:T(8,128)(2,1)S(1)}, u32[]{:S(2)}, u32[]{:S(2)}) collective-permute-start(bf16[128,6656]{1,0:T(8,128)(2,1)S(1)} %shard_map.34), channel_id=1, source_target_pairs={{0,120},{1,121},{2,122},{3,123},{4,124},{5,125},{6,126},{7,127},{8... | collective-permute-start | bytes 5111816 | tf_op jit(solution)/shard_map/ppermute | solution.py:29
  73.1 9.9 %collective-permute-done.9.got_ref = bf16[256,6656]{1,0:T(8,128)(2,1)S(1)} collective-permute-done((bf16[256,6656]{1,0:T(8,128)(2,1)S(1)}, bf16[256,6656]{1,0:T(8,128)(2,1)S(1)}, u32[]{:S(2)}, u32[]{:S(2)}) %collective-permute-start.9) | collective-permute-done | bytes 3407904 | tf_op jit(solution)/shard_map/ppermute | solution.py:29
  83.0 6.1 %shard_map.37 = (f32[2,2,96,256]{3,2,1,0:T(8,128)S(1)}, f32[2,2,96,256]{3,2,1,0:T(8,128)S(1)}, f32[2,2,96,256]{3,2,1,0:T(8,128)S(1)}, f32[2,2,96,256]{3,2,1,0:T(8,128)S(1)}) custom-call(s32[4]{0:T(128)S(1)} %pad_add_fusion.where_ref, bf16[768,6656]{1,0:T(8,128)(2,1)S(1)} %shard_map.29.own_ref, bf16[768,6656]{1,0:T(8,128)(2,1)S(1)} %shard_map.32.pair_ref, ...), custom_call_target="tpu_custom_call" | custom-call | flops 5234491392 | bytes 27262976 | tf_op jit(solution)/shard_map/pallas_call | solution.py:224
  89.1 1.4 collective-permute-start.11
  90.5 1.5 %collective-permute-start.12 = (f32[2,2,96,256]{3,2,1,0:T(8,128)S(1)}, f32[2,2,96,256]{3,2,1,0:T(8,128)S(1)}, u32[]{:S(2)}, u32[]{:S(2)}) collective-permute-start(f32[2,2,96,256]{3,2,1,0:T(8,128)S(1)} %get-tuple-element.115), channel_id=1, source_target_pairs={{0,6},{1,7},{2,0},{3,1},{4,2},{5,3},{6,4},{7,5},{8,14},{9,15},{10,... | collective-permute-start | bytes 1179656 | tf_op jit(solution)/shard_map/ppermute | solution.py:29
  92.0 1.6 %collective-permute-start.13 = (f32[2,2,96,256]{3,2,1,0:T(8,128)S(1)}, f32[2,2,96,256]{3,2,1,0:T(8,128)S(1)}, u32[]{:S(2)}, u32[]{:S(2)}) collective-permute-start(f32[2,2,96,256]{3,2,1,0:T(8,128)S(1)} %get-tuple-element.116), channel_id=1, source_target_pairs={{0,4},{1,5},{2,6},{3,7},{4,0},{5,1},{6,2},{7,3},{8,12},{9,13},{10,... | collective-permute-start | bytes 1179656 | tf_op jit(solution)/shard_map/ppermute | solution.py:29
  93.6 7.7 %collective-permute-done.10.got_ref = bf16[128,6656]{1,0:T(8,128)(2,1)S(1)} collective-permute-done((bf16[128,6656]{1,0:T(8,128)(2,1)S(1)}, bf16[128,6656]{1,0:T(8,128)(2,1)S(1)}, u32[]{:S(2)}, u32[]{:S(2)}) %collective-permute-start.10) | collective-permute-done | bytes 1703968 | tf_op jit(solution)/shard_map/ppermute | solution.py:29
  101.3 6.2 %shard_map.38 = (f32[2,2,96,128]{3,2,1,0:T(8,128)S(1)}, f32[2,2,96,128]{3,2,1,0:T(8,128)S(1)}, f32[2,2,96,128]{3,2,1,0:T(8,128)S(1)}, f32[2,2,96,128]{3,2,1,0:T(8,128)S(1)}) custom-call(s32[4]{0:T(128)S(1)} %pad_add_fusion.where_ref, bf16[768,6656]{1,0:T(8,128)(2,1)S(1)} %shard_map.29.own_ref, bf16[768,6656]{1,0:T(8,128)(2,1)S(1)} %shard_map.32.pair_ref, ...), custom_call_target="tpu_custom_call" | custom-call | flops 2617245696 | bytes 13631488 | tf_op jit(solution)/shard_map/pallas_call | solution.py:224
  107.5 0.0 collective-permute-done.11.refs_9_
  107.5 0.2 collective-permute-done.13.refs_11_
  107.8 1.1 collective-permute-start.14
  108.9 1.5 %collective-permute-start.15 = (f32[2,2,96,128]{3,2,1,0:T(8,128)S(1)}, f32[2,2,96,128]{3,2,1,0:T(8,128)S(1)}, u32[]{:S(2)}, u32[]{:S(2)}) collective-permute-start(f32[2,2,96,128]{3,2,1,0:T(8,128)S(1)} %get-tuple-element.126), channel_id=1, source_target_pairs={{0,6},{1,7},{2,0},{3,1},{4,2},{5,3},{6,4},{7,5},{8,14},{9,15},{10,... | collective-permute-start | bytes 589832 | tf_op jit(solution)/shard_map/ppermute | solution.py:29
  110.4 1.5 %collective-permute-start.16 = (f32[2,2,96,128]{3,2,1,0:T(8,128)S(1)}, f32[2,2,96,128]{3,2,1,0:T(8,128)S(1)}, u32[]{:S(2)}, u32[]{:S(2)}) collective-permute-start(f32[2,2,96,128]{3,2,1,0:T(8,128)S(1)} %get-tuple-element.127), channel_id=1, source_target_pairs={{0,4},{1,5},{2,6},{3,7},{4,0},{5,1},{6,2},{7,3},{8,12},{9,13},{10,... | collective-permute-start | bytes 589832 | tf_op jit(solution)/shard_map/ppermute | solution.py:29
  112.0 0.5 shard_map.36.early_ref
  112.5 0.8 shard_map.39
  113.4 6.1 %collective-permute-done.8.got_ref = bf16[128,6656]{1,0:T(8,128)(2,1)S(1)} collective-permute-done((bf16[128,6656]{1,0:T(8,128)(2,1)S(1)}, bf16[128,6656]{1,0:T(8,128)(2,1)S(1)}, u32[]{:S(2)}, u32[]{:S(2)}) %collective-permute-start.8) | collective-permute-done | bytes 1703968 | tf_op jit(solution)/shard_map/ppermute | solution.py:29
  119.5 0.5 shard_map.40
  120.1 0.0 collective-permute-done.14.refs_1_
  120.1 0.0 collective-permute-done.15.refs_2_
  120.1 1.3 collective-permute-start.17
  121.4 6.0 %shard_map.41 = (f32[2,2,96,128]{3,2,1,0:T(8,128)S(1)}, f32[2,2,96,128]{3,2,1,0:T(8,128)S(1)}, f32[2,2,96,128]{3,2,1,0:T(8,128)S(1)}, f32[2,2,96,128]{3,2,1,0:T(8,128)S(1)}) custom-call(s32[4]{0:T(128)S(1)} %pad_add_fusion.where_ref, bf16[768,6656]{1,0:T(8,128)(2,1)S(1)} %shard_map.29.own_ref, bf16[768,6656]{1,0:T(8,128)(2,1)S(1)} %shard_map.32.pair_ref, ...), custom_call_target="tpu_custom_call" | custom-call | flops 1308622848 | bytes 6815744 | tf_op jit(solution)/shard_map/pallas_call | solution.py:224
  127.4 1.4 collective-permute-start.18
  128.8 1.5 %collective-permute-start.19 = (f32[2,2,96,128]{3,2,1,0:T(8,128)S(1)}, f32[2,2,96,128]{3,2,1,0:T(8,128)S(1)}, u32[]{:S(2)}, u32[]{:S(2)}) collective-permute-start(f32[2,2,96,128]{3,2,1,0:T(8,128)S(1)} %get-tuple-element.138), channel_id=1, source_target_pairs={{0,6},{1,7},{2,0},{3,1},{4,2},{5,3},{6,4},{7,5},{8,14},{9,15},{10,... | collective-permute-start | bytes 589832 | tf_op jit(solution)/shard_map/ppermute | solution.py:29
  130.3 1.6 %collective-permute-start.20 = (f32[2,2,96,128]{3,2,1,0:T(8,128)S(1)}, f32[2,2,96,128]{3,2,1,0:T(8,128)S(1)}, u32[]{:S(2)}, u32[]{:S(2)}) collective-permute-start(f32[2,2,96,128]{3,2,1,0:T(8,128)S(1)} %get-tuple-element.139), channel_id=1, source_target_pairs={{0,4},{1,5},{2,6},{3,7},{4,0},{5,1},{6,2},{7,3},{8,12},{9,13},{10,... | collective-permute-start | bytes 589832 | tf_op jit(solution)/shard_map/ppermute | solution.py:29
  131.9 3.1 %collective-permute-done.18.refs_5_ = f32[2,2,96,128]{3,2,1,0:T(8,128)S(1)} collective-permute-done((f32[2,2,96,128]{3,2,1,0:T(8,128)S(1)}, f32[2,2,96,128]{3,2,1,0:T(8,128)S(1)}, u32[]{:S(2)}, u32[]{:S(2)}) %collective-permute-start.18) | collective-permute-done | bytes 196640 | tf_op jit(solution)/shard_map/ppermute | solution.py:29
  135.0 0.5 collective-permute-done.19.refs_6_
  135.5 1.6 %collective-permute-done.20.refs_7_ = f32[2,2,96,128]{3,2,1,0:T(8,128)S(1)} collective-permute-done((f32[2,2,96,128]{3,2,1,0:T(8,128)S(1)}, f32[2,2,96,128]{3,2,1,0:T(8,128)S(1)}, u32[]{:S(2)}, u32[]{:S(2)}) %collective-permute-start.20) | collective-permute-done | bytes 196640 | tf_op jit(solution)/shard_map/ppermute | solution.py:29
  137.1 0.0 collective-permute-done.17.got_ref
  137.1 0.6 shard_map.43
  137.7 0.1 collective-permute-start.23
  137.8 0.0 copy-start
  137.8 0.6 shard_map.42
  138.4 0.3 collective-permute-start.21
  138.8 2.0 %collective-permute-start.22 = (f32[96,768]{1,0:T(8,128)S(1)}, f32[96,768]{1,0:T(8,128)S(1)}, u32[]{:S(2)}, u32[]{:S(2)}) collective-permute-start(f32[96,768]{1,0:T(8,128)S(1)} %get-tuple-element.143), channel_id=1, source_target_pairs={{0,120},{1,121},{2,122},{3,123},{4,124},{5,125},{6,126},{7,127},{8... | collective-permute-start | bytes 884744 | tf_op jit(solution)/shard_map/ppermute | solution.py:29
  140.8 4.3 %collective-permute-done.23 = f32[96,256]{1,0:T(8,128)S(1)} collective-permute-done((f32[96,256]{1,0:T(8,128)S(1)}, f32[96,256]{1,0:T(8,128)S(1)}, u32[]{:S(2)}, u32[]{:S(2)}) %collective-permute-start.23) | collective-permute-done | bytes 98336 | tf_op jit(solution)/shard_map/ppermute | solution.py:29
  145.2 0.0 collective-permute-done.21
  145.2 5.2 %collective-permute-done.22 = f32[96,768]{1,0:T(8,128)S(1)} collective-permute-done((f32[96,768]{1,0:T(8,128)S(1)}, f32[96,768]{1,0:T(8,128)S(1)}, u32[]{:S(2)}, u32[]{:S(2)}) %collective-permute-start.22) | collective-permute-done | bytes 294944 | tf_op jit(solution)/shard_map/ppermute | solution.py:29
  150.5 1.0 fusion
  (10 shorter events, 0.1 us)
Async XLA Ops:
  0.0 19.9 %collective-permute-start.1 = (bf16[768,6656]{1,0:T(8,128)(2,1)}, bf16[768,6656]{1,0:T(8,128)(2,1)}, u32[]{:S(2)}, u32[]{:S(2)}) collective-permute-start(bf16[768,6656]{1,0:T(8,128)(2,1)} %grad_ref.7), channel_id=1, source_target_pairs={{0,8},{1,9},{2,10},{3,11},{4,12},{5,13},{6,14},{7,15},{8,0},{9,1},... | collective-permute-start | bytes 30670856 | tf_op jit(solution)/shard_map/ppermute | solution.py:29
  3.3 43.2 %collective-permute-start = (bf16[256,6656]{1,0:T(8,128)(2,1)S(1)}, bf16[256,6656]{1,0:T(8,128)(2,1)S(1)}, u32[]{:S(2)}, u32[]{:S(2)}) collective-permute-start(bf16[256,6656]{1,0:T(8,128)(2,1)S(1)} %shard_map.28), channel_id=1, source_target_pairs={{0,120},{1,121},{2,122},{3,123},{4,124},{5,125},{6,126},{7,127},{8... | collective-permute-start | bytes 10223624 | tf_op jit(solution)/shard_map/ppermute | solution.py:29
  19.9 63.1 %collective-permute-start.9 = (bf16[256,6656]{1,0:T(8,128)(2,1)S(1)}, bf16[256,6656]{1,0:T(8,128)(2,1)S(1)}, u32[]{:S(2)}, u32[]{:S(2)}) collective-permute-start(bf16[256,6656]{1,0:T(8,128)(2,1)S(1)} %shard_map.31), channel_id=1, source_target_pairs={{0,120},{1,121},{2,122},{3,123},{4,124},{5,125},{6,126},{7,127},{8... | collective-permute-start | bytes 10223624 | tf_op jit(solution)/shard_map/ppermute | solution.py:29
  24.1 28.5 %collective-permute-start.2 = (f32[2,96,768]{2,1,0:T(8,128)S(1)}, f32[2,96,768]{2,1,0:T(8,128)S(1)}, u32[]{:S(2)}, u32[]{:S(2)}) collective-permute-start(f32[2,96,768]{2,1,0:T(8,128)S(1)} %get-tuple-element.88), channel_id=1, source_target_pairs={{0,2},{1,3},{2,4},{3,5},{4,6},{5,7},{6,0},{7,1},{8,10},{9,11},{10,... | collective-permute-start | bytes 1769480 | tf_op jit(solution)/shard_map/ppermute | solution.py:29
  25.4 27.2 %collective-permute-start.3 = (f32[2,96,768]{2,1,0:T(8,128)S(1)}, f32[2,96,768]{2,1,0:T(8,128)S(1)}, u32[]{:S(2)}, u32[]{:S(2)}) collective-permute-start(f32[2,96,768]{2,1,0:T(8,128)S(1)} %get-tuple-element.89), channel_id=1, source_target_pairs={{0,6},{1,7},{2,0},{3,1},{4,2},{5,3},{6,4},{7,5},{8,14},{9,15},{10,... | collective-permute-start | bytes 1769480 | tf_op jit(solution)/shard_map/ppermute | solution.py:29
  26.9 25.8 %collective-permute-start.4 = (f32[2,96,768]{2,1,0:T(8,128)S(1)}, f32[2,96,768]{2,1,0:T(8,128)S(1)}, u32[]{:S(2)}, u32[]{:S(2)}) collective-permute-start(f32[2,96,768]{2,1,0:T(8,128)S(1)} %get-tuple-element.90), channel_id=1, source_target_pairs={{0,4},{1,5},{2,6},{3,7},{4,0},{5,1},{6,2},{7,3},{8,12},{9,13},{10,... | collective-permute-start | bytes 1769480 | tf_op jit(solution)/shard_map/ppermute | solution.py:29
  52.6 11.2 %collective-permute-start.5 = (f32[2,2,96,256]{3,2,1,0:T(8,128)S(1)}, f32[2,2,96,256]{3,2,1,0:T(8,128)S(1)}, u32[]{:S(2)}, u32[]{:S(2)}) collective-permute-start(f32[2,2,96,256]{3,2,1,0:T(8,128)S(1)} %get-tuple-element.91), channel_id=1, source_target_pairs={{0,2},{1,3},{2,4},{3,5},{4,6},{5,7},{6,0},{7,1},{8,10},{9,11},{10,... | collective-permute-start | bytes 1179656 | tf_op jit(solution)/shard_map/ppermute | solution.py:29
  54.0 11.2 %collective-permute-start.6 = (f32[2,2,96,256]{3,2,1,0:T(8,128)S(1)}, f32[2,2,96,256]{3,2,1,0:T(8,128)S(1)}, u32[]{:S(2)}, u32[]{:S(2)}) collective-permute-start(f32[2,2,96,256]{3,2,1,0:T(8,128)S(1)} %get-tuple-element.92), channel_id=1, source_target_pairs={{0,6},{1,7},{2,0},{3,1},{4,2},{5,3},{6,4},{7,5},{8,14},{9,15},{10,... | collective-permute-start | bytes 1179656 | tf_op jit(solution)/shard_map/ppermute | solution.py:29
  55.7 15.6 %collective-permute-start.7 = (f32[2,2,96,256]{3,2,1,0:T(8,128)S(1)}, f32[2,2,96,256]{3,2,1,0:T(8,128)S(1)}, u32[]{:S(2)}, u32[]{:S(2)}) collective-permute-start(f32[2,2,96,256]{3,2,1,0:T(8,128)S(1)} %get-tuple-element.93), channel_id=1, source_target_pairs={{0,4},{1,5},{2,6},{3,7},{4,0},{5,1},{6,2},{7,3},{8,12},{9,13},{10,... | collective-permute-start | bytes 1179656 | tf_op jit(solution)/shard_map/ppermute | solution.py:29
  57.1 44.2 %collective-permute-start.10 = (bf16[128,6656]{1,0:T(8,128)(2,1)S(1)}, bf16[128,6656]{1,0:T(8,128)(2,1)S(1)}, u32[]{:S(2)}, u32[]{:S(2)}) collective-permute-start(bf16[128,6656]{1,0:T(8,128)(2,1)S(1)} %shard_map.33), channel_id=1, source_target_pairs={{0,120},{1,121},{2,122},{3,123},{4,124},{5,125},{6,126},{7,127},{8... | collective-permute-start | bytes 5111816 | tf_op jit(solution)/shard_map/ppermute | solution.py:29
  71.3 48.2 %collective-permute-start.8 = (bf16[128,6656]{1,0:T(8,128)(2,1)S(1)}, bf16[128,6656]{1,0:T(8,128)(2,1)S(1)}, u32[]{:S(2)}, u32[]{:S(2)}) collective-permute-start(bf16[128,6656]{1,0:T(8,128)(2,1)S(1)} %shard_map.34), channel_id=1, source_target_pairs={{0,120},{1,121},{2,122},{3,123},{4,124},{5,125},{6,126},{7,127},{8... | collective-permute-start | bytes 5111816 | tf_op jit(solution)/shard_map/ppermute | solution.py:29
  89.1 18.4 %collective-permute-start.11 = (f32[2,2,96,256]{3,2,1,0:T(8,128)S(1)}, f32[2,2,96,256]{3,2,1,0:T(8,128)S(1)}, u32[]{:S(2)}, u32[]{:S(2)}) collective-permute-start(f32[2,2,96,256]{3,2,1,0:T(8,128)S(1)} %get-tuple-element.114), channel_id=1, source_target_pairs={{0,2},{1,3},{2,4},{3,5},{4,6},{5,7},{6,0},{7,1},{8,10},{9,11},{10,... | collective-permute-start | bytes 1179656 | tf_op jit(solution)/shard_map/ppermute | solution.py:29
  90.5 17.0 %collective-permute-start.12 = (f32[2,2,96,256]{3,2,1,0:T(8,128)S(1)}, f32[2,2,96,256]{3,2,1,0:T(8,128)S(1)}, u32[]{:S(2)}, u32[]{:S(2)}) collective-permute-start(f32[2,2,96,256]{3,2,1,0:T(8,128)S(1)} %get-tuple-element.115), channel_id=1, source_target_pairs={{0,6},{1,7},{2,0},{3,1},{4,2},{5,3},{6,4},{7,5},{8,14},{9,15},{10,... | collective-permute-start | bytes 1179656 | tf_op jit(solution)/shard_map/ppermute | solution.py:29
  92.0 15.8 %collective-permute-start.13 = (f32[2,2,96,256]{3,2,1,0:T(8,128)S(1)}, f32[2,2,96,256]{3,2,1,0:T(8,128)S(1)}, u32[]{:S(2)}, u32[]{:S(2)}) collective-permute-start(f32[2,2,96,256]{3,2,1,0:T(8,128)S(1)} %get-tuple-element.116), channel_id=1, source_target_pairs={{0,4},{1,5},{2,6},{3,7},{4,0},{5,1},{6,2},{7,3},{8,12},{9,13},{10,... | collective-permute-start | bytes 1179656 | tf_op jit(solution)/shard_map/ppermute | solution.py:29
  107.8 12.3 %collective-permute-start.14 = (f32[2,2,96,128]{3,2,1,0:T(8,128)S(1)}, f32[2,2,96,128]{3,2,1,0:T(8,128)S(1)}, u32[]{:S(2)}, u32[]{:S(2)}) collective-permute-start(f32[2,2,96,128]{3,2,1,0:T(8,128)S(1)} %get-tuple-element.125), channel_id=1, source_target_pairs={{0,2},{1,3},{2,4},{3,5},{4,6},{5,7},{6,0},{7,1},{8,10},{9,11},{10,... | collective-permute-start | bytes 589832 | tf_op jit(solution)/shard_map/ppermute | solution.py:29
  108.9 11.2 %collective-permute-start.15 = (f32[2,2,96,128]{3,2,1,0:T(8,128)S(1)}, f32[2,2,96,128]{3,2,1,0:T(8,128)S(1)}, u32[]{:S(2)}, u32[]{:S(2)}) collective-permute-start(f32[2,2,96,128]{3,2,1,0:T(8,128)S(1)} %get-tuple-element.126), channel_id=1, source_target_pairs={{0,6},{1,7},{2,0},{3,1},{4,2},{5,3},{6,4},{7,5},{8,14},{9,15},{10,... | collective-permute-start | bytes 589832 | tf_op jit(solution)/shard_map/ppermute | solution.py:29
  110.4 9.7 %collective-permute-start.16 = (f32[2,2,96,128]{3,2,1,0:T(8,128)S(1)}, f32[2,2,96,128]{3,2,1,0:T(8,128)S(1)}, u32[]{:S(2)}, u32[]{:S(2)}) collective-permute-start(f32[2,2,96,128]{3,2,1,0:T(8,128)S(1)} %get-tuple-element.127), channel_id=1, source_target_pairs={{0,4},{1,5},{2,6},{3,7},{4,0},{5,1},{6,2},{7,3},{8,12},{9,13},{10,... | collective-permute-start | bytes 589832 | tf_op jit(solution)/shard_map/ppermute | solution.py:29
  120.1 17.0 %collective-permute-start.17 = (f32[96,1792]{1,0:T(8,128)S(1)}, f32[96,1792]{1,0:T(8,128)S(1)}, u32[]{:S(2)}, u32[]{:S(2)}) collective-permute-start(f32[96,1792]{1,0:T(8,128)S(1)} %get-tuple-element.128), channel_id=1, source_target_pairs={{0,1},{1,0},{2,3},{3,2},{4,5},{5,4},{6,7},{7,6},{8,9},{9,8},{10,11... | collective-permute-start | bytes 2064392 | tf_op jit(solution)/shard_map/ppermute | solution.py:29
  127.4 7.5 %collective-permute-start.18 = (f32[2,2,96,128]{3,2,1,0:T(8,128)S(1)}, f32[2,2,96,128]{3,2,1,0:T(8,128)S(1)}, u32[]{:S(2)}, u32[]{:S(2)}) collective-permute-start(f32[2,2,96,128]{3,2,1,0:T(8,128)S(1)} %get-tuple-element.137), channel_id=1, source_target_pairs={{0,2},{1,3},{2,4},{3,5},{4,6},{5,7},{6,0},{7,1},{8,10},{9,11},{10,... | collective-permute-start | bytes 589832 | tf_op jit(solution)/shard_map/ppermute | solution.py:29
  128.8 6.7 %collective-permute-start.19 = (f32[2,2,96,128]{3,2,1,0:T(8,128)S(1)}, f32[2,2,96,128]{3,2,1,0:T(8,128)S(1)}, u32[]{:S(2)}, u32[]{:S(2)}) collective-permute-start(f32[2,2,96,128]{3,2,1,0:T(8,128)S(1)} %get-tuple-element.138), channel_id=1, source_target_pairs={{0,6},{1,7},{2,0},{3,1},{4,2},{5,3},{6,4},{7,5},{8,14},{9,15},{10,... | collective-permute-start | bytes 589832 | tf_op jit(solution)/shard_map/ppermute | solution.py:29
  130.3 6.8 %collective-permute-start.20 = (f32[2,2,96,128]{3,2,1,0:T(8,128)S(1)}, f32[2,2,96,128]{3,2,1,0:T(8,128)S(1)}, u32[]{:S(2)}, u32[]{:S(2)}) collective-permute-start(f32[2,2,96,128]{3,2,1,0:T(8,128)S(1)} %get-tuple-element.139), channel_id=1, source_target_pairs={{0,4},{1,5},{2,6},{3,7},{4,0},{5,1},{6,2},{7,3},{8,12},{9,13},{10,... | collective-permute-start | bytes 589832 | tf_op jit(solution)/shard_map/ppermute | solution.py:29
  137.7 7.4 %collective-permute-start.23 = (f32[96,256]{1,0:T(8,128)S(1)}, f32[96,256]{1,0:T(8,128)S(1)}, u32[]{:S(2)}, u32[]{:S(2)}) collective-permute-start(f32[96,256]{1,0:T(8,128)S(1)} %get-tuple-element.144), channel_id=1, source_target_pairs={{0,121},{1,120},{2,123},{3,122},{4,125},{5,124},{6,127},{7,126},{8... | collective-permute-start | bytes 294920 | tf_op jit(solution)/shard_map/ppermute | solution.py:29
  137.8 12.7 %copy-start = (f32[96,3,768]{2,0,1:T(8,128)S(1)}, f32[96,3,768]{2,0,1:T(8,128)}, u32[]{:S(2)}) copy-start(f32[96,3,768]{2,0,1:T(8,128)} %param.3) | copy-start | bytes 2654212
  138.4 6.8 %collective-permute-start.21 = (f32[96,256]{1,0:T(8,128)S(1)}, f32[96,256]{1,0:T(8,128)S(1)}, u32[]{:S(2)}, u32[]{:S(2)}) collective-permute-start(f32[96,256]{1,0:T(8,128)S(1)} %get-tuple-element.142), channel_id=1, source_target_pairs={{0,1},{1,0},{2,3},{3,2},{4,5},{5,4},{6,7},{7,6},{8,9},{9,8},{10,11... | collective-permute-start | bytes 294920 | tf_op jit(solution)/shard_map/ppermute | solution.py:29
  138.8 11.7 %collective-permute-start.22 = (f32[96,768]{1,0:T(8,128)S(1)}, f32[96,768]{1,0:T(8,128)S(1)}, u32[]{:S(2)}, u32[]{:S(2)}) collective-permute-start(f32[96,768]{1,0:T(8,128)S(1)} %get-tuple-element.143), channel_id=1, source_target_pairs={{0,120},{1,121},{2,122},{3,123},{4,124},{5,125},{6,126},{7,127},{8... | collective-permute-start | bytes 884744 | tf_op jit(solution)/shard_map/ppermute | solution.py:29

commit v3 on v2

--- a/solution.py
+++ b/solution.py
@@ -12,7 +12,6 @@
 CHUNKS = (256, 256, 128, 128)
 BEGINS = (0, 256, 512, 640)
 VMEM_LIMIT = 5 << 20
-SPLIT = 4608
 FIRST = 2
 AXES = ("fsdp", "tensor")
 
@@ -62,8 +61,8 @@
     return lax.dot_general(left, right, (((1,), (1,)), ((), ())), preferred_element_type=jnp.float32)
 
 
-def pick_kernel(begin, thin, span, where_ref, grad_ref, out_ref, sems):
-    core = where_ref[0]
+def pick_kernel(begin, thin, span, grad_ref, out_ref, sems):
+    core, y, _, _ = position()
     copies = []
     for i in range(8):
         offset = pl.multiple_of(jnp.where(core == 0, begin + thin * i, 96 * i + begin // 8), 16)
@@ -75,17 +74,17 @@
         copy.wait()
 
 
-def picked(where, grad, begin, wide, span):
+def picked(grad, begin, wide, span):
     depth = span[1] - span[0]
     return pl.pallas_call(
         functools.partial(pick_kernel, begin, wide // 8, span),
         out_shape=jax.ShapeDtypeStruct((wide, depth), grad.dtype),
-        in_specs=[pl.BlockSpec(memory_space=pltpu.SMEM), pl.BlockSpec(memory_space=pl.ANY)],
+        in_specs=[pl.BlockSpec(memory_space=pl.ANY)],
         out_specs=pl.BlockSpec(memory_space=pltpu.VMEM),
         scratch_shapes=[pltpu.SemaphoreType.DMA((8,))],
         cost_estimate=pl.CostEstimate(flops=0, bytes_accessed=4 * wide * depth, transcendentals=0),
         compiler_params=pltpu.CompilerParams(vmem_limit_bytes=VMEM_LIMIT),
-    )(where, pltpu.with_memory_space_constraint(grad, pltpu.HBM))
+    )(pltpu.with_memory_space_constraint(grad, pltpu.HBM))
 
 
 def hold_kernel(source_ref, out_ref, sem):
@@ -111,7 +110,12 @@
 
 
 def vmem_specs(count):
-    return [pl.BlockSpec(memory_space=pltpu.SMEM)] + [pl.BlockSpec(memory_space=pltpu.VMEM)] * count
+    return [pl.BlockSpec(memory_space=pltpu.VMEM)] * count
+
+
+def position():
+    block, shard = lax.axis_index("fsdp"), lax.axis_index("tensor")
+    return block & 1, shard >> 1, shard & 1, (block & 7) == 1
 
 
 def owner_rows(y, hop, side, count):
@@ -119,16 +123,16 @@
     return pl.ds(pl.multiple_of(count * shard, count), count)
 
 
-def square_kernel(where_ref, own_ref, *refs):
+def square_kernel(own_ref, *refs):
     outs, total = refs[:4], refs[4]
-    y = where_ref[1]
+    _, y, _, _ = position()
     total[...] = contract(own_ref[...], own_ref[...])
     for hop in range(4):
         for side in range(2):
             outs[hop][side] = total[owner_rows(y, hop, side, 96), :]
 
 
-def squared(where, grad):
+def squared(grad):
     rows, depth = grad.shape
     piece = (2, rows // 8, rows)
     return pl.pallas_call(
@@ -141,7 +145,7 @@
             flops=2 * rows * rows * depth, bytes_accessed=2 * depth * rows + 4 * rows * rows, transcendentals=0
         ),
         compiler_params=pltpu.CompilerParams(vmem_limit_bytes=VMEM_LIMIT),
-    )(where, resident(grad))
+    )(resident(grad))
 
 
 def cut_up(core, y, tall, flat, mixed, outs):
@@ -167,9 +171,9 @@
             outs[hop][side, 1] = mixed[owner_rows(y, hop, side, 96), :]
 
 
-def cross_kernel(begin, where_ref, own_ref, pair_ref, got_ref, *refs):
+def cross_kernel(begin, own_ref, pair_ref, got_ref, *refs):
     outs, (tall, flat, mixed) = refs[:4], refs[4:]
-    core = where_ref[0]
+    core, y, _, _ = position()
     wide = got_ref.shape[0]
 
     @pl.when(core == 0)
@@ -182,45 +186,45 @@
         tall[...] = contract(pair_ref[...], got_ref[...])
         mixed[...] = contract(own_ref[...], got_ref[...])
 
-    cut_up(core, where_ref[1], tall, flat, mixed, outs)
-
-
-def early_kernel(begin, wide, where_ref, own_ref, pair_ref, mixed_ref):
-    @pl.when(where_ref[0] == 0)
+    cut_up(core, y, tall, flat, mixed, outs)
+
+
+def early_kernel(begin, wide, own_ref, pair_ref, mixed_ref):
+    @pl.when(position()[0] == 0)
     def _():
         mixed_ref[...] = contract(own_ref[...], pair_ref[begin : begin + wide, :])
 
 
-def middle_kernel(where_ref, own_ref, pair_ref, got_ref, tall_ref, mixed_ref):
-    @pl.when(where_ref[3] != 0)
+def middle_kernel(own_ref, pair_ref, got_ref, tall_ref, mixed_ref):
+    @pl.when(position()[3])
     def _():
         tall_ref[...] = contract(pair_ref[...], got_ref[...])
         mixed_ref[...] = contract(own_ref[...], got_ref[...])
 
 
-def late_kernel(where_ref, own_ref, pair_ref, got_ref, early_ref, tall_ref, middle_ref, *refs):
+def late_kernel(own_ref, pair_ref, got_ref, early_ref, tall_ref, middle_ref, *refs):
     outs, (tall, flat, mixed) = refs[:4], refs[4:]
-    core, ahead = where_ref[0], where_ref[3]
+    core, y, _, ahead = position()
 
     @pl.when(core == 0)
     def _():
         flat[...] = contract(got_ref[...], pair_ref[...])
         mixed[...] = early_ref[...]
 
-    @pl.when((core != 0) & (ahead == 0))
+    @pl.when((core != 0) & ~ahead)
     def _():
         tall[...] = contract(pair_ref[...], got_ref[...])
         mixed[...] = contract(own_ref[...], got_ref[...])
 
-    @pl.when(ahead != 0)
+    @pl.when(ahead)
     def _():
         tall[...] = tall_ref[...]
         mixed[...] = middle_ref[...]
 
-    cut_up(core, where_ref[1], tall, flat, mixed, outs)
-
-
-def product_call(kernel, shapes, scratch, flops, where, *arrays):
+    cut_up(core, y, tall, flat, mixed, outs)
+
+
+def product_call(kernel, shapes, scratch, flops, *arrays):
     return pl.pallas_call(
         kernel,
         out_shape=[jax.ShapeDtypeStruct(shape, jnp.float32) for shape in shapes],
@@ -229,16 +233,16 @@
         scratch_shapes=[pltpu.VMEM(shape, jnp.float32) for shape in scratch],
         cost_estimate=pl.CostEstimate(flops=flops, bytes_accessed=4 * flops // 768, transcendentals=0),
         compiler_params=pltpu.CompilerParams(vmem_limit_bytes=VMEM_LIMIT),
-    )(where, *[resident(array) for array in arrays])
-
-
-def crossed(where, grad, partner, arrived, begin):
+    )(*[resident(array) for array in arrays])
+
+
+def crossed(grad, partner, arrived, begin):
     wide, depth = arrived.shape
     rows = grad.shape[0]
     pieces = [(2, 2, rows // 8, wide)] * 4
     sums = [(rows, wide), (wide, rows), (rows, wide)]
     kernel = functools.partial(cross_kernel, begin)
-    return product_call(kernel, pieces, sums, 4 * rows * wide * depth, where, grad, partner, arrived)
+    return product_call(kernel, pieces, sums, 4 * rows * wide * depth, grad, partner, arrived)
 
 
 def total_of(refs, *at):
@@ -250,8 +254,8 @@
     return slice(start, start + CHUNKS[part])
 
 
-def first_sums_kernel(where_ref, *refs):
-    x_lo = where_ref[2]
+def first_sums_kernel(*refs):
+    _, _, x_lo, _ = position()
     for side, out_ref in ((x_lo, refs[-2]), (1 - x_lo, refs[-1])):
         out_ref[:, :768] = total_of(refs[:4], side)
         for j in range(FIRST):
@@ -259,7 +263,7 @@
                 out_ref[:, columns_of(product, j)] = total_of(refs[4 + 4 * j : 8 + 4 * j], side, product)
 
 
-def first_sums(where, pieces):
+def first_sums(pieces):
     shape = jax.ShapeDtypeStruct((96, 768 + 2 * BEGINS[FIRST]), jnp.float32)
     return pl.pallas_call(
         first_sums_kernel,
@@ -268,12 +272,12 @@
         out_specs=[pl.BlockSpec(memory_space=pltpu.VMEM)] * 2,
         cost_estimate=pl.CostEstimate(flops=4 * 3 * 96 * 768 * 2, bytes_accessed=10 * 3 * 96 * 768 * 4, transcendentals=0),
         compiler_params=pltpu.CompilerParams(vmem_limit_bytes=2 * VMEM_LIMIT),
-    )(where, *pieces)
-
-
-def far_sums_kernel(where_ref, keep_ref, got_ref, *refs):
+    )(*pieces)
+
+
+def far_sums_kernel(keep_ref, got_ref, *refs):
     pieces, (far_ref, give_ref) = refs[:-2], refs[-2:]
-    core, x_lo = where_ref[0], where_ref[2]
+    core, _, x_lo, _ = position()
     start = BEGINS[FIRST]
     for j in range(FIRST, len(CHUNKS)):
         columns = slice(BEGINS[j] - start, BEGINS[j] - start + CHUNKS[j])
@@ -299,9 +303,9 @@
                 far_ref[begin // 8 : begin // 8 + thin, i * wide : (i + 1) * wide] = value
 
 
-def near_sums_kernel(where_ref, keep_ref, got_ref, *refs):
+def near_sums_kernel(keep_ref, got_ref, *refs):
     pieces, (diagonal_ref, near_ref, give_ref) = refs[:-3], refs[-3:]
-    x_lo = where_ref[2]
+    _, _, x_lo, _ = position()
     start = BEGINS[FIRST]
     diagonal_ref[...] = keep_ref[:, :768] + got_ref[:, :768]
     near_ref[:, :start] = keep_ref[:, 768 + start :] + got_ref[:, 768 + start :]
@@ -311,7 +315,13 @@
         give_ref[:, BEGINS[j] - start : BEGINS[j] - start + CHUNKS[j]] = total_of(part, 1 - x_lo, 1)
 
 
-def last_sums(kernel, widths, where, keep, got, pieces):
+def last_sums_kernel(keep_ref, got_ref, *refs):
+    pieces, outs = refs[:-5], refs[-5:]
+    far_sums_kernel(keep_ref, got_ref, *pieces, *outs[:2])
+    near_sums_kernel(keep_ref, got_ref, *pieces, *outs[2:])
+
+
+def last_sums(kernel, widths, keep, got, pieces):
     return pl.pallas_call(
         kernel,
         out_shape=[jax.ShapeDtypeStruct((96, wide), jnp.float32) for wide in widths],
@@ -319,7 +329,7 @@
         out_specs=[pl.BlockSpec(memory_space=pltpu.VMEM)] * len(widths),
         cost_estimate=pl.CostEstimate(flops=2 * 3 * 96 * 768, bytes_accessed=4 * 3 * 96 * 768 * 4, transcendentals=0),
         compiler_params=pltpu.CompilerParams(vmem_limit_bytes=VMEM_LIMIT),
-    )(where, keep, got, *pieces)
+    )(keep, got, *pieces)
 
 
 def tied(*values):
@@ -328,24 +338,21 @@
 
 def shards(grad, old_stats):
     rows = grad.shape[0]
-    core = lax.axis_index("fsdp") & 1
-    y, x_lo = lax.axis_index("tensor") >> 1, lax.axis_index("tensor") & 1
-    ahead = core * ((lax.axis_index("fsdp") & 6) == 0)
-    where = jnp.stack([core, y, x_lo, ahead]).astype(jnp.int32)
+    core = position()[0]
 
     def spread(pieces):
         return [moved(pieces[hop], along_y(hop)) for hop in (1, 3, 2)]
 
     def pick(j, span=(0, grad.shape[1])):
-        return picked(where, grad, BEGINS[j], CHUNKS[j], span)
+        return picked(grad, BEGINS[j], CHUNKS[j], span)
 
     def cross(j):
-        return list(crossed(where, here, partner, flight[j], BEGINS[j]))
+        return list(crossed(here, partner, flight[j], BEGINS[j]))
 
     partner = moved(grad, swap_cores)
     flight = [moved(pick(0), block_flow)]
     here = held(grad)
-    square = squared(where, here)
+    square = squared(here)
     *square, partner, out1 = tied(*square, partner, pick(1))
     flight.append(moved(out1, block_flow))
     square_got = spread(square)
@@ -370,23 +377,23 @@
     got2 = spread(part2)
 
     firsts = [square[0], *square_got, part0[0], *got0, part1[0], *got1]
-    keep, give = first_sums(where, firsts)
+    keep, give = first_sums(firsts)
     wide, start = CHUNKS[3], BEGINS[3]
     flops = 2 * rows * wide * grad.shape[1]
     tall = (rows, wide)
-    (early,) = product_call(functools.partial(early_kernel, start, wide), [tall], [], flops, where, here, partner)
+    (early,) = product_call(functools.partial(early_kernel, start, wide), [tall], [], flops, here, partner)
     flight[3], early, keep = tied(flight[3], early, keep)
-    far3, near3 = product_call(middle_kernel, [tall, tall], [], flops, where, here, partner, flight[3])
+    far3, near3 = product_call(middle_kernel, [tall, tall], [], flops, here, partner, flight[3])
     give, far3, got2[0], got2[1], got2[2] = tied(give, far3, *got2)
     got = moved(give, swap_x)
     scratch = [tall, (wide, rows), tall]
     part3 = product_call(
-        late_kernel, [(2, 2, rows // 8, wide)] * 4, scratch, flops, where, here, partner, flight[3], early, far3, near3
+        late_kernel, [(2, 2, rows // 8, wide)] * 4, scratch, flops, here, partner, flight[3], early, far3, near3
     )
     pieces = [part2[0], *got2, part3[0], *spread(part3)]
     more = rows - BEGINS[FIRST]
-    diagonal, near, near_give = last_sums(near_sums_kernel, (rows, rows, more), where, keep, got, pieces)
-    far, far_give = last_sums(far_sums_kernel, (rows, more), where, keep, got, pieces)
+    widths = (rows, more, rows, rows, more)
+    far, far_give, diagonal, near, near_give = last_sums(last_sums_kernel, widths, keep, got, pieces)
 
     near_more = moved(near_give, swap_x)
     far_more = moved(far_give, to_owner_x)
@@ -399,7 +406,7 @@
         if j >= FIRST
     ]
     far_high = jnp.pad(jnp.concatenate(turned, axis=0), ((96 - more // 8, 0), (0, 0)))
-    far = far + jnp.where(core == 0, far_low, far_high)
+    far = jnp.where(core == 0, far_low, far_high) + far
     summed = jnp.stack([diagonal, near, far], axis=1)
     return decay_rate * old_stats + (1.0 - decay_rate) * COLS ** (-0.5) * summed
 

time: 152 us -> 149 us (0.980)
  Pallas kernels: 53.6 us -> 45.8 us
  waiting for transfers between devices: 60.6 us -> 65.9 us
    ppermute x24, waiting for transfers between devices: 60.6 us -> 65.9 us  [moved(): return lax.ppermute(value, AXES, pairs)]
    pallas_call x6, Pallas kernels: 25.6 us -> 22.1 us  [product_call(): pl.pallas_call(kernel, out_shape=[jax.ShapeDtypeStruct(shape, jnp.float32...]
    pallas_call x4, Pallas kernels: 9.29 us -> 7.13 us  [picked(): pl.pallas_call(functools.partial(pick_kernel, begin, wide // 8, span), ou...]
  transfers between devices with their start and end apart: 24 -> 24, of which waited for: 13 -> 13; matrix products, arithmetic and copies ran while one was open for 0% -> 0% of each run, Pallas kernels for 35% -> 31%
where the time goes in v3:
time: 149 us
  waiting for transfers between devices  65.9 us (44%)
  Pallas kernels  45.8 us (31%)
  starting transfers between devices  35.5 us (24%)
    ppermute x24, waiting for transfers between devices, moved(): return lax.ppermute(value, AXES, pairs)  65.9 us
    ppermute x24, starting transfers between devices, moved(): return lax.ppermute(value, AXES, pairs)  35.5 us
    pallas_call x6, Pallas kernels, product_call(): pl.pallas_call(kernel, out_shape=[jax.ShapeDtypeStruct(shape, jnp.float32...  22.1 us
    pallas_call x1, Pallas kernels, squared(): pl.pallas_call(square_kernel, out_shape=[jax.ShapeDtypeStruct(piece, jnp....  8.29 us
    pallas_call x2, Pallas kernels, held(): pl.pallas_call(hold_kernel, out_shape=pltpu.VMEM(value.shape, value.dtype...  7.85 us
    pallas_call x4, Pallas kernels, picked(): pl.pallas_call(functools.partial(pick_kernel, begin, wide // 8, span), ou...  7.13 us
  transfers between devices with their start and end apart: 24, of which 13 were waited for; matrix products, arithmetic and copies ran while one was open for 0% of the time, Pallas kernels for 31%

profile of v3, /device:TPU:97, one launch (start us, length us, event | category | flops | bytes accessed | tf_op | source)
XLA Modules:
  0.0 148.7 jit_solution(17146048944036008340)
XLA Ops:
  0.0 0.7 collective-permute-start.1
  0.7 2.0 %shard_map.28 = bf16[256,6656]{1,0:T(8,128)(2,1)S(1)} custom-call(bf16[768,6656]{1,0:T(8,128)(2,1)} %grad_ref.7), custom_call_target="tpu_custom_call" | custom-call | bytes 6815744 | tf_op jit(solution)/shard_map/pallas_call | solution.py:79
  2.7 1.3 collective-permute-start
  4.0 3.9 %shard_map.29.own_ref = bf16[768,6656]{1,0:T(8,128)(2,1)S(1)} custom-call(bf16[768,6656]{1,0:T(8,128)(2,1)} %grad_ref.7), custom_call_target="tpu_custom_call" | custom-call | bytes 20447232 | tf_op jit(solution)/shard_map/pallas_call | solution.py:97
  7.9 2.0 %shard_map.31 = bf16[256,6656]{1,0:T(8,128)(2,1)S(1)} custom-call(bf16[768,6656]{1,0:T(8,128)(2,1)} %grad_ref.7), custom_call_target="tpu_custom_call" | custom-call | bytes 6815744 | tf_op jit(solution)/shard_map/pallas_call | solution.py:79
  9.9 8.3 %shard_map.30 = (f32[2,96,768]{2,1,0:T(8,128)S(1)}, f32[2,96,768]{2,1,0:T(8,128)S(1)}, f32[2,96,768]{2,1,0:T(8,128)S(1)}, f32[2,96,768]{2,1,0:T(8,128)S(1)}) custom-call(bf16[768,6656]{1,0:T(8,128)(2,1)S(1)} %shard_map.29.own_ref), custom_call_target="tpu_custom_call" | custom-call | flops 7851737088 | bytes 12582912 | tf_op jit(solution)/shard_map/pallas_call | solution.py:138
  18.2 0.0 collective-permute-done.1.source_ref
  18.3 4.2 %collective-permute-start.9 = (bf16[256,6656]{1,0:T(8,128)(2,1)S(1)}, bf16[256,6656]{1,0:T(8,128)(2,1)S(1)}, u32[]{:S(2)}, u32[]{:S(2)}) collective-permute-start(bf16[256,6656]{1,0:T(8,128)(2,1)S(1)} %shard_map.31), channel_id=1, source_target_pairs={{0,120},{1,121},{2,122},{3,123},{4,124},{5,125},{6,126},{7,127},{8... | collective-permute-start | bytes 10223624 | tf_op jit(solution)/shard_map/ppermute | solution.py:28
  22.4 1.3 collective-permute-start.2
  23.7 1.4 collective-permute-start.3
  25.2 1.6 %collective-permute-start.4 = (f32[2,96,768]{2,1,0:T(8,128)S(1)}, f32[2,96,768]{2,1,0:T(8,128)S(1)}, u32[]{:S(2)}, u32[]{:S(2)}) collective-permute-start(f32[2,96,768]{2,1,0:T(8,128)S(1)} %get-tuple-element.90), channel_id=1, source_target_pairs={{0,4},{1,5},{2,6},{3,7},{4,0},{5,1},{6,2},{7,3},{8,12},{9,13},{10,... | collective-permute-start | bytes 1769480 | tf_op jit(solution)/shard_map/ppermute | solution.py:28
  26.8 1.6 %shard_map.33 = bf16[128,6656]{1,0:T(8,128)(2,1)S(1)} custom-call(bf16[768,6656]{1,0:T(8,128)(2,1)} %grad_ref.7), custom_call_target="tpu_custom_call" | custom-call | bytes 3407872 | tf_op jit(solution)/shard_map/pallas_call | solution.py:79
  28.4 1.6 %shard_map.34 = bf16[128,6656]{1,0:T(8,128)(2,1)S(1)} custom-call(bf16[768,6656]{1,0:T(8,128)(2,1)} %grad_ref.7), custom_call_target="tpu_custom_call" | custom-call | bytes 3407872 | tf_op jit(solution)/shard_map/pallas_call | solution.py:79
  30.0 3.9 %shard_map.32.pair_ref = bf16[768,6656]{1,0:T(8,128)(2,1)S(1)} custom-call(bf16[768,6656]{1,0:T(8,128)(2,1)} %copy-done), custom_call_target="tpu_custom_call" | custom-call | bytes 20447232 | tf_op jit(solution)/shard_map/pallas_call | solution.py:97
  33.9 11.9 %collective-permute-done.got_ref = bf16[256,6656]{1,0:T(8,128)(2,1)S(1)} collective-permute-done((bf16[256,6656]{1,0:T(8,128)(2,1)S(1)}, bf16[256,6656]{1,0:T(8,128)(2,1)S(1)}, u32[]{:S(2)}, u32[]{:S(2)}) %collective-permute-start) | collective-permute-done | bytes 3407904 | tf_op jit(solution)/shard_map/ppermute | solution.py:28
  45.9 5.6 %shard_map.35 = (f32[2,2,96,256]{3,2,1,0:T(8,128)S(1)}, f32[2,2,96,256]{3,2,1,0:T(8,128)S(1)}, f32[2,2,96,256]{3,2,1,0:T(8,128)S(1)}, f32[2,2,96,256]{3,2,1,0:T(8,128)S(1)}) custom-call(bf16[768,6656]{1,0:T(8,128)(2,1)S(1)} %shard_map.29.own_ref, bf16[768,6656]{1,0:T(8,128)(2,1)S(1)} %shard_map.32.pair_ref, bf16[256,6656]{1,0:T(8,128)(2,1)S(1)} %collective-permute-done.got_ref), custom_call_target="tpu_custom_call" | custom-call | flops 5234491392 | bytes 27262976 | tf_op jit(solution)/shard_map/pallas_call | solution.py:228
  51.5 0.0 collective-permute-done.2.refs_1_
  51.5 0.0 collective-permute-done.3.refs_2_
  51.5 0.0 collective-permute-done.4.refs_3_
  51.5 1.4 collective-permute-start.5
  52.8 1.7 %collective-permute-start.6 = (f32[2,2,96,256]{3,2,1,0:T(8,128)S(1)}, f32[2,2,96,256]{3,2,1,0:T(8,128)S(1)}, u32[]{:S(2)}, u32[]{:S(2)}) collective-permute-start(f32[2,2,96,256]{3,2,1,0:T(8,128)S(1)} %get-tuple-element.92), channel_id=1, source_target_pairs={{0,6},{1,7},{2,0},{3,1},{4,2},{5,3},{6,4},{7,5},{8,14},{9,15},{10,... | collective-permute-start | bytes 1179656 | tf_op jit(solution)/shard_map/ppermute | solution.py:28
  54.5 1.4 collective-permute-start.7
  55.9 2.1 %collective-permute-start.10 = (bf16[128,6656]{1,0:T(8,128)(2,1)S(1)}, bf16[128,6656]{1,0:T(8,128)(2,1)S(1)}, u32[]{:S(2)}, u32[]{:S(2)}) collective-permute-start(bf16[128,6656]{1,0:T(8,128)(2,1)S(1)} %shard_map.33), channel_id=1, source_target_pairs={{0,120},{1,121},{2,122},{3,123},{4,124},{5,125},{6,126},{7,127},{8... | collective-permute-start | bytes 5111816 | tf_op jit(solution)/shard_map/ppermute | solution.py:28
  58.0 4.7 %collective-permute-done.5.refs_5_ = f32[2,2,96,256]{3,2,1,0:T(8,128)S(1)} collective-permute-done((f32[2,2,96,256]{3,2,1,0:T(8,128)S(1)}, f32[2,2,96,256]{3,2,1,0:T(8,128)S(1)}, u32[]{:S(2)}, u32[]{:S(2)}) %collective-permute-start.5) | collective-permute-done | bytes 393248 | tf_op jit(solution)/shard_map/ppermute | solution.py:28
  62.7 1.3 collective-permute-done.6.refs_6_
  64.0 6.1 %collective-permute-done.7.refs_7_ = f32[2,2,96,256]{3,2,1,0:T(8,128)S(1)} collective-permute-done((f32[2,2,96,256]{3,2,1,0:T(8,128)S(1)}, f32[2,2,96,256]{3,2,1,0:T(8,128)S(1)}, u32[]{:S(2)}, u32[]{:S(2)}) %collective-permute-start.7) | collective-permute-done | bytes 393248 | tf_op jit(solution)/shard_map/ppermute | solution.py:28
  70.1 1.8 %collective-permute-start.8 = (bf16[128,6656]{1,0:T(8,128)(2,1)S(1)}, bf16[128,6656]{1,0:T(8,128)(2,1)S(1)}, u32[]{:S(2)}, u32[]{:S(2)}) collective-permute-start(bf16[128,6656]{1,0:T(8,128)(2,1)S(1)} %shard_map.34), channel_id=1, source_target_pairs={{0,120},{1,121},{2,122},{3,123},{4,124},{5,125},{6,126},{7,127},{8... | collective-permute-start | bytes 5111816 | tf_op jit(solution)/shard_map/ppermute | solution.py:28
  71.9 10.5 %collective-permute-done.9.got_ref = bf16[256,6656]{1,0:T(8,128)(2,1)S(1)} collective-permute-done((bf16[256,6656]{1,0:T(8,128)(2,1)S(1)}, bf16[256,6656]{1,0:T(8,128)(2,1)S(1)}, u32[]{:S(2)}, u32[]{:S(2)}) %collective-permute-start.9) | collective-permute-done | bytes 3407904 | tf_op jit(solution)/shard_map/ppermute | solution.py:28
  82.4 5.6 %shard_map.37 = (f32[2,2,96,256]{3,2,1,0:T(8,128)S(1)}, f32[2,2,96,256]{3,2,1,0:T(8,128)S(1)}, f32[2,2,96,256]{3,2,1,0:T(8,128)S(1)}, f32[2,2,96,256]{3,2,1,0:T(8,128)S(1)}) custom-call(bf16[768,6656]{1,0:T(8,128)(2,1)S(1)} %shard_map.29.own_ref, bf16[768,6656]{1,0:T(8,128)(2,1)S(1)} %shard_map.32.pair_ref, bf16[256,6656]{1,0:T(8,128)(2,1)S(1)} %collective-permute-done.9.got_ref), custom_call_target="tpu_custom_call" | custom-call | flops 5234491392 | bytes 27262976 | tf_op jit(solution)/shard_map/pallas_call | solution.py:228
  88.0 1.4 collective-permute-start.11
  89.3 1.5 %collective-permute-start.12 = (f32[2,2,96,256]{3,2,1,0:T(8,128)S(1)}, f32[2,2,96,256]{3,2,1,0:T(8,128)S(1)}, u32[]{:S(2)}, u32[]{:S(2)}) collective-permute-start(f32[2,2,96,256]{3,2,1,0:T(8,128)S(1)} %get-tuple-element.115), channel_id=1, source_target_pairs={{0,6},{1,7},{2,0},{3,1},{4,2},{5,3},{6,4},{7,5},{8,14},{9,15},{10,... | collective-permute-start | bytes 1179656 | tf_op jit(solution)/shard_map/ppermute | solution.py:28
  90.9 1.6 %collective-permute-start.13 = (f32[2,2,96,256]{3,2,1,0:T(8,128)S(1)}, f32[2,2,96,256]{3,2,1,0:T(8,128)S(1)}, u32[]{:S(2)}, u32[]{:S(2)}) collective-permute-start(f32[2,2,96,256]{3,2,1,0:T(8,128)S(1)} %get-tuple-element.116), channel_id=1, source_target_pairs={{0,4},{1,5},{2,6},{3,7},{4,0},{5,1},{6,2},{7,3},{8,12},{9,13},{10,... | collective-permute-start | bytes 1179656 | tf_op jit(solution)/shard_map/ppermute | solution.py:28
  92.4 8.2 %collective-permute-done.10.got_ref = bf16[128,6656]{1,0:T(8,128)(2,1)S(1)} collective-permute-done((bf16[128,6656]{1,0:T(8,128)(2,1)S(1)}, bf16[128,6656]{1,0:T(8,128)(2,1)S(1)}, u32[]{:S(2)}, u32[]{:S(2)}) %collective-permute-start.10) | collective-permute-done | bytes 1703968 | tf_op jit(solution)/shard_map/ppermute | solution.py:28
  100.6 5.5 %shard_map.38 = (f32[2,2,96,128]{3,2,1,0:T(8,128)S(1)}, f32[2,2,96,128]{3,2,1,0:T(8,128)S(1)}, f32[2,2,96,128]{3,2,1,0:T(8,128)S(1)}, f32[2,2,96,128]{3,2,1,0:T(8,128)S(1)}) custom-call(bf16[768,6656]{1,0:T(8,128)(2,1)S(1)} %shard_map.29.own_ref, bf16[768,6656]{1,0:T(8,128)(2,1)S(1)} %shard_map.32.pair_ref, bf16[128,6656]{1,0:T(8,128)(2,1)S(1)} %collective-permute-done.10.got_ref), custom_call_target="tpu_custom_call" | custom-call | flops 2617245696 | bytes 13631488 | tf_op jit(solution)/shard_map/pallas_call | solution.py:228
  106.1 0.0 collective-permute-done.11.refs_9_
  106.1 0.0 collective-permute-done.12.refs_10_
  106.1 0.4 collective-permute-done.13.refs_11_
  106.6 1.1 collective-permute-start.14
  107.7 1.5 %collective-permute-start.15 = (f32[2,2,96,128]{3,2,1,0:T(8,128)S(1)}, f32[2,2,96,128]{3,2,1,0:T(8,128)S(1)}, u32[]{:S(2)}, u32[]{:S(2)}) collective-permute-start(f32[2,2,96,128]{3,2,1,0:T(8,128)S(1)} %get-tuple-element.126), channel_id=1, source_target_pairs={{0,6},{1,7},{2,0},{3,1},{4,2},{5,3},{6,4},{7,5},{8,14},{9,15},{10,... | collective-permute-start | bytes 589832 | tf_op jit(solution)/shard_map/ppermute | solution.py:28
  109.3 1.3 collective-permute-start.16
  110.6 0.3 shard_map.39
  110.9 8.0 %collective-permute-done.8.got_ref = bf16[128,6656]{1,0:T(8,128)(2,1)S(1)} collective-permute-done((bf16[128,6656]{1,0:T(8,128)(2,1)S(1)}, bf16[128,6656]{1,0:T(8,128)(2,1)S(1)}, u32[]{:S(2)}, u32[]{:S(2)}) %collective-permute-start.8) | collective-permute-done | bytes 1703968 | tf_op jit(solution)/shard_map/ppermute | solution.py:28
  118.9 0.0 collective-permute-done.14.refs_1_
  118.9 0.0 collective-permute-done.15.refs_2_
  118.9 0.0 collective-permute-done.16.refs_3_
  118.9 1.3 collective-permute-start.17
  120.2 5.5 %shard_map.41 = (f32[2,2,96,128]{3,2,1,0:T(8,128)S(1)}, f32[2,2,96,128]{3,2,1,0:T(8,128)S(1)}, f32[2,2,96,128]{3,2,1,0:T(8,128)S(1)}, f32[2,2,96,128]{3,2,1,0:T(8,128)S(1)}) custom-call(bf16[768,6656]{1,0:T(8,128)(2,1)S(1)} %shard_map.29.own_ref, bf16[768,6656]{1,0:T(8,128)(2,1)S(1)} %shard_map.32.pair_ref, ...), custom_call_target="tpu_custom_call" | custom-call | flops 1308622848 | bytes 6815744 | tf_op jit(solution)/shard_map/pallas_call | solution.py:228
  125.7 0.0 copy-start.1
  125.7 1.4 collective-permute-start.18
  127.0 1.5 %collective-permute-start.19 = (f32[2,2,96,128]{3,2,1,0:T(8,128)S(1)}, f32[2,2,96,128]{3,2,1,0:T(8,128)S(1)}, u32[]{:S(2)}, u32[]{:S(2)}) collective-permute-start(f32[2,2,96,128]{3,2,1,0:T(8,128)S(1)} %get-tuple-element.138), channel_id=1, source_target_pairs={{0,6},{1,7},{2,0},{3,1},{4,2},{5,3},{6,4},{7,5},{8,14},{9,15},{10,... | collective-permute-start | bytes 589832 | tf_op jit(solution)/shard_map/ppermute | solution.py:28
  128.6 1.6 %collective-permute-start.20 = (f32[2,2,96,128]{3,2,1,0:T(8,128)S(1)}, f32[2,2,96,128]{3,2,1,0:T(8,128)S(1)}, u32[]{:S(2)}, u32[]{:S(2)}) collective-permute-start(f32[2,2,96,128]{3,2,1,0:T(8,128)S(1)} %get-tuple-element.139), channel_id=1, source_target_pairs={{0,4},{1,5},{2,6},{3,7},{4,0},{5,1},{6,2},{7,3},{8,12},{9,13},{10,... | collective-permute-start | bytes 589832 | tf_op jit(solution)/shard_map/ppermute | solution.py:28
  130.1 3.1 %collective-permute-done.18.refs_5_ = f32[2,2,96,128]{3,2,1,0:T(8,128)S(1)} collective-permute-done((f32[2,2,96,128]{3,2,1,0:T(8,128)S(1)}, f32[2,2,96,128]{3,2,1,0:T(8,128)S(1)}, u32[]{:S(2)}, u32[]{:S(2)}) %collective-permute-start.18) | collective-permute-done | bytes 196640 | tf_op jit(solution)/shard_map/ppermute | solution.py:28
  133.2 0.5 collective-permute-done.19.refs_6_
  133.8 1.6 %collective-permute-done.20.refs_7_ = f32[2,2,96,128]{3,2,1,0:T(8,128)S(1)} collective-permute-done((f32[2,2,96,128]{3,2,1,0:T(8,128)S(1)}, f32[2,2,96,128]{3,2,1,0:T(8,128)S(1)}, u32[]{:S(2)}, u32[]{:S(2)}) %collective-permute-start.20) | collective-permute-done | bytes 196640 | tf_op jit(solution)/shard_map/ppermute | solution.py:28
  135.4 0.0 collective-permute-done.17.got_ref
  135.4 0.1 shard_map.42
  135.5 0.1 collective-permute-start.22
  135.6 0.3 collective-permute-start.21
  135.9 2.0 %collective-permute-start.23 = (f32[96,768]{1,0:T(8,128)S(1)}, f32[96,768]{1,0:T(8,128)S(1)}, u32[]{:S(2)}, u32[]{:S(2)}) collective-permute-start(f32[96,768]{1,0:T(8,128)S(1)} %get-tuple-element.144), channel_id=1, source_target_pairs={{0,120},{1,121},{2,122},{3,123},{4,124},{5,125},{6,126},{7,127},{8... | collective-permute-start | bytes 884744 | tf_op jit(solution)/shard_map/ppermute | solution.py:28
  137.9 5.0 %collective-permute-done.22 = f32[96,256]{1,0:T(8,128)S(1)} collective-permute-done((f32[96,256]{1,0:T(8,128)S(1)}, f32[96,256]{1,0:T(8,128)S(1)}, u32[]{:S(2)}, u32[]{:S(2)}) %collective-permute-start.22) | collective-permute-done | bytes 98336 | tf_op jit(solution)/shard_map/ppermute | solution.py:28
  143.0 0.0 collective-permute-done.21
  143.1 4.5 %collective-permute-done.23 = f32[96,768]{1,0:T(8,128)S(1)} collective-permute-done((f32[96,768]{1,0:T(8,128)S(1)}, f32[96,768]{1,0:T(8,128)S(1)}, u32[]{:S(2)}, u32[]{:S(2)}) %collective-permute-start.23) | collective-permute-done | bytes 294944 | tf_op jit(solution)/shard_map/ppermute | solution.py:28
  147.6 0.0 copy-done.1
  147.6 1.0 fusion
  (10 shorter events, 0.1 us)
Async XLA Ops:
  0.0 18.2 %collective-permute-start.1 = (bf16[768,6656]{1,0:T(8,128)(2,1)}, bf16[768,6656]{1,0:T(8,128)(2,1)S(1)}, u32[]{:S(2)}, u32[]{:S(2)}) collective-permute-start(bf16[768,6656]{1,0:T(8,128)(2,1)} %grad_ref.7), channel_id=1, source_target_pairs={{0,8},{1,9},{2,10},{3,11},{4,12},{5,13},{6,14},{7,15},{8,0},{9,1},... | collective-permute-start | bytes 30670856 | tf_op jit(solution)/shard_map/ppermute | solution.py:28
  2.7 43.2 %collective-permute-start = (bf16[256,6656]{1,0:T(8,128)(2,1)S(1)}, bf16[256,6656]{1,0:T(8,128)(2,1)S(1)}, u32[]{:S(2)}, u32[]{:S(2)}) collective-permute-start(bf16[256,6656]{1,0:T(8,128)(2,1)S(1)} %shard_map.28), channel_id=1, source_target_pairs={{0,120},{1,121},{2,122},{3,123},{4,124},{5,125},{6,126},{7,127},{8... | collective-permute-start | bytes 10223624 | tf_op jit(solution)/shard_map/ppermute | solution.py:28
  18.3 10.1 %copy-start = (bf16[768,6656]{1,0:T(8,128)(2,1)}, bf16[768,6656]{1,0:T(8,128)(2,1)S(1)}, u32[]{:S(2)}) copy-start(bf16[768,6656]{1,0:T(8,128)(2,1)S(1)} %collective-permute-done.1.source_ref) | copy-start | bytes 30670852
  18.3 64.1 %collective-permute-start.9 = (bf16[256,6656]{1,0:T(8,128)(2,1)S(1)}, bf16[256,6656]{1,0:T(8,128)(2,1)S(1)}, u32[]{:S(2)}, u32[]{:S(2)}) collective-permute-start(bf16[256,6656]{1,0:T(8,128)(2,1)S(1)} %shard_map.31), channel_id=1, source_target_pairs={{0,120},{1,121},{2,122},{3,123},{4,124},{5,125},{6,126},{7,127},{8... | collective-permute-start | bytes 10223624 | tf_op jit(solution)/shard_map/ppermute | solution.py:28
  22.4 29.0 %collective-permute-start.2 = (f32[2,96,768]{2,1,0:T(8,128)S(1)}, f32[2,96,768]{2,1,0:T(8,128)S(1)}, u32[]{:S(2)}, u32[]{:S(2)}) collective-permute-start(f32[2,96,768]{2,1,0:T(8,128)S(1)} %get-tuple-element.88), channel_id=1, source_target_pairs={{0,2},{1,3},{2,4},{3,5},{4,6},{5,7},{6,0},{7,1},{8,10},{9,11},{10,... | collective-permute-start | bytes 1769480 | tf_op jit(solution)/shard_map/ppermute | solution.py:28
  23.7 27.7 %collective-permute-start.3 = (f32[2,96,768]{2,1,0:T(8,128)S(1)}, f32[2,96,768]{2,1,0:T(8,128)S(1)}, u32[]{:S(2)}, u32[]{:S(2)}) collective-permute-start(f32[2,96,768]{2,1,0:T(8,128)S(1)} %get-tuple-element.89), channel_id=1, source_target_pairs={{0,6},{1,7},{2,0},{3,1},{4,2},{5,3},{6,4},{7,5},{8,14},{9,15},{10,... | collective-permute-start | bytes 1769480 | tf_op jit(solution)/shard_map/ppermute | solution.py:28
  25.2 26.3 %collective-permute-start.4 = (f32[2,96,768]{2,1,0:T(8,128)S(1)}, f32[2,96,768]{2,1,0:T(8,128)S(1)}, u32[]{:S(2)}, u32[]{:S(2)}) collective-permute-start(f32[2,96,768]{2,1,0:T(8,128)S(1)} %get-tuple-element.90), channel_id=1, source_target_pairs={{0,4},{1,5},{2,6},{3,7},{4,0},{5,1},{6,2},{7,3},{8,12},{9,13},{10,... | collective-permute-start | bytes 1769480 | tf_op jit(solution)/shard_map/ppermute | solution.py:28
  51.5 11.2 %collective-permute-start.5 = (f32[2,2,96,256]{3,2,1,0:T(8,128)S(1)}, f32[2,2,96,256]{3,2,1,0:T(8,128)S(1)}, u32[]{:S(2)}, u32[]{:S(2)}) collective-permute-start(f32[2,2,96,256]{3,2,1,0:T(8,128)S(1)} %get-tuple-element.91), channel_id=1, source_target_pairs={{0,2},{1,3},{2,4},{3,5},{4,6},{5,7},{6,0},{7,1},{8,10},{9,11},{10,... | collective-permute-start | bytes 1179656 | tf_op jit(solution)/shard_map/ppermute | solution.py:28
  52.8 11.2 %collective-permute-start.6 = (f32[2,2,96,256]{3,2,1,0:T(8,128)S(1)}, f32[2,2,96,256]{3,2,1,0:T(8,128)S(1)}, u32[]{:S(2)}, u32[]{:S(2)}) collective-permute-start(f32[2,2,96,256]{3,2,1,0:T(8,128)S(1)} %get-tuple-element.92), channel_id=1, source_target_pairs={{0,6},{1,7},{2,0},{3,1},{4,2},{5,3},{6,4},{7,5},{8,14},{9,15},{10,... | collective-permute-start | bytes 1179656 | tf_op jit(solution)/shard_map/ppermute | solution.py:28
  54.5 15.6 %collective-permute-start.7 = (f32[2,2,96,256]{3,2,1,0:T(8,128)S(1)}, f32[2,2,96,256]{3,2,1,0:T(8,128)S(1)}, u32[]{:S(2)}, u32[]{:S(2)}) collective-permute-start(f32[2,2,96,256]{3,2,1,0:T(8,128)S(1)} %get-tuple-element.93), channel_id=1, source_target_pairs={{0,4},{1,5},{2,6},{3,7},{4,0},{5,1},{6,2},{7,3},{8,12},{9,13},{10,... | collective-permute-start | bytes 1179656 | tf_op jit(solution)/shard_map/ppermute | solution.py:28
  55.9 44.7 %collective-permute-start.10 = (bf16[128,6656]{1,0:T(8,128)(2,1)S(1)}, bf16[128,6656]{1,0:T(8,128)(2,1)S(1)}, u32[]{:S(2)}, u32[]{:S(2)}) collective-permute-start(bf16[128,6656]{1,0:T(8,128)(2,1)S(1)} %shard_map.33), channel_id=1, source_target_pairs={{0,120},{1,121},{2,122},{3,123},{4,124},{5,125},{6,126},{7,127},{8... | collective-permute-start | bytes 5111816 | tf_op jit(solution)/shard_map/ppermute | solution.py:28
  70.1 48.8 %collective-permute-start.8 = (bf16[128,6656]{1,0:T(8,128)(2,1)S(1)}, bf16[128,6656]{1,0:T(8,128)(2,1)S(1)}, u32[]{:S(2)}, u32[]{:S(2)}) collective-permute-start(bf16[128,6656]{1,0:T(8,128)(2,1)S(1)} %shard_map.34), channel_id=1, source_target_pairs={{0,120},{1,121},{2,122},{3,123},{4,124},{5,125},{6,126},{7,127},{8... | collective-permute-start | bytes 5111816 | tf_op jit(solution)/shard_map/ppermute | solution.py:28
  88.0 18.2 %collective-permute-start.11 = (f32[2,2,96,256]{3,2,1,0:T(8,128)S(1)}, f32[2,2,96,256]{3,2,1,0:T(8,128)S(1)}, u32[]{:S(2)}, u32[]{:S(2)}) collective-permute-start(f32[2,2,96,256]{3,2,1,0:T(8,128)S(1)} %get-tuple-element.114), channel_id=1, source_target_pairs={{0,2},{1,3},{2,4},{3,5},{4,6},{5,7},{6,0},{7,1},{8,10},{9,11},{10,... | collective-permute-start | bytes 1179656 | tf_op jit(solution)/shard_map/ppermute | solution.py:28
  89.3 16.8 %collective-permute-start.12 = (f32[2,2,96,256]{3,2,1,0:T(8,128)S(1)}, f32[2,2,96,256]{3,2,1,0:T(8,128)S(1)}, u32[]{:S(2)}, u32[]{:S(2)}) collective-permute-start(f32[2,2,96,256]{3,2,1,0:T(8,128)S(1)} %get-tuple-element.115), channel_id=1, source_target_pairs={{0,6},{1,7},{2,0},{3,1},{4,2},{5,3},{6,4},{7,5},{8,14},{9,15},{10,... | collective-permute-start | bytes 1179656 | tf_op jit(solution)/shard_map/ppermute | solution.py:28
  90.9 15.7 %collective-permute-start.13 = (f32[2,2,96,256]{3,2,1,0:T(8,128)S(1)}, f32[2,2,96,256]{3,2,1,0:T(8,128)S(1)}, u32[]{:S(2)}, u32[]{:S(2)}) collective-permute-start(f32[2,2,96,256]{3,2,1,0:T(8,128)S(1)} %get-tuple-element.116), channel_id=1, source_target_pairs={{0,4},{1,5},{2,6},{3,7},{4,0},{5,1},{6,2},{7,3},{8,12},{9,13},{10,... | collective-permute-start | bytes 1179656 | tf_op jit(solution)/shard_map/ppermute | solution.py:28
  106.6 12.3 %collective-permute-start.14 = (f32[2,2,96,128]{3,2,1,0:T(8,128)S(1)}, f32[2,2,96,128]{3,2,1,0:T(8,128)S(1)}, u32[]{:S(2)}, u32[]{:S(2)}) collective-permute-start(f32[2,2,96,128]{3,2,1,0:T(8,128)S(1)} %get-tuple-element.125), channel_id=1, source_target_pairs={{0,2},{1,3},{2,4},{3,5},{4,6},{5,7},{6,0},{7,1},{8,10},{9,11},{10,... | collective-permute-start | bytes 589832 | tf_op jit(solution)/shard_map/ppermute | solution.py:28
  107.7 11.2 %collective-permute-start.15 = (f32[2,2,96,128]{3,2,1,0:T(8,128)S(1)}, f32[2,2,96,128]{3,2,1,0:T(8,128)S(1)}, u32[]{:S(2)}, u32[]{:S(2)}) collective-permute-start(f32[2,2,96,128]{3,2,1,0:T(8,128)S(1)} %get-tuple-element.126), channel_id=1, source_target_pairs={{0,6},{1,7},{2,0},{3,1},{4,2},{5,3},{6,4},{7,5},{8,14},{9,15},{10,... | collective-permute-start | bytes 589832 | tf_op jit(solution)/shard_map/ppermute | solution.py:28
  109.3 9.6 %collective-permute-start.16 = (f32[2,2,96,128]{3,2,1,0:T(8,128)S(1)}, f32[2,2,96,128]{3,2,1,0:T(8,128)S(1)}, u32[]{:S(2)}, u32[]{:S(2)}) collective-permute-start(f32[2,2,96,128]{3,2,1,0:T(8,128)S(1)} %get-tuple-element.127), channel_id=1, source_target_pairs={{0,4},{1,5},{2,6},{3,7},{4,0},{5,1},{6,2},{7,3},{8,12},{9,13},{10,... | collective-permute-start | bytes 589832 | tf_op jit(solution)/shard_map/ppermute | solution.py:28
  118.9 16.5 %collective-permute-start.17 = (f32[96,1792]{1,0:T(8,128)S(1)}, f32[96,1792]{1,0:T(8,128)S(1)}, u32[]{:S(2)}, u32[]{:S(2)}) collective-permute-start(f32[96,1792]{1,0:T(8,128)S(1)} %get-tuple-element.128), channel_id=1, source_target_pairs={{0,1},{1,0},{2,3},{3,2},{4,5},{5,4},{6,7},{7,6},{8,9},{9,8},{10,11... | collective-permute-start | bytes 2064392 | tf_op jit(solution)/shard_map/ppermute | solution.py:28
  125.7 21.9 %copy-start.1 = (f32[96,3,768]{2,0,1:T(8,128)S(1)}, f32[96,3,768]{2,0,1:T(8,128)}, u32[]{:S(2)}) copy-start(f32[96,3,768]{2,0,1:T(8,128)} %param.3) | copy-start | bytes 2654212
  125.7 7.6 %collective-permute-start.18 = (f32[2,2,96,128]{3,2,1,0:T(8,128)S(1)}, f32[2,2,96,128]{3,2,1,0:T(8,128)S(1)}, u32[]{:S(2)}, u32[]{:S(2)}) collective-permute-start(f32[2,2,96,128]{3,2,1,0:T(8,128)S(1)} %get-tuple-element.137), channel_id=1, source_target_pairs={{0,2},{1,3},{2,4},{3,5},{4,6},{5,7},{6,0},{7,1},{8,10},{9,11},{10,... | collective-permute-start | bytes 589832 | tf_op jit(solution)/shard_map/ppermute | solution.py:28
  127.0 6.7 %collective-permute-start.19 = (f32[2,2,96,128]{3,2,1,0:T(8,128)S(1)}, f32[2,2,96,128]{3,2,1,0:T(8,128)S(1)}, u32[]{:S(2)}, u32[]{:S(2)}) collective-permute-start(f32[2,2,96,128]{3,2,1,0:T(8,128)S(1)} %get-tuple-element.138), channel_id=1, source_target_pairs={{0,6},{1,7},{2,0},{3,1},{4,2},{5,3},{6,4},{7,5},{8,14},{9,15},{10,... | collective-permute-start | bytes 589832 | tf_op jit(solution)/shard_map/ppermute | solution.py:28
  128.6 6.8 %collective-permute-start.20 = (f32[2,2,96,128]{3,2,1,0:T(8,128)S(1)}, f32[2,2,96,128]{3,2,1,0:T(8,128)S(1)}, u32[]{:S(2)}, u32[]{:S(2)}) collective-permute-start(f32[2,2,96,128]{3,2,1,0:T(8,128)S(1)} %get-tuple-element.139), channel_id=1, source_target_pairs={{0,4},{1,5},{2,6},{3,7},{4,0},{5,1},{6,2},{7,3},{8,12},{9,13},{10,... | collective-permute-start | bytes 589832 | tf_op jit(solution)/shard_map/ppermute | solution.py:28
  135.5 7.4 %collective-permute-start.22 = (f32[96,256]{1,0:T(8,128)S(1)}, f32[96,256]{1,0:T(8,128)S(1)}, u32[]{:S(2)}, u32[]{:S(2)}) collective-permute-start(f32[96,256]{1,0:T(8,128)S(1)} %get-tuple-element.143), channel_id=1, source_target_pairs={{0,121},{1,120},{2,123},{3,122},{4,125},{5,124},{6,127},{7,126},{8... | collective-permute-start | bytes 294920 | tf_op jit(solution)/shard_map/ppermute | solution.py:28
  135.6 7.4 %collective-permute-start.21 = (f32[96,256]{1,0:T(8,128)S(1)}, f32[96,256]{1,0:T(8,128)S(1)}, u32[]{:S(2)}, u32[]{:S(2)}) collective-permute-start(f32[96,256]{1,0:T(8,128)S(1)} %get-tuple-element.142), channel_id=1, source_target_pairs={{0,1},{1,0},{2,3},{3,2},{4,5},{5,4},{6,7},{7,6},{8,9},{9,8},{10,11... | collective-permute-start | bytes 294920 | tf_op jit(solution)/shard_map/ppermute | solution.py:28
  135.9 11.6 %collective-permute-start.23 = (f32[96,768]{1,0:T(8,128)S(1)}, f32[96,768]{1,0:T(8,128)S(1)}, u32[]{:S(2)}, u32[]{:S(2)}) collective-permute-start(f32[96,768]{1,0:T(8,128)S(1)} %get-tuple-element.144), channel_id=1, source_target_pairs={{0,120},{1,121},{2,122},{3,123},{4,124},{5,125},{6,126},{7,127},{8... | collective-permute-start | bytes 884744 | tf_op jit(solution)/shard_map/ppermute | solution.py:28

commit v4 on v3

--- a/solution.py
+++ b/solution.py
@@ -209,19 +209,17 @@
     @pl.when(core == 0)
     def _():
         flat[...] = contract(got_ref[...], pair_ref[...])
-        mixed[...] = early_ref[...]
+        cut_up(core, y, tall, flat, early_ref, outs)
 
     @pl.when((core != 0) & ~ahead)
     def _():
         tall[...] = contract(pair_ref[...], got_ref[...])
         mixed[...] = contract(own_ref[...], got_ref[...])
+        cut_up(core, y, tall, flat, mixed, outs)
 
     @pl.when(ahead)
     def _():
-        tall[...] = tall_ref[...]
-        mixed[...] = middle_ref[...]
-
-    cut_up(core, y, tall, flat, mixed, outs)
+        cut_up(core, y, tall_ref, flat, middle_ref, outs)
 
 
 def product_call(kernel, shapes, scratch, flops, *arrays):

time: 149 us -> 149 us (level)
  no operation moved by 1% of the time
where the time goes in v4:
time: 149 us
  waiting for transfers between devices  65.9 us (44%)
  Pallas kernels  45.8 us (31%)
  starting transfers between devices  35.5 us (24%)
    ppermute x24, waiting for transfers between devices, moved(): return lax.ppermute(value, AXES, pairs)  65.9 us
    ppermute x24, starting transfers between devices, moved(): return lax.ppermute(value, AXES, pairs)  35.5 us
    pallas_call x6, Pallas kernels, product_call(): pl.pallas_call(kernel, out_shape=[jax.ShapeDtypeStruct(shape, jnp.float32...  22.1 us
    pallas_call x1, Pallas kernels, squared(): pl.pallas_call(square_kernel, out_shape=[jax.ShapeDtypeStruct(piece, jnp....  8.29 us
    pallas_call x2, Pallas kernels, held(): pl.pallas_call(hold_kernel, out_shape=pltpu.VMEM(value.shape, value.dtype...  7.85 us
    pallas_call x4, Pallas kernels, picked(): pl.pallas_call(functools.partial(pick_kernel, begin, wide // 8, span), ou...  7.13 us
  transfers between devices with their start and end apart: 24, of which 13 were waited for; matrix products, arithmetic and copies ran while one was open for 0% of the time, Pallas kernels for 31%

profile of v4, /device:TPU:97, one launch (start us, length us, event | category | flops | bytes accessed | tf_op | source)
XLA Modules:
  0.0 148.7 jit_solution(5679910321857976731)
XLA Ops:
  0.0 0.7 collective-permute-start.1
  0.7 2.0 %shard_map.28 = bf16[256,6656]{1,0:T(8,128)(2,1)S(1)} custom-call(bf16[768,6656]{1,0:T(8,128)(2,1)} %grad_ref.7), custom_call_target="tpu_custom_call" | custom-call | bytes 6815744 | tf_op jit(solution)/shard_map/pallas_call | solution.py:79
  2.7 1.3 collective-permute-start
  4.0 3.9 %shard_map.29.own_ref = bf16[768,6656]{1,0:T(8,128)(2,1)S(1)} custom-call(bf16[768,6656]{1,0:T(8,128)(2,1)} %grad_ref.7), custom_call_target="tpu_custom_call" | custom-call | bytes 20447232 | tf_op jit(solution)/shard_map/pallas_call | solution.py:97
  7.9 2.0 %shard_map.31 = bf16[256,6656]{1,0:T(8,128)(2,1)S(1)} custom-call(bf16[768,6656]{1,0:T(8,128)(2,1)} %grad_ref.7), custom_call_target="tpu_custom_call" | custom-call | bytes 6815744 | tf_op jit(solution)/shard_map/pallas_call | solution.py:79
  9.9 8.3 %shard_map.30 = (f32[2,96,768]{2,1,0:T(8,128)S(1)}, f32[2,96,768]{2,1,0:T(8,128)S(1)}, f32[2,96,768]{2,1,0:T(8,128)S(1)}, f32[2,96,768]{2,1,0:T(8,128)S(1)}) custom-call(bf16[768,6656]{1,0:T(8,128)(2,1)S(1)} %shard_map.29.own_ref), custom_call_target="tpu_custom_call" | custom-call | flops 7851737088 | bytes 12582912 | tf_op jit(solution)/shard_map/pallas_call | solution.py:138
  18.2 0.0 collective-permute-done.1.source_ref
  18.3 4.2 %collective-permute-start.9 = (bf16[256,6656]{1,0:T(8,128)(2,1)S(1)}, bf16[256,6656]{1,0:T(8,128)(2,1)S(1)}, u32[]{:S(2)}, u32[]{:S(2)}) collective-permute-start(bf16[256,6656]{1,0:T(8,128)(2,1)S(1)} %shard_map.31), channel_id=1, source_target_pairs={{0,120},{1,121},{2,122},{3,123},{4,124},{5,125},{6,126},{7,127},{8... | collective-permute-start | bytes 10223624 | tf_op jit(solution)/shard_map/ppermute | solution.py:28
  22.4 1.3 collective-permute-start.2
  23.7 1.4 collective-permute-start.3
  25.2 1.6 %collective-permute-start.4 = (f32[2,96,768]{2,1,0:T(8,128)S(1)}, f32[2,96,768]{2,1,0:T(8,128)S(1)}, u32[]{:S(2)}, u32[]{:S(2)}) collective-permute-start(f32[2,96,768]{2,1,0:T(8,128)S(1)} %get-tuple-element.90), channel_id=1, source_target_pairs={{0,4},{1,5},{2,6},{3,7},{4,0},{5,1},{6,2},{7,3},{8,12},{9,13},{10,... | collective-permute-start | bytes 1769480 | tf_op jit(solution)/shard_map/ppermute | solution.py:28
  26.8 1.6 %shard_map.33 = bf16[128,6656]{1,0:T(8,128)(2,1)S(1)} custom-call(bf16[768,6656]{1,0:T(8,128)(2,1)} %grad_ref.7), custom_call_target="tpu_custom_call" | custom-call | bytes 3407872 | tf_op jit(solution)/shard_map/pallas_call | solution.py:79
  28.4 0.0 copy-done
  28.4 1.6 %shard_map.34 = bf16[128,6656]{1,0:T(8,128)(2,1)S(1)} custom-call(bf16[768,6656]{1,0:T(8,128)(2,1)} %grad_ref.7), custom_call_target="tpu_custom_call" | custom-call | bytes 3407872 | tf_op jit(solution)/shard_map/pallas_call | solution.py:79
  30.0 3.9 %shard_map.32.pair_ref = bf16[768,6656]{1,0:T(8,128)(2,1)S(1)} custom-call(bf16[768,6656]{1,0:T(8,128)(2,1)} %copy-done), custom_call_target="tpu_custom_call" | custom-call | bytes 20447232 | tf_op jit(solution)/shard_map/pallas_call | solution.py:97
  33.9 11.9 %collective-permute-done.got_ref = bf16[256,6656]{1,0:T(8,128)(2,1)S(1)} collective-permute-done((bf16[256,6656]{1,0:T(8,128)(2,1)S(1)}, bf16[256,6656]{1,0:T(8,128)(2,1)S(1)}, u32[]{:S(2)}, u32[]{:S(2)}) %collective-permute-start) | collective-permute-done | bytes 3407904 | tf_op jit(solution)/shard_map/ppermute | solution.py:28
  45.9 5.6 %shard_map.35 = (f32[2,2,96,256]{3,2,1,0:T(8,128)S(1)}, f32[2,2,96,256]{3,2,1,0:T(8,128)S(1)}, f32[2,2,96,256]{3,2,1,0:T(8,128)S(1)}, f32[2,2,96,256]{3,2,1,0:T(8,128)S(1)}) custom-call(bf16[768,6656]{1,0:T(8,128)(2,1)S(1)} %shard_map.29.own_ref, bf16[768,6656]{1,0:T(8,128)(2,1)S(1)} %shard_map.32.pair_ref, bf16[256,6656]{1,0:T(8,128)(2,1)S(1)} %collective-permute-done.got_ref), custom_call_target="tpu_custom_call" | custom-call | flops 5234491392 | bytes 27262976 | tf_op jit(solution)/shard_map/pallas_call | solution.py:226
  51.5 0.0 collective-permute-done.2.refs_1_
  51.5 0.0 collective-permute-done.3.refs_2_
  51.5 0.0 collective-permute-done.4.refs_3_
  51.5 1.4 collective-permute-start.5
  52.8 1.7 %collective-permute-start.6 = (f32[2,2,96,256]{3,2,1,0:T(8,128)S(1)}, f32[2,2,96,256]{3,2,1,0:T(8,128)S(1)}, u32[]{:S(2)}, u32[]{:S(2)}) collective-permute-start(f32[2,2,96,256]{3,2,1,0:T(8,128)S(1)} %get-tuple-element.92), channel_id=1, source_target_pairs={{0,6},{1,7},{2,0},{3,1},{4,2},{5,3},{6,4},{7,5},{8,14},{9,15},{10,... | collective-permute-start | bytes 1179656 | tf_op jit(solution)/shard_map/ppermute | solution.py:28
  54.5 1.4 collective-permute-start.7
  55.9 2.1 %collective-permute-start.10 = (bf16[128,6656]{1,0:T(8,128)(2,1)S(1)}, bf16[128,6656]{1,0:T(8,128)(2,1)S(1)}, u32[]{:S(2)}, u32[]{:S(2)}) collective-permute-start(bf16[128,6656]{1,0:T(8,128)(2,1)S(1)} %shard_map.33), channel_id=1, source_target_pairs={{0,120},{1,121},{2,122},{3,123},{4,124},{5,125},{6,126},{7,127},{8... | collective-permute-start | bytes 5111816 | tf_op jit(solution)/shard_map/ppermute | solution.py:28
  58.0 4.7 %collective-permute-done.5.refs_5_ = f32[2,2,96,256]{3,2,1,0:T(8,128)S(1)} collective-permute-done((f32[2,2,96,256]{3,2,1,0:T(8,128)S(1)}, f32[2,2,96,256]{3,2,1,0:T(8,128)S(1)}, u32[]{:S(2)}, u32[]{:S(2)}) %collective-permute-start.5) | collective-permute-done | bytes 393248 | tf_op jit(solution)/shard_map/ppermute | solution.py:28
  62.7 1.3 collective-permute-done.6.refs_6_
  64.0 6.1 %collective-permute-done.7.refs_7_ = f32[2,2,96,256]{3,2,1,0:T(8,128)S(1)} collective-permute-done((f32[2,2,96,256]{3,2,1,0:T(8,128)S(1)}, f32[2,2,96,256]{3,2,1,0:T(8,128)S(1)}, u32[]{:S(2)}, u32[]{:S(2)}) %collective-permute-start.7) | collective-permute-done | bytes 393248 | tf_op jit(solution)/shard_map/ppermute | solution.py:28
  70.1 1.8 %collective-permute-start.8 = (bf16[128,6656]{1,0:T(8,128)(2,1)S(1)}, bf16[128,6656]{1,0:T(8,128)(2,1)S(1)}, u32[]{:S(2)}, u32[]{:S(2)}) collective-permute-start(bf16[128,6656]{1,0:T(8,128)(2,1)S(1)} %shard_map.34), channel_id=1, source_target_pairs={{0,120},{1,121},{2,122},{3,123},{4,124},{5,125},{6,126},{7,127},{8... | collective-permute-start | bytes 5111816 | tf_op jit(solution)/shard_map/ppermute | solution.py:28
  71.9 10.5 %collective-permute-done.9.got_ref = bf16[256,6656]{1,0:T(8,128)(2,1)S(1)} collective-permute-done((bf16[256,6656]{1,0:T(8,128)(2,1)S(1)}, bf16[256,6656]{1,0:T(8,128)(2,1)S(1)}, u32[]{:S(2)}, u32[]{:S(2)}) %collective-permute-start.9) | collective-permute-done | bytes 3407904 | tf_op jit(solution)/shard_map/ppermute | solution.py:28
  82.4 5.6 %shard_map.37 = (f32[2,2,96,256]{3,2,1,0:T(8,128)S(1)}, f32[2,2,96,256]{3,2,1,0:T(8,128)S(1)}, f32[2,2,96,256]{3,2,1,0:T(8,128)S(1)}, f32[2,2,96,256]{3,2,1,0:T(8,128)S(1)}) custom-call(bf16[768,6656]{1,0:T(8,128)(2,1)S(1)} %shard_map.29.own_ref, bf16[768,6656]{1,0:T(8,128)(2,1)S(1)} %shard_map.32.pair_ref, bf16[256,6656]{1,0:T(8,128)(2,1)S(1)} %collective-permute-done.9.got_ref), custom_call_target="tpu_custom_call" | custom-call | flops 5234491392 | bytes 27262976 | tf_op jit(solution)/shard_map/pallas_call | solution.py:226
  88.0 1.4 collective-permute-start.11
  89.3 1.5 %collective-permute-start.12 = (f32[2,2,96,256]{3,2,1,0:T(8,128)S(1)}, f32[2,2,96,256]{3,2,1,0:T(8,128)S(1)}, u32[]{:S(2)}, u32[]{:S(2)}) collective-permute-start(f32[2,2,96,256]{3,2,1,0:T(8,128)S(1)} %get-tuple-element.115), channel_id=1, source_target_pairs={{0,6},{1,7},{2,0},{3,1},{4,2},{5,3},{6,4},{7,5},{8,14},{9,15},{10,... | collective-permute-start | bytes 1179656 | tf_op jit(solution)/shard_map/ppermute | solution.py:28
  90.9 1.6 %collective-permute-start.13 = (f32[2,2,96,256]{3,2,1,0:T(8,128)S(1)}, f32[2,2,96,256]{3,2,1,0:T(8,128)S(1)}, u32[]{:S(2)}, u32[]{:S(2)}) collective-permute-start(f32[2,2,96,256]{3,2,1,0:T(8,128)S(1)} %get-tuple-element.116), channel_id=1, source_target_pairs={{0,4},{1,5},{2,6},{3,7},{4,0},{5,1},{6,2},{7,3},{8,12},{9,13},{10,... | collective-permute-start | bytes 1179656 | tf_op jit(solution)/shard_map/ppermute | solution.py:28
  92.4 8.2 %collective-permute-done.10.got_ref = bf16[128,6656]{1,0:T(8,128)(2,1)S(1)} collective-permute-done((bf16[128,6656]{1,0:T(8,128)(2,1)S(1)}, bf16[128,6656]{1,0:T(8,128)(2,1)S(1)}, u32[]{:S(2)}, u32[]{:S(2)}) %collective-permute-start.10) | collective-permute-done | bytes 1703968 | tf_op jit(solution)/shard_map/ppermute | solution.py:28
  100.6 5.5 %shard_map.38 = (f32[2,2,96,128]{3,2,1,0:T(8,128)S(1)}, f32[2,2,96,128]{3,2,1,0:T(8,128)S(1)}, f32[2,2,96,128]{3,2,1,0:T(8,128)S(1)}, f32[2,2,96,128]{3,2,1,0:T(8,128)S(1)}) custom-call(bf16[768,6656]{1,0:T(8,128)(2,1)S(1)} %shard_map.29.own_ref, bf16[768,6656]{1,0:T(8,128)(2,1)S(1)} %shard_map.32.pair_ref, bf16[128,6656]{1,0:T(8,128)(2,1)S(1)} %collective-permute-done.10.got_ref), custom_call_target="tpu_custom_call" | custom-call | flops 2617245696 | bytes 13631488 | tf_op jit(solution)/shard_map/pallas_call | solution.py:226
  106.1 0.0 collective-permute-done.11.refs_9_
  106.1 0.0 collective-permute-done.12.refs_10_
  106.1 0.4 collective-permute-done.13.refs_11_
  106.6 1.1 collective-permute-start.14
  107.7 1.5 %collective-permute-start.15 = (f32[2,2,96,128]{3,2,1,0:T(8,128)S(1)}, f32[2,2,96,128]{3,2,1,0:T(8,128)S(1)}, u32[]{:S(2)}, u32[]{:S(2)}) collective-permute-start(f32[2,2,96,128]{3,2,1,0:T(8,128)S(1)} %get-tuple-element.126), channel_id=1, source_target_pairs={{0,6},{1,7},{2,0},{3,1},{4,2},{5,3},{6,4},{7,5},{8,14},{9,15},{10,... | collective-permute-start | bytes 589832 | tf_op jit(solution)/shard_map/ppermute | solution.py:28
  109.3 1.3 collective-permute-start.16
  110.6 0.3 shard_map.39
  110.9 8.0 %collective-permute-done.8.got_ref = bf16[128,6656]{1,0:T(8,128)(2,1)S(1)} collective-permute-done((bf16[128,6656]{1,0:T(8,128)(2,1)S(1)}, bf16[128,6656]{1,0:T(8,128)(2,1)S(1)}, u32[]{:S(2)}, u32[]{:S(2)}) %collective-permute-start.8) | collective-permute-done | bytes 1703968 | tf_op jit(solution)/shard_map/ppermute | solution.py:28
  118.9 0.0 collective-permute-done.14.refs_1_
  118.9 0.0 collective-permute-done.15.refs_2_
  118.9 0.0 collective-permute-done.16.refs_3_
  118.9 1.3 collective-permute-start.17
  120.2 5.5 %shard_map.41 = (f32[2,2,96,128]{3,2,1,0:T(8,128)S(1)}, f32[2,2,96,128]{3,2,1,0:T(8,128)S(1)}, f32[2,2,96,128]{3,2,1,0:T(8,128)S(1)}, f32[2,2,96,128]{3,2,1,0:T(8,128)S(1)}) custom-call(bf16[768,6656]{1,0:T(8,128)(2,1)S(1)} %shard_map.29.own_ref, bf16[768,6656]{1,0:T(8,128)(2,1)S(1)} %shard_map.32.pair_ref, ...), custom_call_target="tpu_custom_call" | custom-call | flops 1308622848 | bytes 6815744 | tf_op jit(solution)/shard_map/pallas_call | solution.py:226
  125.7 0.0 copy-start.1
  125.7 1.4 collective-permute-start.18
  127.0 1.5 %collective-permute-start.19 = (f32[2,2,96,128]{3,2,1,0:T(8,128)S(1)}, f32[2,2,96,128]{3,2,1,0:T(8,128)S(1)}, u32[]{:S(2)}, u32[]{:S(2)}) collective-permute-start(f32[2,2,96,128]{3,2,1,0:T(8,128)S(1)} %get-tuple-element.138), channel_id=1, source_target_pairs={{0,6},{1,7},{2,0},{3,1},{4,2},{5,3},{6,4},{7,5},{8,14},{9,15},{10,... | collective-permute-start | bytes 589832 | tf_op jit(solution)/shard_map/ppermute | solution.py:28
  128.6 1.6 %collective-permute-start.20 = (f32[2,2,96,128]{3,2,1,0:T(8,128)S(1)}, f32[2,2,96,128]{3,2,1,0:T(8,128)S(1)}, u32[]{:S(2)}, u32[]{:S(2)}) collective-permute-start(f32[2,2,96,128]{3,2,1,0:T(8,128)S(1)} %get-tuple-element.139), channel_id=1, source_target_pairs={{0,4},{1,5},{2,6},{3,7},{4,0},{5,1},{6,2},{7,3},{8,12},{9,13},{10,... | collective-permute-start | bytes 589832 | tf_op jit(solution)/shard_map/ppermute | solution.py:28
  130.1 3.1 %collective-permute-done.18.refs_5_ = f32[2,2,96,128]{3,2,1,0:T(8,128)S(1)} collective-permute-done((f32[2,2,96,128]{3,2,1,0:T(8,128)S(1)}, f32[2,2,96,128]{3,2,1,0:T(8,128)S(1)}, u32[]{:S(2)}, u32[]{:S(2)}) %collective-permute-start.18) | collective-permute-done | bytes 196640 | tf_op jit(solution)/shard_map/ppermute | solution.py:28
  133.2 0.5 collective-permute-done.19.refs_6_
  133.8 1.6 %collective-permute-done.20.refs_7_ = f32[2,2,96,128]{3,2,1,0:T(8,128)S(1)} collective-permute-done((f32[2,2,96,128]{3,2,1,0:T(8,128)S(1)}, f32[2,2,96,128]{3,2,1,0:T(8,128)S(1)}, u32[]{:S(2)}, u32[]{:S(2)}) %collective-permute-start.20) | collective-permute-done | bytes 196640 | tf_op jit(solution)/shard_map/ppermute | solution.py:28
  135.3 0.0 collective-permute-done.17.got_ref
  135.3 0.1 shard_map.42
  135.5 0.1 collective-permute-start.22
  135.6 0.3 collective-permute-start.21
  135.9 2.0 %collective-permute-start.23 = (f32[96,768]{1,0:T(8,128)S(1)}, f32[96,768]{1,0:T(8,128)S(1)}, u32[]{:S(2)}, u32[]{:S(2)}) collective-permute-start(f32[96,768]{1,0:T(8,128)S(1)} %get-tuple-element.144), channel_id=1, source_target_pairs={{0,120},{1,121},{2,122},{3,123},{4,124},{5,125},{6,126},{7,127},{8... | collective-permute-start | bytes 884744 | tf_op jit(solution)/shard_map/ppermute | solution.py:28
  137.9 5.0 %collective-permute-done.22 = f32[96,256]{1,0:T(8,128)S(1)} collective-permute-done((f32[96,256]{1,0:T(8,128)S(1)}, f32[96,256]{1,0:T(8,128)S(1)}, u32[]{:S(2)}, u32[]{:S(2)}) %collective-permute-start.22) | collective-permute-done | bytes 98336 | tf_op jit(solution)/shard_map/ppermute | solution.py:28
  143.0 0.0 collective-permute-done.21
  143.1 4.5 %collective-permute-done.23 = f32[96,768]{1,0:T(8,128)S(1)} collective-permute-done((f32[96,768]{1,0:T(8,128)S(1)}, f32[96,768]{1,0:T(8,128)S(1)}, u32[]{:S(2)}, u32[]{:S(2)}) %collective-permute-start.23) | collective-permute-done | bytes 294944 | tf_op jit(solution)/shard_map/ppermute | solution.py:28
  147.6 1.0 fusion
  (10 shorter events, 0.1 us)
Async XLA Ops:
  0.0 18.2 %collective-permute-start.1 = (bf16[768,6656]{1,0:T(8,128)(2,1)}, bf16[768,6656]{1,0:T(8,128)(2,1)S(1)}, u32[]{:S(2)}, u32[]{:S(2)}) collective-permute-start(bf16[768,6656]{1,0:T(8,128)(2,1)} %grad_ref.7), channel_id=1, source_target_pairs={{0,8},{1,9},{2,10},{3,11},{4,12},{5,13},{6,14},{7,15},{8,0},{9,1},... | collective-permute-start | bytes 30670856 | tf_op jit(solution)/shard_map/ppermute | solution.py:28
  2.7 43.2 %collective-permute-start = (bf16[256,6656]{1,0:T(8,128)(2,1)S(1)}, bf16[256,6656]{1,0:T(8,128)(2,1)S(1)}, u32[]{:S(2)}, u32[]{:S(2)}) collective-permute-start(bf16[256,6656]{1,0:T(8,128)(2,1)S(1)} %shard_map.28), channel_id=1, source_target_pairs={{0,120},{1,121},{2,122},{3,123},{4,124},{5,125},{6,126},{7,127},{8... | collective-permute-start | bytes 10223624 | tf_op jit(solution)/shard_map/ppermute | solution.py:28
  18.3 10.1 %copy-start = (bf16[768,6656]{1,0:T(8,128)(2,1)}, bf16[768,6656]{1,0:T(8,128)(2,1)S(1)}, u32[]{:S(2)}) copy-start(bf16[768,6656]{1,0:T(8,128)(2,1)S(1)} %collective-permute-done.1.source_ref) | copy-start | bytes 30670852
  18.3 64.1 %collective-permute-start.9 = (bf16[256,6656]{1,0:T(8,128)(2,1)S(1)}, bf16[256,6656]{1,0:T(8,128)(2,1)S(1)}, u32[]{:S(2)}, u32[]{:S(2)}) collective-permute-start(bf16[256,6656]{1,0:T(8,128)(2,1)S(1)} %shard_map.31), channel_id=1, source_target_pairs={{0,120},{1,121},{2,122},{3,123},{4,124},{5,125},{6,126},{7,127},{8... | collective-permute-start | bytes 10223624 | tf_op jit(solution)/shard_map/ppermute | solution.py:28
  22.4 29.0 %collective-permute-start.2 = (f32[2,96,768]{2,1,0:T(8,128)S(1)}, f32[2,96,768]{2,1,0:T(8,128)S(1)}, u32[]{:S(2)}, u32[]{:S(2)}) collective-permute-start(f32[2,96,768]{2,1,0:T(8,128)S(1)} %get-tuple-element.88), channel_id=1, source_target_pairs={{0,2},{1,3},{2,4},{3,5},{4,6},{5,7},{6,0},{7,1},{8,10},{9,11},{10,... | collective-permute-start | bytes 1769480 | tf_op jit(solution)/shard_map/ppermute | solution.py:28
  23.7 27.7 %collective-permute-start.3 = (f32[2,96,768]{2,1,0:T(8,128)S(1)}, f32[2,96,768]{2,1,0:T(8,128)S(1)}, u32[]{:S(2)}, u32[]{:S(2)}) collective-permute-start(f32[2,96,768]{2,1,0:T(8,128)S(1)} %get-tuple-element.89), channel_id=1, source_target_pairs={{0,6},{1,7},{2,0},{3,1},{4,2},{5,3},{6,4},{7,5},{8,14},{9,15},{10,... | collective-permute-start | bytes 1769480 | tf_op jit(solution)/shard_map/ppermute | solution.py:28
  25.2 26.3 %collective-permute-start.4 = (f32[2,96,768]{2,1,0:T(8,128)S(1)}, f32[2,96,768]{2,1,0:T(8,128)S(1)}, u32[]{:S(2)}, u32[]{:S(2)}) collective-permute-start(f32[2,96,768]{2,1,0:T(8,128)S(1)} %get-tuple-element.90), channel_id=1, source_target_pairs={{0,4},{1,5},{2,6},{3,7},{4,0},{5,1},{6,2},{7,3},{8,12},{9,13},{10,... | collective-permute-start | bytes 1769480 | tf_op jit(solution)/shard_map/ppermute | solution.py:28
  51.5 11.2 %collective-permute-start.5 = (f32[2,2,96,256]{3,2,1,0:T(8,128)S(1)}, f32[2,2,96,256]{3,2,1,0:T(8,128)S(1)}, u32[]{:S(2)}, u32[]{:S(2)}) collective-permute-start(f32[2,2,96,256]{3,2,1,0:T(8,128)S(1)} %get-tuple-element.91), channel_id=1, source_target_pairs={{0,2},{1,3},{2,4},{3,5},{4,6},{5,7},{6,0},{7,1},{8,10},{9,11},{10,... | collective-permute-start | bytes 1179656 | tf_op jit(solution)/shard_map/ppermute | solution.py:28
  52.8 11.2 %collective-permute-start.6 = (f32[2,2,96,256]{3,2,1,0:T(8,128)S(1)}, f32[2,2,96,256]{3,2,1,0:T(8,128)S(1)}, u32[]{:S(2)}, u32[]{:S(2)}) collective-permute-start(f32[2,2,96,256]{3,2,1,0:T(8,128)S(1)} %get-tuple-element.92), channel_id=1, source_target_pairs={{0,6},{1,7},{2,0},{3,1},{4,2},{5,3},{6,4},{7,5},{8,14},{9,15},{10,... | collective-permute-start | bytes 1179656 | tf_op jit(solution)/shard_map/ppermute | solution.py:28
  54.5 15.6 %collective-permute-start.7 = (f32[2,2,96,256]{3,2,1,0:T(8,128)S(1)}, f32[2,2,96,256]{3,2,1,0:T(8,128)S(1)}, u32[]{:S(2)}, u32[]{:S(2)}) collective-permute-start(f32[2,2,96,256]{3,2,1,0:T(8,128)S(1)} %get-tuple-element.93), channel_id=1, source_target_pairs={{0,4},{1,5},{2,6},{3,7},{4,0},{5,1},{6,2},{7,3},{8,12},{9,13},{10,... | collective-permute-start | bytes 1179656 | tf_op jit(solution)/shard_map/ppermute | solution.py:28
  55.9 44.7 %collective-permute-start.10 = (bf16[128,6656]{1,0:T(8,128)(2,1)S(1)}, bf16[128,6656]{1,0:T(8,128)(2,1)S(1)}, u32[]{:S(2)}, u32[]{:S(2)}) collective-permute-start(bf16[128,6656]{1,0:T(8,128)(2,1)S(1)} %shard_map.33), channel_id=1, source_target_pairs={{0,120},{1,121},{2,122},{3,123},{4,124},{5,125},{6,126},{7,127},{8... | collective-permute-start | bytes 5111816 | tf_op jit(solution)/shard_map/ppermute | solution.py:28
  70.1 48.8 %collective-permute-start.8 = (bf16[128,6656]{1,0:T(8,128)(2,1)S(1)}, bf16[128,6656]{1,0:T(8,128)(2,1)S(1)}, u32[]{:S(2)}, u32[]{:S(2)}) collective-permute-start(bf16[128,6656]{1,0:T(8,128)(2,1)S(1)} %shard_map.34), channel_id=1, source_target_pairs={{0,120},{1,121},{2,122},{3,123},{4,124},{5,125},{6,126},{7,127},{8... | collective-permute-start | bytes 5111816 | tf_op jit(solution)/shard_map/ppermute | solution.py:28
  88.0 18.2 %collective-permute-start.11 = (f32[2,2,96,256]{3,2,1,0:T(8,128)S(1)}, f32[2,2,96,256]{3,2,1,0:T(8,128)S(1)}, u32[]{:S(2)}, u32[]{:S(2)}) collective-permute-start(f32[2,2,96,256]{3,2,1,0:T(8,128)S(1)} %get-tuple-element.114), channel_id=1, source_target_pairs={{0,2},{1,3},{2,4},{3,5},{4,6},{5,7},{6,0},{7,1},{8,10},{9,11},{10,... | collective-permute-start | bytes 1179656 | tf_op jit(solution)/shard_map/ppermute | solution.py:28
  89.3 16.8 %collective-permute-start.12 = (f32[2,2,96,256]{3,2,1,0:T(8,128)S(1)}, f32[2,2,96,256]{3,2,1,0:T(8,128)S(1)}, u32[]{:S(2)}, u32[]{:S(2)}) collective-permute-start(f32[2,2,96,256]{3,2,1,0:T(8,128)S(1)} %get-tuple-element.115), channel_id=1, source_target_pairs={{0,6},{1,7},{2,0},{3,1},{4,2},{5,3},{6,4},{7,5},{8,14},{9,15},{10,... | collective-permute-start | bytes 1179656 | tf_op jit(solution)/shard_map/ppermute | solution.py:28
  90.9 15.7 %collective-permute-start.13 = (f32[2,2,96,256]{3,2,1,0:T(8,128)S(1)}, f32[2,2,96,256]{3,2,1,0:T(8,128)S(1)}, u32[]{:S(2)}, u32[]{:S(2)}) collective-permute-start(f32[2,2,96,256]{3,2,1,0:T(8,128)S(1)} %get-tuple-element.116), channel_id=1, source_target_pairs={{0,4},{1,5},{2,6},{3,7},{4,0},{5,1},{6,2},{7,3},{8,12},{9,13},{10,... | collective-permute-start | bytes 1179656 | tf_op jit(solution)/shard_map/ppermute | solution.py:28
  106.6 12.3 %collective-permute-start.14 = (f32[2,2,96,128]{3,2,1,0:T(8,128)S(1)}, f32[2,2,96,128]{3,2,1,0:T(8,128)S(1)}, u32[]{:S(2)}, u32[]{:S(2)}) collective-permute-start(f32[2,2,96,128]{3,2,1,0:T(8,128)S(1)} %get-tuple-element.125), channel_id=1, source_target_pairs={{0,2},{1,3},{2,4},{3,5},{4,6},{5,7},{6,0},{7,1},{8,10},{9,11},{10,... | collective-permute-start | bytes 589832 | tf_op jit(solution)/shard_map/ppermute | solution.py:28
  107.7 11.2 %collective-permute-start.15 = (f32[2,2,96,128]{3,2,1,0:T(8,128)S(1)}, f32[2,2,96,128]{3,2,1,0:T(8,128)S(1)}, u32[]{:S(2)}, u32[]{:S(2)}) collective-permute-start(f32[2,2,96,128]{3,2,1,0:T(8,128)S(1)} %get-tuple-element.126), channel_id=1, source_target_pairs={{0,6},{1,7},{2,0},{3,1},{4,2},{5,3},{6,4},{7,5},{8,14},{9,15},{10,... | collective-permute-start | bytes 589832 | tf_op jit(solution)/shard_map/ppermute | solution.py:28
  109.3 9.6 %collective-permute-start.16 = (f32[2,2,96,128]{3,2,1,0:T(8,128)S(1)}, f32[2,2,96,128]{3,2,1,0:T(8,128)S(1)}, u32[]{:S(2)}, u32[]{:S(2)}) collective-permute-start(f32[2,2,96,128]{3,2,1,0:T(8,128)S(1)} %get-tuple-element.127), channel_id=1, source_target_pairs={{0,4},{1,5},{2,6},{3,7},{4,0},{5,1},{6,2},{7,3},{8,12},{9,13},{10,... | collective-permute-start | bytes 589832 | tf_op jit(solution)/shard_map/ppermute | solution.py:28
  118.9 16.5 %collective-permute-start.17 = (f32[96,1792]{1,0:T(8,128)S(1)}, f32[96,1792]{1,0:T(8,128)S(1)}, u32[]{:S(2)}, u32[]{:S(2)}) collective-permute-start(f32[96,1792]{1,0:T(8,128)S(1)} %get-tuple-element.128), channel_id=1, source_target_pairs={{0,1},{1,0},{2,3},{3,2},{4,5},{5,4},{6,7},{7,6},{8,9},{9,8},{10,11... | collective-permute-start | bytes 2064392 | tf_op jit(solution)/shard_map/ppermute | solution.py:28
  125.7 21.9 %copy-start.1 = (f32[96,3,768]{2,0,1:T(8,128)S(1)}, f32[96,3,768]{2,0,1:T(8,128)}, u32[]{:S(2)}) copy-start(f32[96,3,768]{2,0,1:T(8,128)} %param.3) | copy-start | bytes 2654212
  125.7 7.6 %collective-permute-start.18 = (f32[2,2,96,128]{3,2,1,0:T(8,128)S(1)}, f32[2,2,96,128]{3,2,1,0:T(8,128)S(1)}, u32[]{:S(2)}, u32[]{:S(2)}) collective-permute-start(f32[2,2,96,128]{3,2,1,0:T(8,128)S(1)} %get-tuple-element.137), channel_id=1, source_target_pairs={{0,2},{1,3},{2,4},{3,5},{4,6},{5,7},{6,0},{7,1},{8,10},{9,11},{10,... | collective-permute-start | bytes 589832 | tf_op jit(solution)/shard_map/ppermute | solution.py:28
  127.0 6.7 %collective-permute-start.19 = (f32[2,2,96,128]{3,2,1,0:T(8,128)S(1)}, f32[2,2,96,128]{3,2,1,0:T(8,128)S(1)}, u32[]{:S(2)}, u32[]{:S(2)}) collective-permute-start(f32[2,2,96,128]{3,2,1,0:T(8,128)S(1)} %get-tuple-element.138), channel_id=1, source_target_pairs={{0,6},{1,7},{2,0},{3,1},{4,2},{5,3},{6,4},{7,5},{8,14},{9,15},{10,... | collective-permute-start | bytes 589832 | tf_op jit(solution)/shard_map/ppermute | solution.py:28
  128.6 6.8 %collective-permute-start.20 = (f32[2,2,96,128]{3,2,1,0:T(8,128)S(1)}, f32[2,2,96,128]{3,2,1,0:T(8,128)S(1)}, u32[]{:S(2)}, u32[]{:S(2)}) collective-permute-start(f32[2,2,96,128]{3,2,1,0:T(8,128)S(1)} %get-tuple-element.139), channel_id=1, source_target_pairs={{0,4},{1,5},{2,6},{3,7},{4,0},{5,1},{6,2},{7,3},{8,12},{9,13},{10,... | collective-permute-start | bytes 589832 | tf_op jit(solution)/shard_map/ppermute | solution.py:28
  135.5 7.4 %collective-permute-start.22 = (f32[96,256]{1,0:T(8,128)S(1)}, f32[96,256]{1,0:T(8,128)S(1)}, u32[]{:S(2)}, u32[]{:S(2)}) collective-permute-start(f32[96,256]{1,0:T(8,128)S(1)} %get-tuple-element.143), channel_id=1, source_target_pairs={{0,121},{1,120},{2,123},{3,122},{4,125},{5,124},{6,127},{7,126},{8... | collective-permute-start | bytes 294920 | tf_op jit(solution)/shard_map/ppermute | solution.py:28
  135.6 7.4 %collective-permute-start.21 = (f32[96,256]{1,0:T(8,128)S(1)}, f32[96,256]{1,0:T(8,128)S(1)}, u32[]{:S(2)}, u32[]{:S(2)}) collective-permute-start(f32[96,256]{1,0:T(8,128)S(1)} %get-tuple-element.142), channel_id=1, source_target_pairs={{0,1},{1,0},{2,3},{3,2},{4,5},{5,4},{6,7},{7,6},{8,9},{9,8},{10,11... | collective-permute-start | bytes 294920 | tf_op jit(solution)/shard_map/ppermute | solution.py:28
  135.9 11.6 %collective-permute-start.23 = (f32[96,768]{1,0:T(8,128)S(1)}, f32[96,768]{1,0:T(8,128)S(1)}, u32[]{:S(2)}, u32[]{:S(2)}) collective-permute-start(f32[96,768]{1,0:T(8,128)S(1)} %get-tuple-element.144), channel_id=1, source_target_pairs={{0,120},{1,121},{2,122},{3,123},{4,124},{5,125},{6,126},{7,127},{8... | collective-permute-start | bytes 884744 | tf_op jit(solution)/shard_map/ppermute | solution.py:28
